TPU v7x, 32 devices: a whole 2x2x4 slice. The times are simulated.
32 devices in a mesh: dp: 16 (over z, y, x), tensor: 2 (over core).
Axes of the slice: x: 2, y: 2, z: 4, core: 2. Of those that a mesh axis runs over, the one named last changes fastest.
Arguments:
- leaf_tokens: bfloat16 [128, 8, 2048], P(('dp', 'tensor')), may hold values from -40 to 40
- attn_gain: float32 [2048], replicated, may hold values from 0.25 to 2.5
- w_query: bfloat16 [2048, 2048], P(None, 'tensor'), may hold values from -0.125 to 0.125
- w_key: bfloat16 [2048, 2048], P(None, 'tensor'), may hold values from -0.125 to 0.125
- w_value: bfloat16 [2048, 2048], P(None, 'tensor'), may hold values from -0.125 to 0.125
- w_out: bfloat16 [2048, 2048], P('tensor'), may hold values from -0.125 to 0.125
- prefix_kv: bfloat16 [2, 14336, 2048], P(None, 'dp', 'tensor'), may hold values from -104 to 104
- prefix_owner: int32 [128, 3], P('dp'), may hold values from 0 to 15, as said below
- prefix_start: int32 [128, 3], P('dp'), may hold values from 0 to 864, as said below
- prefix_len: int32 [128, 3], P('dp'), may hold values from 1 to 512, as said below
- mlp_gain: float32 [2048], replicated, may hold values from 0.25 to 2.5
- shared_in: bfloat16 [2048, 2, 1408], P(None, None, 'tensor'), may hold values from -0.125 to 0.125
- shared_out: bfloat16 [1408, 2048], P('tensor'), may hold values from -0.15625 to 0.15625
- expert_in: bfloat16 [64, 2048, 2, 1408], P('dp', None, None, 'tensor'), may hold values from -0.125 to 0.125
- expert_out: bfloat16 [64, 1408, 2048], P('dp', 'tensor'), may hold values from -0.15625 to 0.15625
- expert_ids: int32 [128, 8, 6], P('dp'), may hold values from 0 to 63, all different within a row; in each aligned block of 64 rows (0 to 63, 64 to 127, ..., all dimensions but the last counted through in order) at most 8 rows name the same one
- gate_weights: float32 [128, 8, 6], P('dp'), may hold values from 0.05 to 0.4
- request_of: int32 [128], P('dp'), may hold values from 0 to 127, as said below
Outputs:
- layer_out: bfloat16 [128, 8, 2048], P('dp', 'tensor')
Inputs may be any that keep to these rules, and one draw needn't show every extreme that they name: `prefix_owner`: each data group owns exactly one first-level node, two second-level nodes and four third-level nodes; a first-level node serves 8 requests, a second-level node half as many, a third-level node a quarter. The 8 requests of one data group name 8 different owners at each level, and together over the three levels they name no owner more than twice. `prefix_start`: the first level starts at 0; the second at 512 or 640; the third at 768 + q * 32 with q from 0 to 3. `prefix_len`: A node has 1 to 512, 128 or 32 keys at the first, second or third level, each of these maxima reached. Requests naming the same owner and start at a level share that node and its length; each node lies under one node of the level above. `expert_ids`: each row names 6 different experts; in the rows of one data group (aligned blocks of 64 rows) no expert is named more than 8 times. `request_of`: A permutation; the 8 dealt requests of one data group go to 8 different data groups.
All inputs are finite; a program needn't handle non-finite values.
Results may differ from a plain program's by a relative error of at most 0.025.
Values may be sent and summed in bfloat16 or wider, within the bound.
No kernel may reach another device: no remote copies, remote signals or barrier semaphores. Data moves between devices by JAX's collectives and lax.ppermute only.
A program may use at most 128 MiB of HBM per device.

v0:
```python
import functools

import jax
import jax.numpy as jnp
from jax import lax
from jax.experimental import pallas as pl
from jax.experimental.pallas import tpu as pltpu
from jax.sharding import PartitionSpec as P

HEAD_DIM = 128
EPS = 1e-06
ROPE_BASE = 10000.0
LANES = 128
HIDE = -1e30
LOG2E = 1.4426950408889634
LN2 = 0.6931471805599453
MIB = 1 << 20

f32 = jnp.float32
bf16 = jnp.bfloat16


def dot(a, b):
    return lax.dot_general(a, b, (((1,), (0,)), ((), ())), preferred_element_type=f32)


def dot_nt(a, b):
    return lax.dot_general(a, b, (((1,), (1,)), ((), ())), preferred_element_type=f32)


def iota(shape, dim):
    return lax.broadcasted_iota(jnp.int32, shape, dim).astype(f32)


def divided(index, by):
    quotient = jnp.floor((index + 0.5) * (1.0 / by))
    return quotient, index - by * quotient


def one_hot(condition):
    return jnp.where(condition, 1.0, 0.0).astype(bf16)


def rms(values, gain):
    mean_square = jnp.mean(values * values, axis=-1, keepdims=True)
    return (values * lax.rsqrt(mean_square + EPS) * gain).astype(bf16)


def ring_get(piece, count):
    pieces = [piece]
    for step in range(1, count):
        pieces.append(
            lax.ppermute(piece, "tensor", [((i + step) % count, i) for i in range(count)])
        )
    return pieces


def ring_send(pieces):
    count = len(pieces)
    arrived = [pieces[0]]
    for step in range(1, count):
        arrived.append(
            lax.ppermute(pieces[step], "tensor", [(i, (i + step) % count) for i in range(count)])
        )
    return arrived


def exchange(rows, groups):
    blocks = rows.reshape(groups, rows.shape[0] // groups, rows.shape[1])
    return lax.all_to_all(blocks, "dp", split_axis=0, concat_axis=0, tiled=True).reshape(rows.shape)


def whole():
    return pl.BlockSpec(memory_space=pltpu.VMEM)


def scalar():
    return pl.BlockSpec(memory_space=pltpu.SMEM)


def params(mib, grid=0):
    return pltpu.CompilerParams(
        vmem_limit_bytes=mib * MIB,
        dimension_semantics=("arbitrary",) * grid if grid else None,
    )


def cost(flops, nbytes):
    return pl.CostEstimate(flops=int(flops), bytes_accessed=int(nbytes), transcendentals=0)


def routing_kernel(
    table_ref, ids_ref, gates_ref,
    place_ref, meta_ref, pick_ref, send_ref, high_ref, low_ref, final_ref,
    *, requests, leaf_len, groups, capacity, experts,
):
    items = 3 * requests
    rows = requests * leaf_len
    table = table_ref[...].astype(f32)
    owner, start, length = table[0:1], table[1:2], table[2:3]
    dest, place = table[3:4, :requests], table[4:5, :requests]
    down, across = iota((items, items), 0), iota((items, items), 1)
    owner_down = jnp.sum(jnp.where(down == across, owner, 0.0), axis=1, keepdims=True)
    earlier = jnp.where((owner_down == owner) & (down < across), 1.0, 0.0)
    slot = owner * 2.0 + jnp.sum(earlier, axis=0, keepdims=True)
    slot_rows = groups * 2 * leaf_len
    row_slot, row_token = divided(iota((slot_rows, 1), 0), leaf_len)
    request_of_row, token_of_row = divided(iota((1, rows), 1), leaf_len)
    named = slot == row_slot
    _, item_request = divided(iota((items, 1), 0), requests)
    placed = dot(one_hot(named), one_hot(item_request == request_of_row))
    place_ref[...] = jnp.where(row_token == token_of_row, placed, 0.0).astype(bf16)

    first_key = jnp.sum(jnp.where(named, start, 0.0), axis=1, keepdims=True)
    key_count = jnp.sum(jnp.where(named, length, 0.0), axis=1, keepdims=True)
    row_group, _ = divided(row_slot, 2)
    tag = jnp.sum(jnp.where(dest == row_group, place + 1.0, 0.0), axis=1, keepdims=True)
    lane = iota((1, LANES), 1)
    meta = jnp.zeros((slot_rows, LANES), f32)
    for at, value in enumerate(divided(first_key, 32) + divided(key_count, 32) + (tag,)):
        meta = jnp.where(lane == at, value, meta)
    meta_ref[...] = meta.astype(bf16)

    row_request, row_place = divided(iota((rows, 1), 0), leaf_len)
    item_across = iota((1, items), 1)
    slot_across, token_across = divided(iota((1, slot_rows), 1), leaf_len)
    for level in range(3):
        mine = item_across == row_request + level * requests
        slot_down = jnp.sum(jnp.where(mine, slot, 0.0), axis=1, keepdims=True)
        pick_ref[level] = one_hot((slot_down == slot_across) & (row_place == token_across))

    ids = ids_ref[...].astype(f32)
    gates = gates_ref[...]
    expert_down = iota((experts, 1), 0)
    member = jnp.zeros((experts, rows), f32)
    gate = jnp.zeros((experts, rows), f32)
    for choice in range(ids.shape[0]):
        hit = ids[choice : choice + 1] == expert_down
        member = member + jnp.where(hit, 1.0, 0.0)
        gate = gate + jnp.where(hit, gates[choice : choice + 1], 0.0)
    ahead = one_hot(iota((rows, rows), 0) < iota((rows, rows), 1))
    member = member.astype(bf16)
    before = dot(member, ahead).astype(bf16)
    slots = experts * capacity
    slot_expert, slot_place = divided(iota((slots, 1), 0), capacity)
    spread = one_hot(slot_expert == iota((1, experts), 1))
    taken = (dot(spread, member) > 0.5) & (dot(spread, before) == slot_place)
    send_ref[...] = one_hot(taken)
    high = gate.astype(bf16)
    low = (gate - high.astype(f32)).astype(bf16)
    for part, ref in ((high, high_ref), (low, low_ref)):
        ref[...] = jnp.transpose(jnp.where(taken, dot(spread, part), 0.0)).astype(bf16)

    final_rows = groups * leaf_len
    final_group, final_token = divided(iota((final_rows, 1), 0), leaf_len)
    going = dot(
        one_hot(dest == final_group),
        one_hot(iota((requests, 1), 0) == request_of_row),
    )
    final_ref[...] = jnp.where(final_token == token_of_row, going, 0.0).astype(bf16)


def rotated(product, cosine, sine, heads):
    columns = []
    for head in range(heads):
        part = product[:, head * HEAD_DIM : (head + 1) * HEAD_DIM]
        columns.append(part * cosine + pltpu.roll(part, HEAD_DIM // 2, 1) * sine)
    return jnp.concatenate(columns, axis=1).astype(bf16)


def query_kernel(*refs, tensors, heads):
    index_ref, pieces, refs = refs[0], refs[1 : 1 + tensors], refs[1 + tensors :]
    (gain_ref, weight_ref, cos_ref, sin_ref, place_ref, meta_ref,
     raw_ref, normed_ref, query_ref, send_ref, rows_ref) = refs
    step = pl.program_id(0)
    shard = pieces[0].shape[0]

    @pl.when(step == 0)
    def _():
        for at, piece in enumerate(pieces):
            owner = lax.rem(index_ref[0] + at, tensors)
            rows_ref[pl.ds(pl.multiple_of(owner * shard, shard), shard), :] = piece[...]
        raw_ref[...] = rows_ref[...]
        normed_ref[...] = rms(rows_ref[...].astype(f32), gain_ref[...])
        send_ref[:, send_ref.shape[1] - LANES :] = meta_ref[...]

    product = dot(normed_ref[...], weight_ref[...])
    query = rotated(product, cos_ref[...], sin_ref[...], heads)
    query_ref[...] = query
    width = heads * HEAD_DIM
    send_ref[:, pl.ds(pl.multiple_of(step * width, width), width)] = dot(
        place_ref[...], query
    ).astype(bf16)


def leaf_kernel(
    normed_ref, query_ref, key_ref, value_ref, cos_ref, sin_ref, out_ref, lse_ref,
    *, heads, leaf_len, scale,
):
    step = pl.program_id(0)
    normed = normed_ref[...]
    rows = normed.shape[0]
    keys = rotated(dot(normed, key_ref[...]), cos_ref[...], sin_ref[...], heads)
    values = dot(normed, value_ref[...]).astype(bf16)
    down, across = iota((rows, 1), 0), iota((1, rows), 1)
    visible = (divided(down, leaf_len)[0] == divided(across, leaf_len)[0]) & (across <= down)
    lane = lax.broadcasted_iota(jnp.int32, (1, LANES), 1)

    @pl.when(step == 0)
    def _():
        lse_ref[...] = jnp.zeros_like(lse_ref)

    for head in range(heads):
        at = slice(head * HEAD_DIM, (head + 1) * HEAD_DIM)
        scores = jnp.where(visible, dot_nt(query_ref[:, at], keys[:, at]) * scale, HIDE)
        highest = jnp.max(scores, axis=1, keepdims=True)
        weights = jnp.exp(scores - highest)
        total = jnp.sum(weights, axis=1, keepdims=True)
        out_ref[:, at] = dot(weights.astype(bf16), values[:, at]) / total
        lse = highest + jnp.log(total)
        lse_ref[...] = jnp.where(lane == step * heads + head, lse, lse_ref[...])


def owner_kernel(
    query_ref, meta_ref, kv_ref, back_ref, bias_ref, lse_ref, *, heads, all_heads, scale
):
    step = pl.program_id(0)
    rows, keys = bias_ref.shape
    width = heads * HEAD_DIM
    lane = lax.broadcasted_iota(jnp.int32, (1, LANES), 1)

    @pl.when(step == 0)
    def _():
        meta = meta_ref[...].astype(f32)
        first = meta[:, 0:1] * 32.0 + meta[:, 1:2]
        last = first + meta[:, 2:3] * 32.0 + meta[:, 3:4]
        key = iota((1, keys), 1)
        bias_ref[...] = jnp.where((key >= first) & (key < last), 0.0, HIDE)
        lse_ref[...] = jnp.zeros_like(lse_ref)

    chunk = 64
    for head in range(heads):
        at = slice(head * HEAD_DIM, (head + 1) * HEAD_DIM)
        here = lane == step * heads + head
        there = lane == step * heads + head + all_heads
        for low in range(0, rows, chunk):
            part = slice(low, low + chunk)
            scores = dot_nt(query_ref[part, at], kv_ref[0, :, at]) * (scale * LOG2E)
            scores = scores + bias_ref[part, :]
            highest = jnp.max(scores, axis=1, keepdims=True)
            weights = jnp.exp2(scores - highest)
            total = jnp.sum(weights, axis=1, keepdims=True)
            out = dot(weights.astype(bf16), kv_ref[1, :, at]) / total
            lane_at = pl.multiple_of(step * width + head * HEAD_DIM, HEAD_DIM)
            back_ref[part, pl.ds(lane_at, HEAD_DIM)] = out.astype(bf16)
            lse = highest * LN2 + jnp.log(total)
            lse_high = lse.astype(bf16).astype(f32)
            kept = jnp.where(here, lse_high, lse_ref[part, :])
            lse_ref[part, :] = jnp.where(there, lse - lse_high, kept)

    @pl.when(step == pl.num_programs(0) - 1)
    def _():
        back_ref[:, back_ref.shape[1] - LANES :] = lse_ref[...].astype(bf16)


def merge_kernel(back_ref, pick_ref, leaf_ref, lse_ref, weight_ref, out_ref, attended_ref, *, heads):
    width = heads * HEAD_DIM

    @pl.when(pl.program_id(0) == 0)
    def _():
        back = back_ref[...]
        outputs, sums = [leaf_ref[...]], [lse_ref[...]]
        for level in range(3):
            rows = dot(pick_ref[level], back)
            outputs.append(rows[:, :width])
            tail = rows[:, width:]
            sums.append(tail + pltpu.roll(tail, LANES - heads, 1))
        highest = functools.reduce(jnp.maximum, sums)
        scales = [jnp.exp(one - highest) for one in sums]
        total = sum(scales[1:], scales[0])
        scales = [one / total for one in scales]
        for head in range(heads):
            at = slice(head * HEAD_DIM, (head + 1) * HEAD_DIM)
            mixed = sum(
                scales[i][:, head : head + 1] * outputs[i][:, at] for i in range(4)
            )
            attended_ref[:, at] = mixed.astype(bf16)

    out_ref[...] = dot(attended_ref[...], weight_ref[...]).astype(bf16)


def middle_kernel(*refs, tensors):
    index_ref, raw_ref, gain_ref, send_ref = refs[:4]
    pieces = refs[4 : 4 + tensors]
    normed_ref, own_ref, rows_ref, resid_ref = refs[4 + tensors :]
    width = own_ref.shape[1]
    own = pl.ds(pl.multiple_of(index_ref[0] * width, width), width)
    total = raw_ref[...].astype(f32)
    for piece in pieces:
        total = total + piece[...].astype(f32)
    resid_ref[...] = total
    own_ref[...] = resid_ref[:, own]
    normed_ref[...] = rms(total, gain_ref[...])
    rows_ref[...] = dot(send_ref[...], normed_ref[:, own]).astype(bf16)


def shared_kernel(*refs, tensors):
    index_ref, rows_ref, in_ref, down_ref = refs[:4]
    pieces, total_ref = refs[4 : 4 + tensors], refs[4 + tensors]
    rows = rows_ref[...]
    gate = dot_nt(rows, in_ref[0])
    up = dot_nt(rows, in_ref[1])
    hidden = (gate / (1.0 + jnp.exp(-gate)) * up).astype(bf16)
    total_ref[...] = dot(hidden, down_ref[...])
    width = pieces[0].shape[1]
    for at, piece in enumerate(pieces):
        column = lax.rem(index_ref[0] + at, tensors) * width
        piece[...] = total_ref[:, pl.ds(pl.multiple_of(column, width), width)].astype(bf16)


def expert_kernel(*refs, tensors, experts, capacity):
    index_ref, arrived, refs = refs[0], refs[1 : 1 + tensors], refs[1 + tensors :]
    in_ref, down_ref, refs = refs[0], refs[1], refs[2:]
    pieces, rows_ref, total_ref = refs[:tensors], refs[tensors], refs[tensors + 1]
    expert = pl.program_id(0)
    groups, _, width = arrived[0].shape
    count = groups * capacity

    @pl.when(expert == 0)
    def _():
        for at, piece in enumerate(arrived):
            column = lax.rem(index_ref[0] + at, tensors) * width
            columns = pl.ds(pl.multiple_of(column, width), width)
            values = piece[...].astype(f32)
            for e in range(experts):
                mine = values[:, e * capacity : (e + 1) * capacity, :].reshape(count, width)
                rows_ref[e, :, columns] = mine.astype(bf16)

    rows = rows_ref[expert]
    gate = dot_nt(rows, in_ref[0, 0])
    up = dot_nt(rows, in_ref[0, 1])
    hidden = (gate / (1.0 + jnp.exp(-gate)) * up).astype(bf16)
    value = dot(hidden, down_ref[0])
    at = pl.ds(pl.multiple_of(expert * capacity, capacity), capacity)
    total_ref[:, at, :] = value.reshape(groups, capacity, value.shape[1])

    @pl.when(expert == experts - 1)
    def _():
        for at, piece in enumerate(pieces):
            column = lax.rem(index_ref[0] + at, tensors) * width
            columns = pl.ds(pl.multiple_of(column, width), width)
            piece[...] = total_ref[:, :, columns].astype(bf16)


def combine_kernel(*refs, tensors):
    returned_ref, high_ref, low_ref, resid_ref, final_ref = refs[:5]
    shared, out_ref = refs[5 : 5 + tensors], refs[5 + tensors]
    returned = returned_ref[...]
    total = resid_ref[...]
    for piece in shared:
        total = total + piece[...].astype(f32)
    total = total + dot(high_ref[...], returned) + dot(low_ref[...], returned)
    out_ref[...] = dot(final_ref[...], total.astype(bf16)).astype(bf16)


def settle_kernel(*refs, tensors, leaf_len):
    index_ref, meta_ref, rows_ref = refs[:3]
    pieces = refs[3:]
    slot_rows, final_rows = meta_ref.shape[0], rows_ref.shape[0]
    places = pieces[0].shape[0]
    share = leaf_len // tensors
    tag_down = meta_ref[...].astype(f32)[:, 4:5]
    group, token = divided(iota((1, final_rows), 1), leaf_len)
    source = iota((slot_rows, 1), 0) == group * (2.0 * leaf_len) + token
    tag = jnp.sum(jnp.where(source, tag_down, 0.0), axis=0, keepdims=True)
    request, position = divided(iota((places, 1), 0), share)
    for at, piece in enumerate(pieces):
        shift = (lax.rem(index_ref[0] + at, tensors) * share).astype(f32)
        chosen = one_hot((tag == request + 1.0) & (token == position + shift))
        piece[...] = dot(chosen, rows_ref[...]).astype(bf16)


def on_device(
    leaf_tokens,
    attn_gain,
    w_query,
    w_key,
    w_value,
    w_out,
    prefix_kv,
    prefix_owner,
    prefix_start,
    prefix_len,
    mlp_gain,
    shared_in,
    shared_out,
    expert_in,
    expert_out,
    expert_ids,
    gate_weights,
    request_of,
):
    groups = lax.axis_size("dp")
    tensors = lax.axis_size("tensor")
    index = lax.axis_index("tensor").astype(jnp.int32).reshape(1)
    shard_requests, leaf_len, model_width = leaf_tokens.shape
    requests = prefix_owner.shape[0]
    rows = requests * leaf_len
    local_width = w_query.shape[1]
    local_heads = local_width // HEAD_DIM
    scale = HEAD_DIM ** (-0.5)
    column_share = model_width // tensors
    top_count = expert_ids.shape[2]
    local_experts = expert_in.shape[0]
    experts = local_experts * groups
    assignments = rows * top_count
    capacity = tensors * max(1, assignments * 4 // (experts * 3 * tensors))
    slots = experts * capacity
    slot_rows = groups * 2 * leaf_len
    final_rows = groups * leaf_len
    shape = jax.ShapeDtypeStruct

    raw_pieces = ring_get(leaf_tokens.reshape(shard_requests * leaf_len, model_width), tensors)

    pad = ((0, 0), (0, 2 * requests))
    table = jnp.concatenate(
        [
            prefix_owner.T.reshape(1, -1),
            prefix_start.T.reshape(1, -1),
            prefix_len.T.reshape(1, -1),
            jnp.pad((request_of // requests).reshape(1, -1), pad),
            jnp.pad((request_of % requests).reshape(1, -1), pad),
        ],
        axis=0,
    )
    ids = jnp.transpose(expert_ids, (2, 0, 1)).reshape(top_count, rows)
    gates = jnp.transpose(gate_weights, (2, 0, 1)).reshape(top_count, rows)
    place, meta, pick, send, gate_high, gate_low, final = pl.pallas_call(
        functools.partial(
            routing_kernel, requests=requests, leaf_len=leaf_len, groups=groups,
            capacity=capacity, experts=experts,
        ),
        out_shape=[
            shape((slot_rows, rows), bf16),
            shape((slot_rows, LANES), bf16),
            shape((3, rows, slot_rows), bf16),
            shape((slots, rows), bf16),
            shape((rows, slots), bf16),
            shape((rows, slots), bf16),
            shape((final_rows, rows), bf16),
        ],
        in_specs=[whole()] * 3,
        out_specs=[whole()] * 7,
        compiler_params=params(24),
        name="routing",
    )(table, ids, gates)

    offsets = jnp.sum(prefix_len, axis=1).astype(f32)
    positions = (offsets[:, None] + jnp.arange(leaf_len, dtype=f32)[None, :]).reshape(rows, 1)
    half = HEAD_DIM // 2
    frequency = ROPE_BASE ** (-2.0 * jnp.arange(half, dtype=f32) / HEAD_DIM)
    angles = positions * frequency[None, :]
    cosine = jnp.concatenate([jnp.cos(angles)] * 2, axis=1)
    sine = jnp.concatenate([-jnp.sin(angles), jnp.sin(angles)], axis=1)

    step_heads = min(2, local_heads)
    step_width = step_heads * HEAD_DIM
    steps = local_heads // step_heads
    fixed = lambda *dims: pl.BlockSpec(dims, lambda i: (0,) * len(dims))
    columns = lambda *dims: pl.BlockSpec(dims, lambda i: (0,) * (len(dims) - 1) + (i,))
    send_width = local_width + LANES
    shard_rows = shard_requests * leaf_len
    raw, normed, query, query_send = pl.pallas_call(
        functools.partial(query_kernel, tensors=tensors, heads=step_heads),
        grid=(steps,),
        out_shape=[
            shape((rows, model_width), bf16),
            shape((rows, model_width), bf16),
            shape((rows, local_width), bf16),
            shape((slot_rows, send_width), bf16),
        ],
        in_specs=[scalar()]
        + [fixed(shard_rows, model_width)] * tensors
        + [
            fixed(1, model_width),
            columns(model_width, step_width),
            fixed(rows, LANES),
            fixed(rows, LANES),
            fixed(slot_rows, rows),
            fixed(slot_rows, LANES),
        ],
        out_specs=[
            fixed(rows, model_width),
            fixed(rows, model_width),
            columns(rows, step_width),
            fixed(slot_rows, send_width),
        ],
        scratch_shapes=[pltpu.VMEM((rows, model_width), bf16)],
        compiler_params=params(24, 1),
        cost_estimate=cost(2 * rows * model_width * local_width, 2 * model_width * local_width),
        name="queries",
    )(
        index, *raw_pieces, attn_gain.reshape(1, -1), w_query, cosine, sine, place, meta
    )

    query_arrived = exchange(query_send, groups)

    leaf_out, leaf_lse = pl.pallas_call(
        functools.partial(leaf_kernel, heads=step_heads, leaf_len=leaf_len, scale=scale),
        grid=(steps,),
        out_shape=[shape((rows, local_width), f32), shape((rows, LANES), f32)],
        in_specs=[
            fixed(rows, model_width),
            columns(rows, step_width),
            columns(model_width, step_width),
            columns(model_width, step_width),
            fixed(rows, LANES),
            fixed(rows, LANES),
        ],
        out_specs=[columns(rows, step_width), fixed(rows, LANES)],
        compiler_params=params(24, 1),
        cost_estimate=cost(4 * rows * model_width * local_width, 4 * model_width * local_width),
        name="leaf",
    )(normed, query, w_key, w_value, cosine, sine)

    pool = prefix_kv.shape[1]
    back_send = pl.pallas_call(
        functools.partial(owner_kernel, heads=step_heads, all_heads=local_heads, scale=scale),
        grid=(steps,),
        out_shape=shape((slot_rows, send_width), bf16),
        in_specs=[
            columns(slot_rows, step_width),
            pl.BlockSpec((slot_rows, LANES), lambda i: (0, local_heads)),
            columns(2, pool, step_width),
        ],
        out_specs=fixed(slot_rows, send_width),
        scratch_shapes=[pltpu.VMEM((slot_rows, pool), f32), pltpu.VMEM((slot_rows, LANES), f32)],
        compiler_params=params(32, 1),
        cost_estimate=cost(4 * slot_rows * pool * local_width, 4 * pool * local_width),
        name="owner",
    )(query_arrived, query_arrived, prefix_kv)

    back = exchange(back_send, groups)

    out_step = min(512, model_width)
    partial_out = pl.pallas_call(
        functools.partial(merge_kernel, heads=local_heads),
        grid=(model_width // out_step,),
        out_shape=shape((rows, model_width), bf16),
        in_specs=[
            fixed(slot_rows, send_width),
            fixed(3, rows, slot_rows),
            fixed(rows, local_width),
            fixed(rows, LANES),
            columns(local_width, out_step),
        ],
        out_specs=columns(rows, out_step),
        scratch_shapes=[pltpu.VMEM((rows, local_width), bf16)],
        compiler_params=params(24, 1),
        cost_estimate=cost(2 * rows * local_width * model_width, 2 * local_width * model_width),
        name="merge",
    )(back, pick, leaf_out, leaf_lse, w_out)

    out_pieces = ring_get(partial_out, tensors)

    normed_mlp, resid_own, send_rows = pl.pallas_call(
        functools.partial(middle_kernel, tensors=tensors),
        out_shape=[
            shape((rows, model_width), bf16),
            shape((rows, column_share), f32),
            shape((slots, column_share), bf16),
        ],
        in_specs=[scalar()] + [whole()] * (3 + tensors),
        out_specs=[whole()] * 3,
        scratch_shapes=[pltpu.VMEM((rows, model_width), f32)],
        compiler_params=params(24),
        cost_estimate=cost(2 * slots * rows * column_share, 4 * slots * column_share),
        name="middle",
    )(index, raw, mlp_gain.reshape(1, -1), send, *out_pieces)

    arrived = exchange(send_rows, groups)

    hidden = shared_out.shape[0]
    shared_pieces = pl.pallas_call(
        functools.partial(shared_kernel, tensors=tensors),
        out_shape=[shape((rows, column_share), bf16)] * tensors,
        in_specs=[scalar()] + [whole()] * 3,
        out_specs=[whole()] * tensors,
        scratch_shapes=[pltpu.VMEM((rows, model_width), f32)],
        compiler_params=params(24),
        cost_estimate=cost(6 * rows * hidden * model_width, 6 * hidden * model_width),
        name="shared",
    )(index, normed_mlp, jnp.transpose(shared_in, (1, 2, 0)), shared_out)
    shared_pieces = ring_send(shared_pieces)

    block = local_experts * capacity
    arrived_pieces = ring_get(arrived.reshape(groups, block, column_share), tensors)
    expert_hidden = expert_out.shape[1]
    partial_pieces = pl.pallas_call(
        functools.partial(
            expert_kernel, tensors=tensors, experts=local_experts, capacity=capacity
        ),
        grid=(local_experts,),
        out_shape=[shape((groups, block, column_share), bf16)] * tensors,
        in_specs=[scalar()]
        + [fixed(groups, block, column_share)] * tensors
        + [
            pl.BlockSpec((1, 2, expert_hidden, model_width), lambda i: (i, 0, 0, 0)),
            pl.BlockSpec((1, expert_hidden, model_width), lambda i: (i, 0, 0)),
        ],
        out_specs=[fixed(groups, block, column_share)] * tensors,
        scratch_shapes=[
            pltpu.VMEM((local_experts, groups * capacity, model_width), bf16),
            pltpu.VMEM((groups, block, model_width), f32),
        ],
        compiler_params=params(48, 1),
        cost_estimate=cost(
            6 * slots * expert_hidden * model_width,
            6 * local_experts * expert_hidden * model_width,
        ),
        name="experts",
    )(index, *arrived_pieces, jnp.transpose(expert_in, (0, 2, 3, 1)), expert_out)
    partial_pieces = ring_send(partial_pieces)
    summed = sum(piece.astype(f32) for piece in partial_pieces).astype(bf16)

    returned = exchange(summed.reshape(slots, column_share), groups)

    final_send = pl.pallas_call(
        functools.partial(combine_kernel, tensors=tensors),
        out_shape=shape((final_rows, column_share), bf16),
        in_specs=[whole()] * (5 + tensors),
        out_specs=whole(),
        compiler_params=params(24),
        name="combine",
    )(returned, gate_high, gate_low, resid_own, final, *shared_pieces)

    final_arrived = exchange(final_send, groups)

    places = requests * (leaf_len // tensors)
    settled = pl.pallas_call(
        functools.partial(settle_kernel, tensors=tensors, leaf_len=leaf_len),
        grid=(1,),
        out_shape=[shape((places, column_share), bf16)] * tensors,
        in_specs=[
            scalar(),
            pl.BlockSpec((slot_rows, LANES), lambda i: (0, local_heads)),
            fixed(final_rows, column_share),
        ],
        out_specs=[fixed(places, column_share)] * tensors,
        compiler_params=params(24, 1),
        name="settle",
    )(index, query_arrived, final_arrived)
    settled = ring_send(settled)
    if tensors == 2:
        first = index[0] == 0
        own, other = settled
        result = jnp.concatenate(
            [jnp.where(first, own, other), jnp.where(first, other, own)], axis=1
        )
    else:
        result = jnp.zeros((places, model_width), bf16)
        for at, piece in enumerate(settled):
            column = ((index[0] - at + tensors) % tensors) * column_share
            result = lax.dynamic_update_slice(result, piece, (0, column))
    return result.reshape(requests, leaf_len // tensors, model_width)


def solution(mesh):
    in_specs = (
        P(("dp", "tensor"), None, None),
        P(),
        P(None, "tensor"),
        P(None, "tensor"),
        P(None, "tensor"),
        P("tensor", None),
        P(None, "dp", "tensor"),
        P("dp", None),
        P("dp", None),
        P("dp", None),
        P(),
        P(None, None, "tensor"),
        P("tensor", None),
        P("dp", None, None, "tensor"),
        P("dp", "tensor", None),
        P("dp", None, None),
        P("dp", None, None),
        P("dp"),
    )
    out_specs = P("dp", "tensor", None)
    return jax.shard_map(
        on_device, mesh=mesh, in_specs=in_specs, out_specs=out_specs, check_vma=False
    )
```

profile of v0, /device:TPU:0, one launch (start us, length us, event | category | flops | bytes accessed | tf_op | source)
XLA Modules:
  0.0 176.8 jit_solution(4326538079606129592)
XLA Ops:
  2.2 0.8 reshape.86
  3.0 0.8 reshape.87
  3.8 0.8 reshape.88
  4.5 0.8 reshape.91.ids_ref
  5.3 0.8 reshape.92.gates_ref
  6.8 2.2 %copy-done.1 = bf16[2048,1024]{1,0:T(8,128)(2,1)S(1)} copy-done((bf16[2048,1024]{1,0:T(8,128)(2,1)S(1)}, bf16[2048,1024]{1,0:T(8,128)(2,1)}, u32[]{:S(2)}) %copy-start.1) | copy-done | bytes 4194328
  9.0 0.9 copy-done.7
  10.6 3.2 %queries.1 = (bf16[64,2048]{1,0:T(8,128)(2,1)S(1)}, bf16[64,2048]{1,0:T(8,128)(2,1)S(1)}, bf16[64,1024]{1,0:T(8,128)(2,1)S(1)}, bf16[256,1152]{1,0:T(8,128)(2,1)S(1)}) custom-call(s32[1]{0:T(128)} %bitcast.refs_0_, bf16[32,2048]{1,0:T(8,128)(2,1)S(1)} %bitcast.34, bf16[32,2048]{1,0:T(8,128)(2,1)S(1)} %collective-permute-done.refs_2_, ...), custom_call_target="tpu_custom_call" | custom-call | flops 268435456 | bytes 4194304 | tf_op jit(solution)/shard_map/queries/pallas_call | solution.py:473
  13.8 25.8 %all_to_all.25 = bf16[16,16,1152]{2,1,0:T(8,128)(2,1)S(1)} all-to-all(bf16[16,16,1152]{2,1,0:T(8,128)(2,1)S(1)} %bitcast.32), channel_id=1, replica_groups=mesh['dp'=16,'tensor'=2] {'dp'}, dimensions={0} | all-to-all | bytes 1179648 | tf_op jit(solution)/shard_map/all_to_all | solution.py:70
  39.6 12.8 %owner.1 = bf16[256,1152]{1,0:T(8,128)(2,1)} custom-call(bf16[256,1152]{1,0:T(8,128)(2,1)S(1)} %bitcast.23, bf16[256,1152]{1,0:T(8,128)(2,1)S(1)} %bitcast.24, bf16[2,896,1024]{2,1,0:T(8,128)(2,1)S(1)} %copy-done.5), custom_call_target="tpu_custom_call" | custom-call | flops 939524096 | bytes 3670016 | tf_op jit(solution)/shard_map/owner/pallas_call | solution.py:527
  52.4 3.6 %all-to-all-start.1 = ((bf16[16,16,1152]{2,1,0:T(8,128)(2,1)}), bf16[16,16,1152]{2,1,0:T(8,128)(2,1)S(1)}, u32[]{:S(2)}, u32[]{:S(2)}) async-start(bf16[16,16,1152]{2,1,0:T(8,128)(2,1)} %bitcast.13), calls=%async_computation.1 | async-start | bytes 1179648 | tf_op jit(solution)/shard_map/all_to_all | solution.py:70
  56.0 2.2 %copy-done.2 = bf16[2048,1024]{1,0:T(8,128)(2,1)S(1)} copy-done((bf16[2048,1024]{1,0:T(8,128)(2,1)S(1)}, bf16[2048,1024]{1,0:T(8,128)(2,1)}, u32[]{:S(2)}) %copy-start.2) | copy-done | bytes 4194328
  58.2 2.2 %copy-done.3 = bf16[2048,1024]{1,0:T(8,128)(2,1)S(1)} copy-done((bf16[2048,1024]{1,0:T(8,128)(2,1)S(1)}, bf16[2048,1024]{1,0:T(8,128)(2,1)}, u32[]{:S(2)}) %copy-start.3) | copy-done | bytes 4194328
  60.4 4.8 %leaf.1 = (f32[64,1024]{1,0:T(8,128)S(1)}, f32[64,128]{1,0:T(8,128)S(1)}) custom-call(bf16[64,2048]{1,0:T(8,128)(2,1)S(1)} %get-tuple-element.33.normed_ref, bf16[64,1024]{1,0:T(8,128)(2,1)S(1)} %get-tuple-element.34.query_ref, bf16[2048,1024]{1,0:T(8,128)(2,1)S(1)} %copy-done.2, bf16[2048,1024]{1,0:T(8,128)(2,1)S(1)} %copy-done.3, ...), custom_call_target="tpu_custom_call" | custom-call | flops 536870912 | bytes 8388608 | tf_op jit(solution)/shard_map/leaf/pallas_call | solution.py:508
  65.2 6.5 %all-to-all-done.1 = bf16[16,16,1152]{2,1,0:T(8,128)(2,1)S(1)} async-done(((bf16[16,16,1152]{2,1,0:T(8,128)(2,1)}), bf16[16,16,1152]{2,1,0:T(8,128)(2,1)S(1)}, u32[]{:S(2)}, u32[]{:S(2)}) %all-to-all-start.1) | async-done | bytes 589856 | tf_op jit(solution)/shard_map/all_to_all | solution.py:70
  71.7 2.2 %copy-done.4 = bf16[1024,2048]{1,0:T(8,128)(2,1)S(1)} copy-done((bf16[1024,2048]{1,0:T(8,128)(2,1)S(1)}, bf16[1024,2048]{1,0:T(8,128)(2,1)}, u32[]{:S(2)}) %copy-start.4) | copy-done | bytes 4194328
  73.9 2.5 %merge.1.refs_4_ = bf16[64,2048]{1,0:T(8,128)(2,1)S(1)} custom-call(bf16[256,1152]{1,0:T(8,128)(2,1)S(1)} %bitcast.28, bf16[3,64,256]{2,1,0:T(8,128)(2,1)S(1)} %get-tuple-element.32.pick_ref, f32[64,1024]{1,0:T(8,128)S(1)} %get-tuple-element.35.leaf_ref, f32[64,128]{1,0:T(8,128)S(1)} %get-tuple-element.36.lse_ref, bf16[1024,2048]{1,0:T(8,128)(2,1)S(1)} %copy-done.4), custom_call_target="tpu_custom_call" | custom-call | flops 268435456 | bytes 4194304 | tf_op jit(solution)/shard_map/merge/pallas_call | solution.py:546
  76.4 1.5 collective-permute-done.1.refs_5_
  78.6 30.5 %all_to_all.26.refs_1_ = bf16[16,32,1024]{2,1,0:T(8,128)(2,1)S(1)} all-to-all(bf16[16,32,1024]{2,1,0:T(8,128)(2,1)S(1)} %bitcast.31), channel_id=1, replica_groups=mesh['dp'=16,'tensor'=2] {'dp'}, dimensions={0} | all-to-all | bytes 2097152 | tf_op jit(solution)/shard_map/all_to_all | solution.py:70
  109.1 2.7 %collective-permute-done.2.refs_2_ = bf16[16,32,1024]{2,1,0:T(8,128)(2,1)S(1)} collective-permute-done((bf16[16,32,1024]{2,1,0:T(8,128)(2,1)S(1)}, bf16[16,32,1024]{2,1,0:T(8,128)(2,1)S(1)}, u32[]{:S(2)}, u32[]{:S(2)}) %collective-permute-start.2) | collective-permute-done | bytes 1048608 | tf_op jit(solution)/shard_map/ppermute | solution.py:53
  111.8 14.9 %experts.1 = (bf16[16,32,1024]{2,1,0:T(8,128)(2,1)S(1)}, bf16[16,32,1024]{2,1,0:T(8,128)(2,1)S(1)}) custom-call(s32[1]{0:T(128)} %bitcast.refs_0_, bf16[16,32,1024]{2,1,0:T(8,128)(2,1)S(1)} %all_to_all.26.refs_1_, bf16[16,32,1024]{2,1,0:T(8,128)(2,1)S(1)} %collective-permute-done.2.refs_2_, bf16[4,2,704,2048]{3,2,1,0:T(8,128)(2,1)} %bitcast.37, ...), custom_call_target="tpu_custom_call" | custom-call | flops 4429185024 | bytes 34603008 | tf_op jit(solution)/shard_map/experts/pallas_call | solution.py:599
  126.8 2.5 %collective-permute-done.3 = bf16[16,32,1024]{2,1,0:T(8,128)(2,1)S(1)} collective-permute-done((bf16[16,32,1024]{2,1,0:T(8,128)(2,1)S(1)}, bf16[16,32,1024]{2,1,0:T(8,128)(2,1)S(1)}, u32[]{:S(2)}, u32[]{:S(2)}) %collective-permute-start.3) | collective-permute-done | bytes 1048608 | tf_op jit(solution)/shard_map/ppermute | solution.py:63
  129.4 1.4 add_convert_fusion
  130.8 3.9 %all-to-all-start.3 = ((bf16[16,32,1024]{2,1,0:T(8,128)(2,1)}), bf16[16,32,1024]{2,1,0:T(8,128)(2,1)S(1)}, u32[]{:S(2)}, u32[]{:S(2)}) async-start(bf16[16,32,1024]{2,1,0:T(8,128)(2,1)} %add_convert_fusion), calls=%async_computation.3 | async-start | bytes 2097152 | tf_op jit(solution)/shard_map/all_to_all | solution.py:70
  134.8 2.6 %copy-done = bf16[2048,2,704]{0,2,1:T(8,128)(2,1)S(1)} copy-done((bf16[2048,2,704]{0,2,1:T(8,128)(2,1)S(1)}, bf16[2048,2,704]{0,2,1:T(8,128)(2,1)}, u32[]{:S(2)}) %copy-start) | copy-done | bytes 5767192
  137.4 1.8 %copy-done.6 = bf16[704,2048]{1,0:T(8,128)(2,1)S(1)} copy-done((bf16[704,2048]{1,0:T(8,128)(2,1)S(1)}, bf16[704,2048]{1,0:T(8,128)(2,1)}, u32[]{:S(2)}) %copy-start.6) | copy-done | bytes 2883608
  139.2 2.4 %shared.1 = (bf16[64,1024]{1,0:T(8,128)(2,1)S(1)}, bf16[64,1024]{1,0:T(8,128)(2,1)S(1)}) custom-call(s32[1]{0:T(128)} %bitcast.refs_0_, bf16[64,2048]{1,0:T(8,128)(2,1)S(1)} %get-tuple-element.44.refs_1_, bf16[2,704,2048]{2,1,0:T(8,128)(2,1)S(1)} %bitcast.26, bf16[704,2048]{1,0:T(8,128)(2,1)S(1)} %copy-done.6), custom_call_target="tpu_custom_call" | custom-call | flops 553648128 | bytes 8650752 | tf_op jit(solution)/shard_map/shared/pallas_call | solution.py:584
  141.6 1.3 collective-permute-done.4.refs_6_
  143.0 16.4 %all-to-all-done.3 = bf16[16,32,1024]{2,1,0:T(8,128)(2,1)S(1)} async-done(((bf16[16,32,1024]{2,1,0:T(8,128)(2,1)}), bf16[16,32,1024]{2,1,0:T(8,128)(2,1)S(1)}, u32[]{:S(2)}, u32[]{:S(2)}) %all-to-all-start.3) | async-done | bytes 1048608 | tf_op jit(solution)/shard_map/all_to_all | solution.py:70
  160.0 14.4 %all_to_all.27 = bf16[16,8,1024]{2,1,0:T(8,128)(2,1)S(1)} all-to-all(bf16[16,8,1024]{2,1,0:T(8,128)(2,1)S(1)} %bitcast.29), channel_id=1, replica_groups=mesh['dp'=16,'tensor'=2] {'dp'}, dimensions={0} | all-to-all | bytes 524288 | tf_op jit(solution)/shard_map/all_to_all | solution.py:70
  174.8 1.2 collective-permute-done.5
  176.1 0.7 reshape.102
  (37 shorter events, 5.5 us)
Async XLA Ops:
  0.0 6.8 %collective-permute-start = (bf16[32,2048]{1,0:T(8,128)(2,1)}, bf16[32,2048]{1,0:T(8,128)(2,1)S(1)}, u32[]{:S(2)}, u32[]{:S(2)}) collective-permute-start(bf16[32,2048]{1,0:T(8,128)(2,1)} %bitcast.33), channel_id=1, source_target_pairs={{1,0},{0,1},{3,2},{2,3},{5,4},{4,5},{7,6},{6,7},{9,8},{8,9},{11,10... | collective-permute-start | bytes 393224 | tf_op jit(solution)/shard_map/ppermute | solution.py:53
  6.8 2.2 %copy-start.1 = (bf16[2048,1024]{1,0:T(8,128)(2,1)S(1)}, bf16[2048,1024]{1,0:T(8,128)(2,1)}, u32[]{:S(2)}) copy-start(bf16[2048,1024]{1,0:T(8,128)(2,1)} %refs_4_.2) | copy-start | bytes 12582916
  9.0 0.9 copy-start.7
  9.9 0.7 copy-start.8
  10.6 29.0 %copy-start.5 = (bf16[2,896,1024]{2,1,0:T(8,128)(2,1)S(1)}, bf16[2,896,1024]{2,1,0:T(8,128)(2,1)}, u32[]{:S(2)}) copy-start(bf16[2,896,1024]{2,1,0:T(8,128)(2,1)} %kv_ref.1) | copy-start | bytes 11010052
  52.4 19.3 %all-to-all-start.1 = ((bf16[16,16,1152]{2,1,0:T(8,128)(2,1)}), bf16[16,16,1152]{2,1,0:T(8,128)(2,1)S(1)}, u32[]{:S(2)}, u32[]{:S(2)}) async-start(bf16[16,16,1152]{2,1,0:T(8,128)(2,1)} %bitcast.13), calls=%async_computation.1 | async-start | bytes 1179648 | tf_op jit(solution)/shard_map/all_to_all | solution.py:70
  56.0 2.2 %copy-start.2 = (bf16[2048,1024]{1,0:T(8,128)(2,1)S(1)}, bf16[2048,1024]{1,0:T(8,128)(2,1)}, u32[]{:S(2)}) copy-start(bf16[2048,1024]{1,0:T(8,128)(2,1)} %key_ref.1) | copy-start | bytes 12582916
  58.2 2.2 %copy-start.3 = (bf16[2048,1024]{1,0:T(8,128)(2,1)S(1)}, bf16[2048,1024]{1,0:T(8,128)(2,1)}, u32[]{:S(2)}) copy-start(bf16[2048,1024]{1,0:T(8,128)(2,1)} %value_ref.1) | copy-start | bytes 12582916
  60.4 17.6 %copy-start.9 = (f32[2048]{0:T(1024)S(1)}, f32[2048]{0:T(1024)}, u32[]{:S(2)}) copy-start(f32[2048]{0:T(1024)} %param.28) | copy-start | bytes 24580
  71.7 2.2 %copy-start.4 = (bf16[1024,2048]{1,0:T(8,128)(2,1)S(1)}, bf16[1024,2048]{1,0:T(8,128)(2,1)}, u32[]{:S(2)}) copy-start(bf16[1024,2048]{1,0:T(8,128)(2,1)} %weight_ref.1) | copy-start | bytes 12582916
  76.3 1.6 collective-permute-start.1
  109.1 2.7 %collective-permute-start.2 = (bf16[16,32,1024]{2,1,0:T(8,128)(2,1)S(1)}, bf16[16,32,1024]{2,1,0:T(8,128)(2,1)S(1)}, u32[]{:S(2)}, u32[]{:S(2)}) collective-permute-start(bf16[16,32,1024]{2,1,0:T(8,128)(2,1)S(1)} %all_to_all.26.refs_1_), channel_id=1, source_target_pairs={{1,0},{0,1},{3,2},{2,3},{5,4},{4,5},{7,6},{6,7},{9,8},{8,9},{11,10... | collective-permute-start | bytes 3145736 | tf_op jit(solution)/shard_map/ppermute | solution.py:53
  126.6 2.7 %collective-permute-start.3 = (bf16[16,32,1024]{2,1,0:T(8,128)(2,1)S(1)}, bf16[16,32,1024]{2,1,0:T(8,128)(2,1)S(1)}, u32[]{:S(2)}, u32[]{:S(2)}) collective-permute-start(bf16[16,32,1024]{2,1,0:T(8,128)(2,1)S(1)} %get-tuple-element.39), channel_id=1, source_target_pairs={{0,1},{1,0},{2,3},{3,2},{4,5},{5,4},{6,7},{7,6},{8,9},{9,8},{10,11... | collective-permute-start | bytes 3145736 | tf_op jit(solution)/shard_map/ppermute | solution.py:63
  130.8 28.6 %all-to-all-start.3 = ((bf16[16,32,1024]{2,1,0:T(8,128)(2,1)}), bf16[16,32,1024]{2,1,0:T(8,128)(2,1)S(1)}, u32[]{:S(2)}, u32[]{:S(2)}) async-start(bf16[16,32,1024]{2,1,0:T(8,128)(2,1)} %add_convert_fusion), calls=%async_computation.3 | async-start | bytes 2097152 | tf_op jit(solution)/shard_map/all_to_all | solution.py:70
  134.7 2.6 %copy-start = (bf16[2048,2,704]{0,2,1:T(8,128)(2,1)S(1)}, bf16[2048,2,704]{0,2,1:T(8,128)(2,1)}, u32[]{:S(2)}) copy-start(bf16[2048,2,704]{0,2,1:T(8,128)(2,1)} %param.29) | copy-start | bytes 17301508
  137.4 1.8 %copy-start.6 = (bf16[704,2048]{1,0:T(8,128)(2,1)S(1)}, bf16[704,2048]{1,0:T(8,128)(2,1)}, u32[]{:S(2)}) copy-start(bf16[704,2048]{1,0:T(8,128)(2,1)} %refs_3_.1) | copy-start | bytes 8650756
  141.6 1.4 collective-permute-start.4
  174.7 1.3 collective-permute-start.5
where the time goes:
time: 178 us; the launch traced here: 177 us
  blocking collectives  70.7 us (40%)
  Pallas kernels  42.6 us (24%)
  waiting for transfers between devices  32.1 us (18%)
  local copies, waits for them, and re-layouts  19.5 us (11%)
  starting transfers between devices  8.38 us (5%)
  other arithmetic  3.2 us (2%)
    all_to_all x3, blocking collectives, exchange(): lax.all_to_all(blocks, 'dp', split_axis=0, concat_axis=0, tiled=True)  70.7 us
    all_to_all x2, waiting for transfers between devices, exchange(): lax.all_to_all(blocks, 'dp', split_axis=0, concat_axis=0, tiled=True)  22.8 us
    pallas_call x1, Pallas kernels, on_device(): pl.pallas_call(functools.partial(expert_kernel, tensors=tensors, experts=...  14.9 us
    unnamed x20, local copies, waits for them, and re-layouts  14.8 us
    pallas_call x1, Pallas kernels, on_device(): pl.pallas_call(functools.partial(owner_kernel, heads=step_heads, all_head...  12.8 us
    all_to_all x2, starting transfers between devices, exchange(): lax.all_to_all(blocks, 'dp', split_axis=0, concat_axis=0, tiled=True)  7.52 us
    ppermute x3, waiting for transfers between devices, ring_send(): lax.ppermute(pieces[step], 'tensor', [(i, (i + step) % count) for i in ra...  5.1 us
    pallas_call x1, Pallas kernels, on_device(): pl.pallas_call(functools.partial(leaf_kernel, heads=step_heads, leaf_len=...  4.82 us
  transfers between devices with their start and end apart: 8, of which 7 were waited for; matrix products, arithmetic and copies ran while one was open for 3% of the time, Pallas kernels for 4%

commit v1 on v0

v1 whole, which is shorter than its diff:
```python
import functools
import math

import jax
import jax.numpy as jnp
from jax import lax
from jax.experimental import pallas as pl
from jax.experimental.pallas import tpu as pltpu
from jax.sharding import PartitionSpec as P

HEAD_DIM = 128
EPS = 1e-06
ROPE_BASE = 10000.0
LANES = 128
HIDE = -1e30
LOG2E = 1.4426950408889634
LN2 = 0.6931471805599453
LEVEL_KEYS = (512, 256, 128)
MIB = 1 << 20

f32 = jnp.float32
bf16 = jnp.bfloat16


def dot(a, b):
    return lax.dot_general(a, b, (((1,), (0,)), ((), ())), preferred_element_type=f32)


def dot_nt(a, b):
    return lax.dot_general(a, b, (((1,), (1,)), ((), ())), preferred_element_type=f32)


def iota(shape, dim):
    return lax.broadcasted_iota(jnp.int32, shape, dim).astype(f32)


def divided(index, by):
    quotient = jnp.floor((index + 0.5) * (1.0 / by))
    return quotient, index - by * quotient


def one_hot(condition):
    return jnp.where(condition, 1.0, 0.0).astype(bf16)


def rms(values, gain):
    mean_square = jnp.mean(values * values, axis=-1, keepdims=True)
    return (values * lax.rsqrt(mean_square + EPS) * gain).astype(bf16)


def ring_get(piece, count):
    pieces = [piece]
    for step in range(1, count):
        pieces.append(
            lax.ppermute(piece, "tensor", [((i + step) % count, i) for i in range(count)])
        )
    return pieces


def ring_send(pieces):
    count = len(pieces)
    arrived = [pieces[0]]
    for step in range(1, count):
        arrived.append(
            lax.ppermute(pieces[step], "tensor", [(i, (i + step) % count) for i in range(count)])
        )
    return arrived


def exchange(rows, groups, halves=False):
    size = groups // 2 if halves else groups
    blocks = rows.reshape(size, rows.shape[0] // size, rows.shape[1])
    parts = [list(range(size)), list(range(size, groups))] if halves else None
    return lax.all_to_all(
        blocks, "dp", split_axis=0, concat_axis=0, tiled=True, axis_index_groups=parts
    ).reshape(rows.shape)


def from_partner(array, groups):
    return lax.ppermute(array, "dp", [(i, (i + groups // 2) % groups) for i in range(groups)])


def in_hbm(array):
    return pltpu.with_memory_space_constraint(array, pltpu.HBM)


def whole():
    return pl.BlockSpec(memory_space=pltpu.VMEM)


def scalar():
    return pl.BlockSpec(memory_space=pltpu.SMEM)


def params(mib, grid=0):
    return pltpu.CompilerParams(
        vmem_limit_bytes=mib * MIB,
        dimension_semantics=("arbitrary",) * grid if grid else None,
    )


def cost(flops, nbytes):
    return pl.CostEstimate(flops=int(flops), bytes_accessed=int(nbytes), transcendentals=0)


def upright(row):
    size = row.shape[1]
    diagonal = iota((size, size), 0) == iota((size, size), 1)
    return jnp.sum(jnp.where(diagonal, row, 0.0), axis=1, keepdims=True)


def in_rows(values, leaf_len):
    choices, requests, _ = values.shape
    rows = requests * leaf_len
    request_of_row, token_of_row = divided(iota((1, rows), 1), leaf_len)
    flat = values.astype(f32).reshape(choices * requests, leaf_len).astype(bf16)
    spread = dot(flat, one_hot(iota((leaf_len, 1), 0) == token_of_row))
    _, request = divided(iota((choices * requests, 1), 0), requests)
    kept = jnp.where(request == request_of_row, spread, 0.0)
    return jnp.sum(kept.reshape(choices, requests, rows), axis=1)


def across_rows(column):
    size = column.shape[0]
    diagonal = iota((size, size), 0) == iota((size, size), 1)
    return jnp.sum(jnp.where(diagonal, column, 0.0), axis=0, keepdims=True)


def owner_slots(owner):
    rows = []
    for level in range(3):
        mine, repeated = owner[level : level + 1], 0.0
        for earlier in range(level):
            same = upright(owner[earlier : earlier + 1]) == mine
            repeated = repeated + jnp.max(jnp.where(same, 1.0, 0.0), axis=0, keepdims=True)
        rows.append(mine * 2.0 + repeated)
    return rows


def prelude_kernel(
    owner_ref, start_ref, length_ref, request_ref, ids_ref, gates_ref,
    place_ref, meta_ref, cos_ref, sin_ref, table_ref,
    *, leaf_len,
):
    requests = owner_ref.shape[1]
    slot_rows, rows = place_ref.shape
    start, length = start_ref[...].astype(f32), length_ref[...].astype(f32)
    row_slot, row_token = divided(iota((slot_rows, 1), 0), leaf_len)
    request_of_row, token_of_row = divided(iota((1, rows), 1), leaf_len)
    named, first_key, key_count = 0.0, 0.0, 0.0
    for level, slot in enumerate(owner_slots(owner_ref[...].astype(f32))):
        here = jnp.where(slot == row_slot, 1.0, 0.0)
        named = named + here
        first_key = first_key + here * start[level : level + 1]
        key_count = key_count + here * length[level : level + 1]
    placed = dot(named.astype(bf16), one_hot(iota((requests, 1), 0) == request_of_row))
    place_ref[...] = jnp.where(row_token == token_of_row, placed, 0.0).astype(bf16)

    first_key = jnp.sum(first_key, axis=1, keepdims=True)
    key_count = jnp.sum(key_count, axis=1, keepdims=True)
    dest, place = divided(request_ref[...].astype(f32), requests)
    row_group, _ = divided(row_slot, 2)
    tag = jnp.sum(jnp.where(dest == row_group, place + 1.0, 0.0), axis=1, keepdims=True)
    lane = iota((1, LANES), 1)
    meta = jnp.zeros((slot_rows, LANES), f32)
    for at, value in enumerate(divided(first_key, 32) + divided(key_count, 32) + (tag,)):
        meta = jnp.where(lane == at, value, meta)
    meta_ref[...] = meta.astype(bf16)

    offsets = length[0:1] + length[1:2] + length[2:3]
    row_request, row_place = divided(iota((rows, 1), 0), leaf_len)
    mine = iota((1, requests), 1) == row_request
    position = jnp.sum(jnp.where(mine, offsets, 0.0), axis=1, keepdims=True) + row_place
    half = HEAD_DIM // 2
    pair = jnp.where(lane < half, lane, lane - half)
    angle = position * jnp.exp(pair * (-2.0 * math.log(ROPE_BASE) / HEAD_DIM))
    cos_ref[...] = jnp.cos(angle)
    sin_ref[...] = jnp.sin(angle) * jnp.where(lane < half, -1.0, 1.0)

    gates = gates_ref[...]
    gates_high = gates.astype(bf16).astype(f32)
    choices = gates.shape[0]
    for at, values in enumerate((ids_ref[...], gates_high, gates - gates_high)):
        table_ref[at * choices : (at + 1) * choices, :] = in_rows(values, leaf_len)
    dest_down = jnp.sum(jnp.where(mine, dest, 0.0), axis=1, keepdims=True)
    last = 3 * choices
    size = table_ref.shape[0] - last
    table_ref[last:, :] = jnp.broadcast_to(across_rows(dest_down), (size, rows))


def routing_kernel(
    half_ref, after_ref, owner_ref, table_ref, far_table_ref,
    pick_ref, send_ref, high_ref, low_ref, final_ref,
    *, leaf_len, groups, capacity, experts, choices,
):
    requests = owner_ref.shape[1]
    rows = requests * leaf_len
    slot_rows = groups * 2 * leaf_len
    row_request, row_place = divided(iota((rows, 1), 0), leaf_len)
    _, token_of_row = divided(iota((1, rows), 1), leaf_len)
    slot_across, token_across = divided(iota((1, slot_rows), 1), leaf_len)
    mine = iota((1, requests), 1) == row_request
    for level, slot in enumerate(owner_slots(owner_ref[...].astype(f32))):
        slot_down = jnp.sum(jnp.where(mine, slot, 0.0), axis=1, keepdims=True)
        pick_ref[level] = one_hot((slot_down == slot_across) & (row_place == token_across))

    slots = send_ref.shape[0]
    local = experts // groups
    block, slot_place = divided(iota((slots, 1), 0), capacity)
    block, local_expert = divided(block, local)
    device, slot_source = divided(block, 2)
    first_expert = (half_ref[0] * (experts // 2)).astype(f32)
    spread = one_hot(first_expert + device * local + local_expert == iota((1, experts), 1))
    expert_down = iota((experts, 1), 0)
    ahead = one_hot(iota((rows, rows), 0) < iota((rows, rows), 1))
    final_group, final_token = divided(iota((slot_rows, 1), 0), leaf_len)
    final_group, final_source = divided(final_group, 2)
    send, high, low, final = [], [], [], []
    for source, table in enumerate((table_ref[...], far_table_ref[...])):
        member, gate_high, gate_low = 0.0, 0.0, 0.0
        for choice in range(choices):
            hit = jnp.where(table[choice : choice + 1] == expert_down, 1.0, 0.0)
            member = member + hit
            gate_high = gate_high + hit * table[choices + choice : choices + choice + 1]
            gate_low = gate_low + hit * table[2 * choices + choice : 2 * choices + choice + 1]
        member = member.astype(bf16)
        before = dot(member, ahead).astype(bf16)
        taken = (dot(spread, member) > 0.5) & (dot(spread, before) == slot_place)
        taken = taken & (slot_source == source)
        send.append(jnp.where(taken, 1.0, 0.0))
        high.append(jnp.where(taken, dot(spread, gate_high.astype(bf16)), 0.0))
        low.append(jnp.where(taken, dot(spread, gate_low.astype(bf16)), 0.0))
        going = (table[3 * choices : 3 * choices + 1] == final_group) & (final_source == source)
        final.append(jnp.where(going & (final_token == token_of_row), 1.0, 0.0))
    send_ref[...] = jnp.concatenate(send, axis=1).astype(bf16)
    high_ref[...] = jnp.transpose(jnp.concatenate(high, axis=1)).astype(bf16)
    low_ref[...] = jnp.transpose(jnp.concatenate(low, axis=1)).astype(bf16)
    final_ref[...] = jnp.concatenate(final, axis=1).astype(bf16)


def rotated(product, cosine, sine, heads):
    columns = []
    for head in range(heads):
        part = product[:, head * HEAD_DIM : (head + 1) * HEAD_DIM]
        columns.append(part * cosine + pltpu.roll(part, HEAD_DIM // 2, 1) * sine)
    return jnp.concatenate(columns, axis=1).astype(bf16)


def query_kernel(*refs, tensors, heads):
    index_ref, pieces, refs = refs[0], refs[1 : 1 + tensors], refs[1 + tensors :]
    (gain_ref, weight_ref, cos_ref, sin_ref, place_ref, meta_ref,
     raw_ref, normed_ref, query_ref, send_ref, buffer_ref, semaphores) = refs
    width = heads * HEAD_DIM
    copies = column_copies(weight_ref, buffer_ref, semaphores, width)
    shard = pieces[0].shape[0]
    for at, piece in enumerate(pieces):
        owner = lax.rem(index_ref[0] + at, tensors)
        raw_ref[pl.ds(pl.multiple_of(owner * shard, shard), shard), :] = piece[...]
    normed_ref[...] = rms(raw_ref[...].astype(f32), gain_ref[...])
    send_ref[:, send_ref.shape[1] - LANES :] = meta_ref[...]
    for at, copy in enumerate(copies):
        copy.wait()
        columns = slice(at * width, (at + 1) * width)
        product = dot(normed_ref[...], buffer_ref[:, columns])
        query = rotated(product, cos_ref[...], sin_ref[...], heads)
        query_ref[:, columns] = query
        send_ref[:, columns] = dot(place_ref[...], query).astype(bf16)


def leaf_kernel(
    normed_ref, query_ref, key_ref, value_ref, cos_ref, sin_ref, out_ref, lse_ref,
    *, heads, leaf_len, scale,
):
    step = pl.program_id(0)
    normed = normed_ref[...]
    rows = normed.shape[0]
    keys = rotated(dot(normed, key_ref[...]), cos_ref[...], sin_ref[...], heads)
    values = dot(normed, value_ref[...]).astype(bf16)
    down, across = iota((rows, 1), 0), iota((1, rows), 1)
    visible = (divided(down, leaf_len)[0] == divided(across, leaf_len)[0]) & (across <= down)
    lane = lax.broadcasted_iota(jnp.int32, (1, LANES), 1)

    @pl.when(step == 0)
    def _():
        lse_ref[...] = jnp.zeros_like(lse_ref)

    for head in range(heads):
        at = slice(head * HEAD_DIM, (head + 1) * HEAD_DIM)
        scores = jnp.where(visible, dot_nt(query_ref[:, at], keys[:, at]) * scale, HIDE)
        highest = jnp.max(scores, axis=1, keepdims=True)
        weights = jnp.exp(scores - highest)
        total = jnp.sum(weights, axis=1, keepdims=True)
        out_ref[:, at] = dot(weights.astype(bf16), values[:, at]) / total
        lse = highest + jnp.log(total)
        lse_ref[...] = jnp.where(lane == step * heads + head, lse, lse_ref[...])


def owner_kernel(
    arrived_ref, kv_ref, back_ref, query_ref, out_ref,
    *, heads, requests, leaf_len, scale,
):
    slot_rows = arrived_ref.shape[0]
    width = heads * HEAD_DIM
    count = requests * leaf_len
    packed = arrived_ref[:, width:]
    meta = packed.astype(f32)
    first = meta[:, 0:1] * 32.0 + meta[:, 1:2]
    used = meta[:, 2:3] + meta[:, 3:4] > 0.0
    begins = [sum(LEVEL_KEYS[:level]) for level in range(3)]
    level = jnp.where(first >= begins[1], 1.0, 0.0) + jnp.where(first >= begins[2], 1.0, 0.0)
    level = jnp.where(used, level, 3.0)
    lane = lax.broadcasted_iota(jnp.int32, (1, LANES), 1)
    of_level = level == lane.astype(f32)
    ahead = one_hot(iota((slot_rows, slot_rows), 1) < iota((slot_rows, slot_rows), 0))
    rank = dot(ahead, one_hot(of_level))
    rank = jnp.sum(jnp.where(of_level, rank, 0.0), axis=1, keepdims=True)
    target = jnp.where(used, level * count + rank, -1.0)
    spread = jnp.where(target == iota((1, 3 * count), 1), 1.0, 0.0)
    ordered = jnp.transpose(spread).astype(bf16)
    query_ref[...] = dot(ordered, arrived_ref[:, :width]).astype(bf16)
    meta = dot(ordered, packed)
    first = meta[:, 0:1] * 32.0 + meta[:, 1:2]
    last = first + meta[:, 2:3] * 32.0 + meta[:, 3:4]
    for level in range(3):
        size = LEVEL_KEYS[level]
        part = slice(level * count, (level + 1) * count)
        keys = slice(begins[level], begins[level] + size)
        key = iota((1, size), 1) + float(begins[level])
        bias = jnp.where((key >= first[part]) & (key < last[part]), 0.0, HIDE)
        ones = jnp.ones((size, HEAD_DIM), bf16)
        sums = jnp.zeros((count, LANES), f32)
        for head in range(heads):
            at = slice(head * HEAD_DIM, (head + 1) * HEAD_DIM)
            scores = dot_nt(query_ref[part, at], kv_ref[0, keys, at]) * (scale * LOG2E) + bias
            highest = jnp.max(scores, axis=1, keepdims=True)
            weights = jnp.exp2(scores - highest).astype(bf16)
            both = dot(weights, jnp.concatenate([kv_ref[1, keys, at], ones], axis=1))
            total = both[:, HEAD_DIM:]
            out_ref[part, at] = (both[:, :HEAD_DIM] / total).astype(bf16)
            lse = highest * LN2 + jnp.log(total)
            lse_high = lse.astype(bf16).astype(f32)
            sums = jnp.where(lane == head, lse_high, sums)
            sums = jnp.where(lane == head + heads, lse - lse_high, sums)
        out_ref[part, width:] = sums.astype(bf16)
    back_ref[...] = dot(spread.astype(bf16), out_ref[...]).astype(bf16)


def column_copies(source_ref, target_ref, semaphores, step):
    copies = []
    for at in range(source_ref.shape[1] // step):
        columns = pl.ds(at * step, step)
        copy = pltpu.make_async_copy(
            source_ref.at[:, columns], target_ref.at[:, columns], semaphores.at[at]
        )
        copy.start()
        copies.append(copy)
    return copies


def merge_kernel(
    back_ref, pick_ref, leaf_ref, lse_ref, weight_ref, out_ref, buffer_ref, attended_ref, semaphores,
    *, heads, step,
):
    copies = column_copies(weight_ref, buffer_ref, semaphores, step)
    width = heads * HEAD_DIM
    back = back_ref[...]
    outputs, sums = [leaf_ref[...]], [lse_ref[...]]
    for level in range(3):
        rows = dot(pick_ref[level], back)
        outputs.append(rows[:, :width])
        tail = rows[:, width:]
        sums.append(tail + pltpu.roll(tail, LANES - heads, 1))
    highest = functools.reduce(jnp.maximum, sums)
    scales = [jnp.exp(one - highest) for one in sums]
    total = sum(scales[1:], scales[0])
    scales = [one / total for one in scales]
    for head in range(heads):
        at = slice(head * HEAD_DIM, (head + 1) * HEAD_DIM)
        mixed = sum(scales[i][:, head : head + 1] * outputs[i][:, at] for i in range(4))
        attended_ref[:, at] = mixed.astype(bf16)
    for at, copy in enumerate(copies):
        copy.wait()
        columns = slice(at * step, (at + 1) * step)
        out_ref[:, columns] = dot(attended_ref[...], buffer_ref[:, columns]).astype(bf16)


def middle_kernel(*refs, tensors):
    index_ref, raw_ref, gain_ref = refs[:3]
    pieces = refs[3 : 3 + tensors]
    normed_ref, own_ref, resid_own_ref, resid_ref = refs[3 + tensors :]
    width = own_ref.shape[1]
    own = pl.ds(pl.multiple_of(index_ref[0] * width, width), width)
    total = raw_ref[...].astype(f32)
    for piece in pieces:
        total = total + piece[...].astype(f32)
    resid_ref[...] = total
    resid_own_ref[...] = resid_ref[:, own]
    normed_ref[...] = rms(total, gain_ref[...])
    own_ref[...] = normed_ref[:, own]


def dispatch_kernel(after_ref, also_after_ref, send_ref, own_ref, far_ref, out_ref):
    both = jnp.concatenate([own_ref[...], far_ref[...]], axis=0)
    out_ref[...] = dot(send_ref[...], both).astype(bf16)


def shared_kernel(*refs, tensors):
    index_ref, rows_ref, in_hbm_ref, down_hbm_ref = refs[:4]
    pieces, refs = refs[4 : 4 + tensors], refs[4 + tensors :]
    in_ref, down_ref, total_ref, semaphores = refs
    copies = [
        pltpu.make_async_copy(in_hbm_ref.at[0], in_ref.at[0], semaphores.at[0]),
        pltpu.make_async_copy(in_hbm_ref.at[1], in_ref.at[1], semaphores.at[1]),
        pltpu.make_async_copy(down_hbm_ref, down_ref, semaphores.at[2]),
    ]
    for copy in copies:
        copy.start()
    rows = rows_ref[...]
    copies[0].wait()
    gate = dot_nt(rows, in_ref[0])
    copies[1].wait()
    up = dot_nt(rows, in_ref[1])
    hidden = (gate / (1.0 + jnp.exp(-gate)) * up).astype(bf16)
    copies[2].wait()
    total_ref[...] = dot(hidden, down_ref[...])
    width = pieces[0].shape[1]
    for at, piece in enumerate(pieces):
        column = lax.rem(index_ref[0] + at, tensors) * width
        piece[...] = total_ref[:, pl.ds(pl.multiple_of(column, width), width)].astype(bf16)


def load_kernel(after_ref, in_ref, down_ref, in_out_ref, down_out_ref, semaphores):
    copies = [
        pltpu.make_async_copy(in_ref.at[0], in_out_ref, semaphores.at[0]),
        pltpu.make_async_copy(down_ref.at[0], down_out_ref, semaphores.at[1]),
    ]
    for copy in copies:
        copy.start()
    for copy in copies:
        copy.wait()


def rows_of_experts(piece, experts, capacity):
    groups, _, width = piece.shape
    values = piece[...].astype(f32)
    for e in range(experts):
        mine = values[:, e * capacity : (e + 1) * capacity, :].reshape(groups * capacity, width)
        yield mine.astype(bf16)


def expert_kernel(*refs, tensors, experts, capacity):
    index_ref, arrived, refs = refs[0], refs[1 : 1 + tensors], refs[1 + tensors :]
    (first_in_ref, first_down_ref, in_hbm_ref, down_hbm_ref), refs = refs[:4], refs[4:]
    pieces, refs = refs[:tensors], refs[tensors:]
    in_ref, down_ref, rows_ref, total_ref, semaphores = refs
    copies = []
    for e in range(1, experts):
        copies.append(
            (
                pltpu.make_async_copy(in_hbm_ref.at[e], in_ref.at[e - 1], semaphores.at[0, e]),
                pltpu.make_async_copy(down_hbm_ref.at[e], down_ref.at[e - 1], semaphores.at[1, e]),
            )
        )
        for copy in copies[-1]:
            copy.start()
    groups, _, width = arrived[0].shape
    columns = [
        pl.ds(pl.multiple_of(lax.rem(index_ref[0] + at, tensors) * width, width), width)
        for at in range(tensors)
    ]
    for at, piece in enumerate(arrived):
        for e, rows in enumerate(rows_of_experts(piece, experts, capacity)):
            rows_ref[e, :, columns[at]] = rows
    for e in range(experts):
        if e == 0:
            gate_weight, up_weight, down = first_in_ref.at[0], first_in_ref.at[1], first_down_ref
        else:
            gate_weight, up_weight, down = in_ref.at[e - 1, 0], in_ref.at[e - 1, 1], down_ref.at[e - 1]
            copies[e - 1][0].wait()
        gate = dot_nt(rows_ref[e], gate_weight[...])
        up = dot_nt(rows_ref[e], up_weight[...])
        hidden = (gate / (1.0 + jnp.exp(-gate)) * up).astype(bf16)
        if e > 0:
            copies[e - 1][1].wait()
        mine = slice(e * capacity, (e + 1) * capacity)
        for at in range(tensors):
            value = dot(hidden, down[:, columns[at]])
            total_ref[at, :, mine, :] = value.reshape(groups, capacity, width)
    for at, piece in enumerate(pieces):
        piece[...] = total_ref[at].astype(bf16)


def add_kernel(*refs):
    out_ref = refs[-1]
    out_ref[...] = sum(piece[...].astype(f32) for piece in refs[:-1]).astype(bf16)


def combine_kernel(*refs, tensors):
    returned_ref, high_ref, low_ref, resid_ref, final_ref = refs[:5]
    shared, out_ref = refs[5 : 5 + tensors], refs[5 + tensors]
    returned = returned_ref[...]
    routed = dot(high_ref[...], returned) + dot(low_ref[...], returned)
    rows = resid_ref.shape[0]
    total = resid_ref[...]
    for piece in shared:
        total = total + piece[...].astype(f32)
    both = jnp.concatenate([total + routed[:rows], routed[rows:]], axis=0).astype(bf16)
    out_ref[...] = dot(final_ref[...], both).astype(bf16)


def settle_kernel(*refs, tensors, leaf_len, groups):
    index_ref, meta_ref, rows_ref = refs[:3]
    pieces = refs[3:]
    slot_rows = meta_ref.shape[0]
    places = pieces[0].shape[0]
    share = leaf_len // tensors
    tag_down = meta_ref[...].astype(f32)[:, 4:5]
    block, token = divided(iota((1, slot_rows), 1), leaf_len)
    group, source = divided(block, 2)
    _, home = divided(group + source * (groups // 2), groups)
    tagged = iota((slot_rows, 1), 0) == home * (2.0 * leaf_len) + token
    tag = jnp.sum(jnp.where(tagged, tag_down, 0.0), axis=0, keepdims=True)
    request, position = divided(iota((places, 1), 0), share)
    for at, piece in enumerate(pieces):
        shift = (lax.rem(index_ref[0] + at, tensors) * share).astype(f32)
        chosen = one_hot((tag == request + 1.0) & (token == position + shift))
        piece[...] = dot(chosen, rows_ref[...]).astype(bf16)


def on_device(
    leaf_tokens,
    attn_gain,
    w_query,
    w_key,
    w_value,
    w_out,
    prefix_kv,
    prefix_owner,
    prefix_start,
    prefix_len,
    mlp_gain,
    shared_in,
    shared_out,
    expert_in,
    expert_out,
    expert_ids,
    gate_weights,
    request_of,
):
    groups = lax.axis_size("dp")
    tensors = lax.axis_size("tensor")
    index = lax.axis_index("tensor").astype(jnp.int32).reshape(1)
    shard_requests, leaf_len, model_width = leaf_tokens.shape
    requests = prefix_owner.shape[0]
    rows = requests * leaf_len
    local_width = w_query.shape[1]
    local_heads = local_width // HEAD_DIM
    scale = HEAD_DIM ** (-0.5)
    column_share = model_width // tensors
    top_count = expert_ids.shape[2]
    local_experts = expert_in.shape[0]
    experts = local_experts * groups
    assignments = rows * top_count
    capacity = tensors * max(1, assignments * 4 // (experts * 3 * tensors))
    slots = experts * capacity
    slot_rows = groups * 2 * leaf_len
    shape = jax.ShapeDtypeStruct

    raw_pieces = ring_get(leaf_tokens.reshape(shard_requests * leaf_len, model_width), tensors)

    owner_rows, request_row = prefix_owner.T, request_of.reshape(1, requests)
    table_rows = -(-(3 * top_count + 1) // 8) * 8
    place, meta, cosine, sine, table = pl.pallas_call(
        functools.partial(prelude_kernel, leaf_len=leaf_len),
        out_shape=[
            shape((slot_rows, rows), bf16),
            shape((slot_rows, LANES), bf16),
            shape((rows, LANES), f32),
            shape((rows, LANES), f32),
            shape((table_rows, rows), f32),
        ],
        in_specs=[whole()] * 6,
        out_specs=[whole()] * 5,
        compiler_params=params(24),
        name="prelude",
    )(
        in_hbm(owner_rows), in_hbm(prefix_start.T), in_hbm(prefix_len.T), in_hbm(request_row),
        in_hbm(jnp.transpose(expert_ids, (2, 0, 1))),
        in_hbm(jnp.transpose(gate_weights, (2, 0, 1))),
    )
    far_table = from_partner(table, groups)

    step_heads = min(2, local_heads)
    step_width = step_heads * HEAD_DIM
    steps = local_heads // step_heads
    query_heads = min(4, local_heads)
    fixed = lambda *dims: pl.BlockSpec(dims, lambda i: (0,) * len(dims))
    columns = lambda *dims: pl.BlockSpec(dims, lambda i: (0,) * (len(dims) - 1) + (i,))
    send_width = local_width + LANES
    raw, normed, query, query_send = pl.pallas_call(
        functools.partial(query_kernel, tensors=tensors, heads=query_heads),
        out_shape=[
            shape((rows, model_width), bf16),
            shape((rows, model_width), bf16),
            shape((rows, local_width), bf16),
            shape((slot_rows, send_width), bf16),
        ],
        in_specs=[scalar()]
        + [whole()] * (tensors + 1)
        + [pl.BlockSpec(memory_space=pltpu.HBM)]
        + [whole()] * 4,
        out_specs=[whole()] * 4,
        scratch_shapes=[
            pltpu.VMEM((model_width, local_width), bf16),
            pltpu.SemaphoreType.DMA((local_heads // query_heads,)),
        ],
        compiler_params=params(24),
        cost_estimate=cost(2 * rows * model_width * local_width, 2 * model_width * local_width),
        name="queries",
    )(
        index, in_hbm(raw_pieces[0]), *raw_pieces[1:], in_hbm(attn_gain.reshape(1, -1)), in_hbm(w_query),
        cosine, sine, place, meta,
    )

    query_arrived = exchange(query_send, groups)

    leaf_out, leaf_lse = pl.pallas_call(
        functools.partial(leaf_kernel, heads=step_heads, leaf_len=leaf_len, scale=scale),
        grid=(steps,),
        out_shape=[shape((rows, local_width), f32), shape((rows, LANES), f32)],
        in_specs=[
            fixed(rows, model_width),
            columns(rows, step_width),
            columns(model_width, step_width),
            columns(model_width, step_width),
            fixed(rows, LANES),
            fixed(rows, LANES),
        ],
        out_specs=[columns(rows, step_width), fixed(rows, LANES)],
        compiler_params=params(24, 1),
        cost_estimate=cost(4 * rows * model_width * local_width, 4 * model_width * local_width),
        name="leaf",
    )(normed, query, in_hbm(w_key), in_hbm(w_value), cosine, sine)

    half = (lax.axis_index("dp") // (groups // 2)).astype(jnp.int32).reshape(1)
    pick, send, gate_high, gate_low, final = pl.pallas_call(
        functools.partial(
            routing_kernel, leaf_len=leaf_len, groups=groups, capacity=capacity, experts=experts,
            choices=top_count,
        ),
        out_shape=[
            shape((3, rows, slot_rows), bf16),
            shape((slots, 2 * rows), bf16),
            shape((2 * rows, slots), bf16),
            shape((2 * rows, slots), bf16),
            shape((slot_rows, 2 * rows), bf16),
        ],
        in_specs=[scalar(), pl.BlockSpec(memory_space=pl.ANY)] + [whole()] * 3,
        out_specs=[whole()] * 5,
        compiler_params=params(24),
        cost_estimate=cost(1 << 30, 1 << 20),
        name="routing",
    )(half, query_arrived, owner_rows, table, far_table)

    pool = prefix_kv.shape[1]
    back_send = pl.pallas_call(
        functools.partial(
            owner_kernel, heads=local_heads, requests=requests, leaf_len=leaf_len, scale=scale
        ),
        out_shape=shape((slot_rows, send_width), bf16),
        in_specs=[whole()] * 2,
        out_specs=whole(),
        scratch_shapes=[
            pltpu.VMEM((3 * rows, local_width), bf16),
            pltpu.VMEM((3 * rows, send_width), bf16),
        ],
        compiler_params=params(32),
        cost_estimate=cost(4 * slot_rows * pool * local_width, 4 * pool * local_width),
        name="owner",
    )(query_arrived, prefix_kv)

    back = exchange(back_send, groups)

    out_step = min(512, model_width)
    partial_out = pl.pallas_call(
        functools.partial(merge_kernel, heads=local_heads, step=out_step),
        out_shape=shape((rows, model_width), bf16),
        in_specs=[whole()] * 4 + [pl.BlockSpec(memory_space=pltpu.HBM)],
        out_specs=whole(),
        scratch_shapes=[
            pltpu.VMEM((local_width, model_width), bf16),
            pltpu.VMEM((rows, local_width), bf16),
            pltpu.SemaphoreType.DMA((model_width // out_step,)),
        ],
        compiler_params=params(24),
        cost_estimate=cost(2 * rows * local_width * model_width, 2 * local_width * model_width),
        name="merge",
    )(back, pick, leaf_out, leaf_lse, in_hbm(w_out))

    out_pieces = ring_get(partial_out, tensors)

    normed_mlp, own_columns, resid_own = pl.pallas_call(
        functools.partial(middle_kernel, tensors=tensors),
        out_shape=[
            shape((rows, model_width), bf16),
            shape((rows, column_share), bf16),
            shape((rows, column_share), f32),
        ],
        in_specs=[scalar()] + [whole()] * (2 + tensors),
        out_specs=[whole()] * 3,
        scratch_shapes=[pltpu.VMEM((rows, model_width), f32)],
        compiler_params=params(24),
        name="middle",
    )(index, raw, mlp_gain.reshape(1, -1), *out_pieces)

    far_columns = from_partner(own_columns, groups)
    hbm = pl.BlockSpec(memory_space=pltpu.HBM)
    hidden = shared_out.shape[0]
    shared_pieces = pl.pallas_call(
        functools.partial(shared_kernel, tensors=tensors),
        out_shape=[shape((rows, column_share), bf16)] * tensors,
        in_specs=[scalar(), whole(), hbm, hbm],
        out_specs=[whole()] * tensors,
        scratch_shapes=[
            pltpu.VMEM((2, hidden, model_width), bf16),
            pltpu.VMEM((hidden, model_width), bf16),
            pltpu.VMEM((rows, model_width), f32),
            pltpu.SemaphoreType.DMA((3,)),
        ],
        compiler_params=params(16),
        cost_estimate=cost(1, 1),
        name="shared",
    )(index, normed_mlp, in_hbm(jnp.transpose(shared_in, (1, 2, 0))), in_hbm(shared_out))
    expert_hidden = expert_out.shape[1]
    expert_in = in_hbm(jnp.transpose(expert_in, (0, 2, 3, 1)))
    expert_out = in_hbm(expert_out)
    first_in, first_down = pl.pallas_call(
        load_kernel,
        out_shape=[
            pltpu.VMEM((2, expert_hidden, model_width), bf16),
            pltpu.VMEM((expert_hidden, model_width), bf16),
        ],
        in_specs=[pl.BlockSpec(memory_space=pl.ANY), hbm, hbm],
        out_specs=[whole()] * 2,
        scratch_shapes=[pltpu.SemaphoreType.DMA((2,))],
        compiler_params=params(1),
        cost_estimate=cost(1, 1),
        name="load",
    )(normed_mlp, expert_in, expert_out)

    send_rows = pl.pallas_call(
        dispatch_kernel,
        out_shape=shape((slots, column_share), bf16),
        in_specs=[pl.BlockSpec(memory_space=pl.ANY)] * 2 + [whole()] * 3,
        out_specs=whole(),
        compiler_params=params(8),
        name="dispatch",
    )(shared_pieces[0], first_down, send, own_columns, far_columns)

    arrived = exchange(send_rows, groups, halves=True)

    block = local_experts * capacity
    arrived_pieces = ring_get(arrived.reshape(groups, block, column_share), tensors)
    partial_pieces = pl.pallas_call(
        functools.partial(
            expert_kernel, tensors=tensors, experts=local_experts, capacity=capacity
        ),
        out_shape=[shape((groups, block, column_share), bf16)] * tensors,
        in_specs=[scalar()] + [whole()] * (tensors + 2) + [hbm, hbm],
        out_specs=[whole()] * tensors,
        scratch_shapes=[
            pltpu.VMEM((local_experts - 1, 2, expert_hidden, model_width), bf16),
            pltpu.VMEM((local_experts - 1, expert_hidden, model_width), bf16),
            pltpu.VMEM((local_experts, groups * capacity, model_width), bf16),
            pltpu.VMEM((tensors, groups, block, column_share), f32),
            pltpu.SemaphoreType.DMA((2, local_experts)),
        ],
        compiler_params=params(35),
        cost_estimate=cost(
            6 * slots * expert_hidden * model_width,
            6 * local_experts * expert_hidden * model_width,
        ),
        name="experts",
    )(
        index,
        *arrived_pieces,
        pltpu.with_memory_space_constraint(first_in, pltpu.VMEM),
        pltpu.with_memory_space_constraint(first_down, pltpu.VMEM),
        expert_in,
        expert_out,
    )
    partial_pieces = ring_send(partial_pieces)
    summed = pl.pallas_call(
        add_kernel,
        out_shape=shape((groups, block, column_share), bf16),
        in_specs=[whole()] * tensors,
        out_specs=whole(),
        compiler_params=params(12),
        name="add",
    )(*partial_pieces)

    shared_pieces = ring_send(shared_pieces)
    returned = exchange(summed.reshape(slots, column_share), groups, halves=True)

    final_send = pl.pallas_call(
        functools.partial(combine_kernel, tensors=tensors),
        out_shape=shape((slot_rows, column_share), bf16),
        in_specs=[whole()] * (5 + tensors),
        out_specs=whole(),
        compiler_params=params(24),
        name="combine",
    )(returned, gate_high, gate_low, resid_own, final, *shared_pieces)

    final_arrived = exchange(final_send, groups)

    places = requests * (leaf_len // tensors)
    settled = pl.pallas_call(
        functools.partial(
            settle_kernel, tensors=tensors, leaf_len=leaf_len, groups=groups
        ),
        grid=(1,),
        out_shape=[shape((places, column_share), bf16)] * tensors,
        in_specs=[
            scalar(),
            pl.BlockSpec((slot_rows, LANES), lambda i: (0, local_heads)),
            fixed(slot_rows, column_share),
        ],
        out_specs=[fixed(places, column_share)] * tensors,
        compiler_params=params(24, 1),
        name="settle",
    )(index, query_arrived, final_arrived)
    settled = ring_send(settled)
    if tensors == 2:
        first = index[0] == 0
        own, other = settled
        result = jnp.concatenate(
            [jnp.where(first, own, other), jnp.where(first, other, own)], axis=1
        )
    else:
        result = jnp.zeros((places, model_width), bf16)
        for at, piece in enumerate(settled):
            column = ((index[0] - at + tensors) % tensors) * column_share
            result = lax.dynamic_update_slice(result, piece, (0, column))
    return result.reshape(requests, leaf_len // tensors, model_width)


def solution(mesh):
    in_specs = (
        P(("dp", "tensor"), None, None),
        P(),
        P(None, "tensor"),
        P(None, "tensor"),
        P(None, "tensor"),
        P("tensor", None),
        P(None, "dp", "tensor"),
        P("dp", None),
        P("dp", None),
        P("dp", None),
        P(),
        P(None, None, "tensor"),
        P("tensor", None),
        P("dp", None, None, "tensor"),
        P("dp", "tensor", None),
        P("dp", None, None),
        P("dp", None, None),
        P("dp"),
    )
    out_specs = P("dp", "tensor", None)
    return jax.shard_map(
        on_device, mesh=mesh, in_specs=in_specs, out_specs=out_specs, check_vma=False
    )
```

time: 178 us -> 151 us (0.85)
  local copies, waits for them, and re-layouts: 19.5 us -> 0.72 us
  blocking collectives: 70.7 us -> 64.4 us
  other arithmetic: 3.2 us -> 0.02 us
  starting transfers between devices: 8.38 us -> 11.4 us
  waiting for transfers between devices: 32.1 us -> 29.9 us
  Pallas kernels: 42.6 us -> 44.4 us
    unnamed x20 -> x6, local copies, waits for them, and re-layouts: 14.8 us -> 0.01 us
    all_to_all x2, waiting for transfers between devices: 22.8 us -> 13.7 us  [exchange(): lax.all_to_all(blocks, 'dp', split_axis=0, concat_axis=0, tiled=True, axi...]
    ppermute x0 -> x2, waiting for transfers between devices: none -> 7.11 us  [from_partner(): lax.ppermute(array, 'dp', [(i, (i + groups // 2) % groups) for i in range...]
    all_to_all x3, blocking collectives: 70.7 us -> 64.4 us  [exchange(): lax.all_to_all(blocks, 'dp', split_axis=0, concat_axis=0, tiled=True, axi...]
    reshape x5 -> x0, local copies, waits for them, and re-layouts: 3.92 us -> none  [the longest x1 0.81 us: on_device(): ids = jnp.transpose(expert_ids, (2, 0, 1)).reshape(top_count, rows)]
    ppermute x0 -> x2, starting transfers between devices: none -> 3.22 us  [from_partner(): lax.ppermute(array, 'dp', [(i, (i + groups // 2) % groups) for i in range...]
    pallas_call x1, Pallas kernels: 2.36 us -> 4.86 us  [on_device(): pl.pallas_call(functools.partial(shared_kernel, tensors=tensors), out_sha...]
    pallas_call x1, Pallas kernels: 14.9 us -> 12.7 us  [on_device(): pl.pallas_call(functools.partial(expert_kernel, tensors=tensors, experts=...]
  transfers between devices with their start and end apart: 8 -> 10, of which waited for: 7 -> 8; matrix products, arithmetic and copies ran while one was open for 3% -> 0% of each run, Pallas kernels for 4% -> 11%
where the time goes in v1:
time: 151 us
  blocking collectives  64.4 us (43%)
  Pallas kernels  44.4 us (29%)
  waiting for transfers between devices  29.9 us (20%)
  starting transfers between devices  11.4 us (8%)
    all_to_all x3, blocking collectives, exchange(): lax.all_to_all(blocks, 'dp', split_axis=0, concat_axis=0, tiled=True, axi...  64.4 us
    all_to_all x2, waiting for transfers between devices, exchange(): lax.all_to_all(blocks, 'dp', split_axis=0, concat_axis=0, tiled=True, axi...  13.7 us
    pallas_call x1, Pallas kernels, on_device(): pl.pallas_call(functools.partial(expert_kernel, tensors=tensors, experts=...  12.7 us
    all_to_all x2, starting transfers between devices, exchange(): lax.all_to_all(blocks, 'dp', split_axis=0, concat_axis=0, tiled=True, axi...  7.14 us
    ppermute x2, waiting for transfers between devices, from_partner(): lax.ppermute(array, 'dp', [(i, (i + groups // 2) % groups) for i in range...  7.11 us
    pallas_call x1, Pallas kernels, on_device(): pl.pallas_call(functools.partial(leaf_kernel, heads=step_heads, leaf_len=...  6.08 us
    pallas_call x1, Pallas kernels, on_device(): pl.pallas_call(functools.partial(owner_kernel, heads=local_heads, request...  5.15 us
    ppermute x3, waiting for transfers between devices, ring_send(): lax.ppermute(pieces[step], 'tensor', [(i, (i + step) % count) for i in ra...  4.97 us
  transfers between devices with their start and end apart: 10, of which 8 were waited for; matrix products, arithmetic and copies ran while one was open for 0% of the time, Pallas kernels for 11%

profile of v1, /device:TPU:0, one launch (start us, length us, event | category | flops | bytes accessed | tf_op | source)
XLA Modules:
  0.0 151.0 jit_solution(12371030775237468282)
XLA Ops:
  0.0 0.5 collective-permute-start
  0.5 1.4 prelude.1
  1.9 4.1 %queries.1 = (bf16[64,2048]{1,0:T(8,128)(2,1)S(1)}, bf16[64,2048]{1,0:T(8,128)(2,1)S(1)}, bf16[64,1024]{1,0:T(8,128)(2,1)S(1)}, bf16[256,1152]{1,0:T(8,128)(2,1)S(1)}) custom-call(s32[1]{0:T(128)} %bitcast.refs_0_, bf16[32,2048]{1,0:T(8,128)(2,1)} %bitcast.41, bf16[32,2048]{1,0:T(8,128)(2,1)S(1)} %collective-permute-done.refs_2_, f32[1,2048]{1,0:T(1,128)} %bitcast.44, ...), custom_call_target="tpu_custom_call" | custom-call | flops 268435456 | bytes 4194304 | tf_op jit(solution)/shard_map/queries/pallas_call | solution.py:600
  6.0 25.8 %all_to_all.25 = bf16[16,16,1152]{2,1,0:T(8,128)(2,1)S(1)} all-to-all(bf16[16,16,1152]{2,1,0:T(8,128)(2,1)S(1)} %bitcast.33), channel_id=1, replica_groups=mesh['dp'=16,'tensor'=2] {'dp'}, dimensions={0} | all-to-all | bytes 1179648 | tf_op jit(solution)/shard_map/all_to_all | solution.py:74
  31.8 5.1 %owner.1 = bf16[256,1152]{1,0:T(8,128)(2,1)} custom-call(bf16[256,1152]{1,0:T(8,128)(2,1)S(1)} %bitcast.23, bf16[2,896,1024]{2,1,0:T(8,128)(2,1)S(1)} %copy-done), custom_call_target="tpu_custom_call" | custom-call | flops 939524096 | bytes 3670016 | tf_op jit(solution)/shard_map/owner/pallas_call | solution.py:666
  37.0 3.6 %all-to-all-start.1 = ((bf16[16,16,1152]{2,1,0:T(8,128)(2,1)}), bf16[16,16,1152]{2,1,0:T(8,128)(2,1)S(1)}, u32[]{:S(2)}, u32[]{:S(2)}) async-start(bf16[16,16,1152]{2,1,0:T(8,128)(2,1)} %bitcast.12), calls=%async_computation.1 | async-start | bytes 1179648 | tf_op jit(solution)/shard_map/all_to_all | solution.py:74
  40.6 2.8 %collective-permute-start.1 = (f32[24,64]{1,0:T(8,128)S(1)}, f32[24,64]{1,0:T(8,128)S(1)}, u32[]{:S(2)}, u32[]{:S(2)}) collective-permute-start(f32[24,64]{1,0:T(8,128)S(1)} %get-tuple-element.38.table_ref), channel_id=1, source_target_pairs={{0,16},{2,18},{4,20},{6,22},{8,24},{10,26},{12,28},{14,30},{16,0},... | collective-permute-start | bytes 18440 | tf_op jit(solution)/shard_map/ppermute | solution.py:80
  43.3 6.1 %leaf.1 = (f32[64,1024]{1,0:T(8,128)S(1)}, f32[64,128]{1,0:T(8,128)S(1)}) custom-call(bf16[64,2048]{1,0:T(8,128)(2,1)S(1)} %get-tuple-element.40.normed_ref, bf16[64,1024]{1,0:T(8,128)(2,1)S(1)} %get-tuple-element.41.query_ref, bf16[2048,1024]{1,0:T(8,128)(2,1)} %key_ref.1, bf16[2048,1024]{1,0:T(8,128)(2,1)} %value_ref.1, ...), custom_call_target="tpu_custom_call" | custom-call | flops 536870912 | bytes 8388608 | tf_op jit(solution)/shard_map/leaf/pallas_call | solution.py:627
  49.4 6.7 %collective-permute-done.1.far_table_ref = f32[24,64]{1,0:T(8,128)S(1)} collective-permute-done((f32[24,64]{1,0:T(8,128)S(1)}, f32[24,64]{1,0:T(8,128)S(1)}, u32[]{:S(2)}, u32[]{:S(2)}) %collective-permute-start.1) | collective-permute-done | bytes 6176 | tf_op jit(solution)/shard_map/ppermute | solution.py:80
  56.1 0.9 routing.1
  57.0 2.7 %merge.1.refs_3_ = bf16[64,2048]{1,0:T(8,128)(2,1)S(1)} custom-call(bf16[256,1152]{1,0:T(8,128)(2,1)S(1)} %bitcast.30, bf16[3,64,256]{2,1,0:T(8,128)(2,1)S(1)} %get-tuple-element.39.pick_ref, f32[64,1024]{1,0:T(8,128)S(1)} %get-tuple-element.42.leaf_ref, f32[64,128]{1,0:T(8,128)S(1)} %get-tuple-element.43.lse_ref, bf16[1024,2048]{1,0:T(8,128)(2,1)} %weight_ref.1), custom_call_target="tpu_custom_call" | custom-call | flops 268435456 | bytes 4194304 | tf_op jit(solution)/shard_map/merge/pallas_call | solution.py:685
  59.8 1.5 %collective-permute-done.2.refs_4_ = bf16[64,2048]{1,0:T(8,128)(2,1)S(1)} collective-permute-done((bf16[64,2048]{1,0:T(8,128)(2,1)S(1)}, bf16[64,2048]{1,0:T(8,128)(2,1)S(1)}, u32[]{:S(2)}, u32[]{:S(2)}) %collective-permute-start.2) | collective-permute-done | bytes 262176 | tf_op jit(solution)/shard_map/ppermute | solution.py:55
  61.4 0.2 middle.1
  61.6 0.5 collective-permute-start.3
  62.1 3.5 %load.1 = (bf16[2,704,2048]{2,1,0:T(8,128)(2,1)S(1)}, bf16[704,2048]{1,0:T(8,128)(2,1)S(1)}) custom-call(bf16[64,2048]{1,0:T(8,128)(2,1)S(1)} %get-tuple-element.44.refs_1_.after_ref, bf16[4,2,704,2048]{3,2,1,0:T(8,128)(2,1)} %bitcast.37, bf16[4,704,2048]{2,1,0:T(8,128)(2,1)} %refs_6_.1), custom_call_target="tpu_custom_call" | custom-call | flops 1 | bytes 1 | tf_op jit(solution)/shard_map/load/pallas_call | solution.py:737
  65.6 4.9 %shared.1 = (bf16[64,1024]{1,0:T(8,128)(2,1)S(1)}, bf16[64,1024]{1,0:T(8,128)(2,1)S(1)}) custom-call(s32[1]{0:T(128)} %bitcast.refs_0_, bf16[64,2048]{1,0:T(8,128)(2,1)S(1)} %get-tuple-element.44.refs_1_.after_ref, bf16[2,704,2048]{2,1,0:T(8,128)(2,1)} %bitcast.39, bf16[704,2048]{1,0:T(8,128)(2,1)} %refs_3_.1), custom_call_target="tpu_custom_call" | custom-call | flops 1 | bytes 1 | tf_op jit(solution)/shard_map/shared/pallas_call | solution.py:719
  70.5 0.4 collective-permute-done.3.far_ref
  70.9 0.4 dispatch.1
  71.3 19.2 %all_to_all.26 = bf16[8,64,1024]{2,1,0:T(8,128)(2,1)S(1)} all-to-all(bf16[8,64,1024]{2,1,0:T(8,128)(2,1)S(1)} %bitcast.28), channel_id=1, replica_groups={{0,2,4,6,8,10,12,14},{16,18,20,22,24,26,28,30},{1,3,5,7,9,11,13,15},{17..., dimensions={0} | all-to-all | bytes 2097152 | tf_op jit(solution)/shard_map/all_to_all | solution.py:74
  90.5 2.7 %collective-permute-done.4.refs_2_ = bf16[16,32,1024]{2,1,0:T(8,128)(2,1)S(1)} collective-permute-done((bf16[16,32,1024]{2,1,0:T(8,128)(2,1)S(1)}, bf16[16,32,1024]{2,1,0:T(8,128)(2,1)S(1)}, u32[]{:S(2)}, u32[]{:S(2)}) %collective-permute-start.4) | collective-permute-done | bytes 1048608 | tf_op jit(solution)/shard_map/ppermute | solution.py:55
  93.2 12.7 %experts.1 = (bf16[16,32,1024]{2,1,0:T(8,128)(2,1)S(1)}, bf16[16,32,1024]{2,1,0:T(8,128)(2,1)S(1)}) custom-call(s32[1]{0:T(128)} %bitcast.refs_0_, bf16[16,32,1024]{2,1,0:T(8,128)(2,1)S(1)} %bitcast.27, bf16[16,32,1024]{2,1,0:T(8,128)(2,1)S(1)} %collective-permute-done.4.refs_2_, bf16[2,704,2048]{2,1,0:T(8,128)(2,1)S(1)} %get-tuple-element.49.refs_3_, ...), custom_call_target="tpu_custom_call" | custom-call | flops 4429185024 | bytes 34603008 | tf_op jit(solution)/shard_map/experts/pallas_call | solution.py:764
  105.8 0.2 collective-permute-start.5
  106.0 2.5 %collective-permute-done.5.refs_1_ = bf16[16,32,1024]{2,1,0:T(8,128)(2,1)S(1)} collective-permute-done((bf16[16,32,1024]{2,1,0:T(8,128)(2,1)S(1)}, bf16[16,32,1024]{2,1,0:T(8,128)(2,1)S(1)}, u32[]{:S(2)}, u32[]{:S(2)}) %collective-permute-start.5) | collective-permute-done | bytes 1048608 | tf_op jit(solution)/shard_map/ppermute | solution.py:65
  108.6 1.2 add.2
  109.8 3.6 %all-to-all-start.3 = ((bf16[8,64,1024]{2,1,0:T(8,128)(2,1)}), bf16[8,64,1024]{2,1,0:T(8,128)(2,1)S(1)}, u32[]{:S(2)}, u32[]{:S(2)}) async-start(bf16[8,64,1024]{2,1,0:T(8,128)(2,1)} %bitcast.19), calls=%async_computation.3 | async-start | bytes 2097152 | tf_op jit(solution)/shard_map/all_to_all | solution.py:74
  113.6 1.2 collective-permute-done.6.refs_6_
  114.8 13.7 %all-to-all-done.3 = bf16[8,64,1024]{2,1,0:T(8,128)(2,1)S(1)} async-done(((bf16[8,64,1024]{2,1,0:T(8,128)(2,1)}), bf16[8,64,1024]{2,1,0:T(8,128)(2,1)S(1)}, u32[]{:S(2)}, u32[]{:S(2)}) %all-to-all-start.3) | async-done | bytes 1048608 | tf_op jit(solution)/shard_map/all_to_all | solution.py:74
  128.5 0.6 combine.1
  129.1 19.5 %all_to_all.27 = bf16[16,16,1024]{2,1,0:T(8,128)(2,1)S(1)} all-to-all(bf16[16,16,1024]{2,1,0:T(8,128)(2,1)S(1)} %bitcast.31), channel_id=1, replica_groups=mesh['dp'=16,'tensor'=2] {'dp'}, dimensions={0} | all-to-all | bytes 1048576 | tf_op jit(solution)/shard_map/all_to_all | solution.py:74
  148.6 0.4 settle.1
  149.0 1.2 collective-permute-done.7
  150.3 0.7 reshape.59
  (14 shorter events, 0.4 us)
Async XLA Ops:
  0.0 1.9 %collective-permute-start = (bf16[32,2048]{1,0:T(8,128)(2,1)}, bf16[32,2048]{1,0:T(8,128)(2,1)S(1)}, u32[]{:S(2)}, u32[]{:S(2)}) collective-permute-start(bf16[32,2048]{1,0:T(8,128)(2,1)} %bitcast.40), channel_id=1, source_target_pairs={{1,0},{0,1},{3,2},{2,3},{5,4},{4,5},{7,6},{6,7},{9,8},{8,9},{11,10... | collective-permute-start | bytes 393224 | tf_op jit(solution)/shard_map/ppermute | solution.py:55
  0.5 31.4 %copy-start = (bf16[2,896,1024]{2,1,0:T(8,128)(2,1)S(1)}, bf16[2,896,1024]{2,1,0:T(8,128)(2,1)}, u32[]{:S(2)}) copy-start(bf16[2,896,1024]{2,1,0:T(8,128)(2,1)} %kv_ref.1) | copy-start | bytes 11010052
  37.0 20.0 %all-to-all-start.1 = ((bf16[16,16,1152]{2,1,0:T(8,128)(2,1)}), bf16[16,16,1152]{2,1,0:T(8,128)(2,1)S(1)}, u32[]{:S(2)}, u32[]{:S(2)}) async-start(bf16[16,16,1152]{2,1,0:T(8,128)(2,1)} %bitcast.12), calls=%async_computation.1 | async-start | bytes 1179648 | tf_op jit(solution)/shard_map/all_to_all | solution.py:74
  40.6 15.5 %collective-permute-start.1 = (f32[24,64]{1,0:T(8,128)S(1)}, f32[24,64]{1,0:T(8,128)S(1)}, u32[]{:S(2)}, u32[]{:S(2)}) collective-permute-start(f32[24,64]{1,0:T(8,128)S(1)} %get-tuple-element.38.table_ref), channel_id=1, source_target_pairs={{0,16},{2,18},{4,20},{6,22},{8,24},{10,26},{12,28},{14,30},{16,0},... | collective-permute-start | bytes 18440 | tf_op jit(solution)/shard_map/ppermute | solution.py:80
  43.3 12.8 %copy-start.2 = (s32[8,3]{0,1:T(4,128)S(1)}, s32[8,3]{0,1:T(4,128)}, u32[]{:S(2)}) copy-start(s32[8,3]{0,1:T(4,128)} %param.25) | copy-start | bytes 292
  56.1 5.3 %copy-start.1 = (f32[2048]{0:T(1024)S(1)}, f32[2048]{0:T(1024)}, u32[]{:S(2)}) copy-start(f32[2048]{0:T(1024)} %param.28) | copy-start | bytes 24580
  59.8 1.6 %collective-permute-start.2 = (bf16[64,2048]{1,0:T(8,128)(2,1)S(1)}, bf16[64,2048]{1,0:T(8,128)(2,1)S(1)}, u32[]{:S(2)}, u32[]{:S(2)}) collective-permute-start(bf16[64,2048]{1,0:T(8,128)(2,1)S(1)} %merge.1.refs_3_), channel_id=1, source_target_pairs={{1,0},{0,1},{3,2},{2,3},{5,4},{4,5},{7,6},{6,7},{9,8},{8,9},{11,10... | collective-permute-start | bytes 786440 | tf_op jit(solution)/shard_map/ppermute | solution.py:55
  61.6 9.3 %collective-permute-start.3 = (bf16[64,1024]{1,0:T(8,128)(2,1)S(1)}, bf16[64,1024]{1,0:T(8,128)(2,1)S(1)}, u32[]{:S(2)}, u32[]{:S(2)}) collective-permute-start(bf16[64,1024]{1,0:T(8,128)(2,1)S(1)} %get-tuple-element.48.own_ref), channel_id=1, source_target_pairs={{0,16},{2,18},{4,20},{6,22},{8,24},{10,26},{12,28},{14,30},{16,0},... | collective-permute-start | bytes 393224 | tf_op jit(solution)/shard_map/ppermute | solution.py:80
  90.5 2.7 %collective-permute-start.4 = (bf16[16,32,1024]{2,1,0:T(8,128)(2,1)S(1)}, bf16[16,32,1024]{2,1,0:T(8,128)(2,1)S(1)}, u32[]{:S(2)}, u32[]{:S(2)}) collective-permute-start(bf16[16,32,1024]{2,1,0:T(8,128)(2,1)S(1)} %bitcast.26), channel_id=1, source_target_pairs={{1,0},{0,1},{3,2},{2,3},{5,4},{4,5},{7,6},{6,7},{9,8},{8,9},{11,10... | collective-permute-start | bytes 3145736 | tf_op jit(solution)/shard_map/ppermute | solution.py:55
  105.8 2.7 %collective-permute-start.5 = (bf16[16,32,1024]{2,1,0:T(8,128)(2,1)S(1)}, bf16[16,32,1024]{2,1,0:T(8,128)(2,1)S(1)}, u32[]{:S(2)}, u32[]{:S(2)}) collective-permute-start(bf16[16,32,1024]{2,1,0:T(8,128)(2,1)S(1)} %get-tuple-element.51), channel_id=1, source_target_pairs={{0,1},{1,0},{2,3},{3,2},{4,5},{5,4},{6,7},{7,6},{8,9},{9,8},{10,11... | collective-permute-start | bytes 3145736 | tf_op jit(solution)/shard_map/ppermute | solution.py:65
  109.8 18.7 %all-to-all-start.3 = ((bf16[8,64,1024]{2,1,0:T(8,128)(2,1)}), bf16[8,64,1024]{2,1,0:T(8,128)(2,1)S(1)}, u32[]{:S(2)}, u32[]{:S(2)}) async-start(bf16[8,64,1024]{2,1,0:T(8,128)(2,1)} %bitcast.19), calls=%async_computation.3 | async-start | bytes 2097152 | tf_op jit(solution)/shard_map/all_to_all | solution.py:74
  113.4 1.4 collective-permute-start.6
  149.0 1.3 collective-permute-start.7

commit v2 on v1

--- a/solution.py
+++ b/solution.py
@@ -139,7 +139,7 @@
 
 def prelude_kernel(
     owner_ref, start_ref, length_ref, request_ref, ids_ref, gates_ref,
-    place_ref, meta_ref, cos_ref, sin_ref, table_ref,
+    place_ref, meta_ref, cos_ref, sin_ref, table_ref, pick_ref,
     *, leaf_len,
 ):
     requests = owner_ref.shape[1]
@@ -147,8 +147,13 @@
     start, length = start_ref[...].astype(f32), length_ref[...].astype(f32)
     row_slot, row_token = divided(iota((slot_rows, 1), 0), leaf_len)
     request_of_row, token_of_row = divided(iota((1, rows), 1), leaf_len)
+    row_request, row_place = divided(iota((rows, 1), 0), leaf_len)
+    mine = iota((1, requests), 1) == row_request
+    slot_across, token_across = divided(iota((1, slot_rows), 1), leaf_len)
     named, first_key, key_count = 0.0, 0.0, 0.0
     for level, slot in enumerate(owner_slots(owner_ref[...].astype(f32))):
+        slot_down = jnp.sum(jnp.where(mine, slot, 0.0), axis=1, keepdims=True)
+        pick_ref[level] = one_hot((slot_down == slot_across) & (row_place == token_across))
         here = jnp.where(slot == row_slot, 1.0, 0.0)
         named = named + here
         first_key = first_key + here * start[level : level + 1]
@@ -168,8 +173,6 @@
     meta_ref[...] = meta.astype(bf16)
 
     offsets = length[0:1] + length[1:2] + length[2:3]
-    row_request, row_place = divided(iota((rows, 1), 0), leaf_len)
-    mine = iota((1, requests), 1) == row_request
     position = jnp.sum(jnp.where(mine, offsets, 0.0), axis=1, keepdims=True) + row_place
     half = HEAD_DIM // 2
     pair = jnp.where(lane < half, lane, lane - half)
@@ -189,20 +192,14 @@
 
 
 def routing_kernel(
-    half_ref, after_ref, owner_ref, table_ref, far_table_ref,
-    pick_ref, send_ref, high_ref, low_ref, final_ref,
-    *, leaf_len, groups, capacity, experts, choices,
+    half_ref, after_ref, table_ref, far_table_ref,
+    send_ref, high_ref, low_ref, final_ref,
+    *, tensors, leaf_len, groups, capacity, experts, choices,
 ):
-    requests = owner_ref.shape[1]
-    rows = requests * leaf_len
-    slot_rows = groups * 2 * leaf_len
-    row_request, row_place = divided(iota((rows, 1), 0), leaf_len)
+    rows = table_ref.shape[1]
+    final_rows = final_ref.shape[0]
+    share = leaf_len // tensors
     _, token_of_row = divided(iota((1, rows), 1), leaf_len)
-    slot_across, token_across = divided(iota((1, slot_rows), 1), leaf_len)
-    mine = iota((1, requests), 1) == row_request
-    for level, slot in enumerate(owner_slots(owner_ref[...].astype(f32))):
-        slot_down = jnp.sum(jnp.where(mine, slot, 0.0), axis=1, keepdims=True)
-        pick_ref[level] = one_hot((slot_down == slot_across) & (row_place == token_across))
 
     slots = send_ref.shape[0]
     local = experts // groups
@@ -213,8 +210,10 @@
     spread = one_hot(first_expert + device * local + local_expert == iota((1, experts), 1))
     expert_down = iota((experts, 1), 0)
     ahead = one_hot(iota((rows, rows), 0) < iota((rows, rows), 1))
-    final_group, final_token = divided(iota((slot_rows, 1), 0), leaf_len)
-    final_group, final_source = divided(final_group, 2)
+    block, final_place = divided(iota((final_rows, 1), 0), share)
+    block, final_source = divided(block, 2)
+    final_group, final_half = divided(block, tensors)
+    final_token = final_half * share + final_place
     send, high, low, final = [], [], [], []
     for source, table in enumerate((table_ref[...], far_table_ref[...])):
         member, gate_high, gate_low = 0.0, 0.0, 0.0
@@ -358,7 +357,7 @@
 
 
 def merge_kernel(
-    back_ref, pick_ref, leaf_ref, lse_ref, weight_ref, out_ref, buffer_ref, attended_ref, semaphores,
+    after_ref, back_ref, pick_ref, leaf_ref, lse_ref, weight_ref, out_ref, buffer_ref, attended_ref, semaphores,
     *, heads, step,
 ):
     copies = column_copies(weight_ref, buffer_ref, semaphores, step)
@@ -385,9 +384,9 @@
 
 
 def middle_kernel(*refs, tensors):
-    index_ref, raw_ref, gain_ref = refs[:3]
-    pieces = refs[3 : 3 + tensors]
-    normed_ref, own_ref, resid_own_ref, resid_ref = refs[3 + tensors :]
+    index_ref, _, raw_ref, gain_ref = refs[:4]
+    pieces = refs[4 : 4 + tensors]
+    normed_ref, own_ref, resid_own_ref, resid_ref = refs[4 + tensors :]
     width = own_ref.shape[1]
     own = pl.ds(pl.multiple_of(index_ref[0] * width, width), width)
     total = raw_ref[...].astype(f32)
@@ -490,7 +489,7 @@
         piece[...] = total_ref[at].astype(bf16)
 
 
-def add_kernel(*refs):
+def add_kernel(after_ref, *refs):
     out_ref = refs[-1]
     out_ref[...] = sum(piece[...].astype(f32) for piece in refs[:-1]).astype(bf16)
 
@@ -508,23 +507,25 @@
     out_ref[...] = dot(final_ref[...], both).astype(bf16)
 
 
-def settle_kernel(*refs, tensors, leaf_len, groups):
-    index_ref, meta_ref, rows_ref = refs[:3]
-    pieces = refs[3:]
-    slot_rows = meta_ref.shape[0]
-    places = pieces[0].shape[0]
-    share = leaf_len // tensors
+def settle_kernel(meta_ref, rows_ref, out_ref, *, tensors, leaf_len, groups):
+    slot_rows, final_rows = meta_ref.shape[0], rows_ref.shape[0]
+    requests, share, _ = out_ref.shape
+    width = rows_ref.shape[1]
     tag_down = meta_ref[...].astype(f32)[:, 4:5]
-    block, token = divided(iota((1, slot_rows), 1), leaf_len)
-    group, source = divided(block, 2)
+    block, place = divided(iota((1, final_rows), 1), share)
+    block, source = divided(block, 2)
+    group, half = divided(block, tensors)
     _, home = divided(group + source * (groups // 2), groups)
-    tagged = iota((slot_rows, 1), 0) == home * (2.0 * leaf_len) + token
+    tagged = iota((slot_rows, 1), 0) == home * (2.0 * leaf_len)
     tag = jnp.sum(jnp.where(tagged, tag_down, 0.0), axis=0, keepdims=True)
-    request, position = divided(iota((places, 1), 0), share)
-    for at, piece in enumerate(pieces):
-        shift = (lax.rem(index_ref[0] + at, tensors) * share).astype(f32)
-        chosen = one_hot((tag == request + 1.0) & (token == position + shift))
-        piece[...] = dot(chosen, rows_ref[...]).astype(bf16)
+    request, position = divided(iota((requests * share, 1), 0), share)
+    wanted = (tag == request + 1.0) & (place == position)
+    for at in range(tensors):
+        value = dot(one_hot(wanted & (half == at)), rows_ref[...])
+        for r in range(requests):
+            out_ref[r, :, at * width : (at + 1) * width] = value[
+                r * share : (r + 1) * share
+            ].astype(bf16)
 
 
 def on_device(
@@ -570,7 +571,7 @@
 
     owner_rows, request_row = prefix_owner.T, request_of.reshape(1, requests)
     table_rows = -(-(3 * top_count + 1) // 8) * 8
-    place, meta, cosine, sine, table = pl.pallas_call(
+    place, meta, cosine, sine, table, pick = pl.pallas_call(
         functools.partial(prelude_kernel, leaf_len=leaf_len),
         out_shape=[
             shape((slot_rows, rows), bf16),
@@ -578,9 +579,10 @@
             shape((rows, LANES), f32),
             shape((rows, LANES), f32),
             shape((table_rows, rows), f32),
+            shape((3, rows, slot_rows), bf16),
         ],
         in_specs=[whole()] * 6,
-        out_specs=[whole()] * 5,
+        out_specs=[whole()] * 6,
         compiler_params=params(24),
         name="prelude",
     )(
@@ -642,26 +644,6 @@
         name="leaf",
     )(normed, query, in_hbm(w_key), in_hbm(w_value), cosine, sine)
 
-    half = (lax.axis_index("dp") // (groups // 2)).astype(jnp.int32).reshape(1)
-    pick, send, gate_high, gate_low, final = pl.pallas_call(
-        functools.partial(
-            routing_kernel, leaf_len=leaf_len, groups=groups, capacity=capacity, experts=experts,
-            choices=top_count,
-        ),
-        out_shape=[
-            shape((3, rows, slot_rows), bf16),
-            shape((slots, 2 * rows), bf16),
-            shape((2 * rows, slots), bf16),
-            shape((2 * rows, slots), bf16),
-            shape((slot_rows, 2 * rows), bf16),
-        ],
-        in_specs=[scalar(), pl.BlockSpec(memory_space=pl.ANY)] + [whole()] * 3,
-        out_specs=[whole()] * 5,
-        compiler_params=params(24),
-        cost_estimate=cost(1 << 30, 1 << 20),
-        name="routing",
-    )(half, query_arrived, owner_rows, table, far_table)
-
     pool = prefix_kv.shape[1]
     back_send = pl.pallas_call(
         functools.partial(
@@ -685,7 +667,9 @@
     partial_out = pl.pallas_call(
         functools.partial(merge_kernel, heads=local_heads, step=out_step),
         out_shape=shape((rows, model_width), bf16),
-        in_specs=[whole()] * 4 + [pl.BlockSpec(memory_space=pltpu.HBM)],
+        in_specs=[pl.BlockSpec(memory_space=pl.ANY)]
+        + [whole()] * 4
+        + [pl.BlockSpec(memory_space=pltpu.HBM)],
         out_specs=whole(),
         scratch_shapes=[
             pltpu.VMEM((local_width, model_width), bf16),
@@ -695,9 +679,28 @@
         compiler_params=params(24),
         cost_estimate=cost(2 * rows * local_width * model_width, 2 * local_width * model_width),
         name="merge",
-    )(back, pick, leaf_out, leaf_lse, in_hbm(w_out))
+    )(far_table, back, pick, leaf_out, leaf_lse, in_hbm(w_out))
 
     out_pieces = ring_get(partial_out, tensors)
+
+    half = (lax.axis_index("dp") // (groups // 2)).astype(jnp.int32).reshape(1)
+    send, gate_high, gate_low, final = pl.pallas_call(
+        functools.partial(
+            routing_kernel, tensors=tensors, leaf_len=leaf_len, groups=groups,
+            capacity=capacity, experts=experts, choices=top_count,
+        ),
+        out_shape=[
+            shape((slots, 2 * rows), bf16),
+            shape((2 * rows, slots), bf16),
+            shape((2 * rows, slots), bf16),
+            shape((slot_rows, 2 * rows), bf16),
+        ],
+        in_specs=[scalar(), pl.BlockSpec(memory_space=pl.ANY)] + [whole()] * 2,
+        out_specs=[whole()] * 4,
+        compiler_params=params(16),
+        cost_estimate=cost(1, 1),
+        name="routing",
+    )(half, partial_out, table, far_table)
 
     normed_mlp, own_columns, resid_own = pl.pallas_call(
         functools.partial(middle_kernel, tensors=tensors),
@@ -706,12 +709,12 @@
             shape((rows, column_share), bf16),
             shape((rows, column_share), f32),
         ],
-        in_specs=[scalar()] + [whole()] * (2 + tensors),
+        in_specs=[scalar(), pl.BlockSpec(memory_space=pl.ANY)] + [whole()] * (2 + tensors),
         out_specs=[whole()] * 3,
         scratch_shapes=[pltpu.VMEM((rows, model_width), f32)],
         compiler_params=params(24),
         name="middle",
-    )(index, raw, mlp_gain.reshape(1, -1), *out_pieces)
+    )(index, send, raw, mlp_gain.reshape(1, -1), *out_pieces)
 
     far_columns = from_partner(own_columns, groups)
     hbm = pl.BlockSpec(memory_space=pltpu.HBM)
@@ -789,17 +792,18 @@
         expert_in,
         expert_out,
     )
+    partial_pieces, shared_pieces = lax.optimization_barrier((partial_pieces, shared_pieces))
+    shared_pieces = ring_send(shared_pieces)
     partial_pieces = ring_send(partial_pieces)
     summed = pl.pallas_call(
         add_kernel,
         out_shape=shape((groups, block, column_share), bf16),
-        in_specs=[whole()] * tensors,
+        in_specs=[pl.BlockSpec(memory_space=pl.ANY)] + [whole()] * tensors,
         out_specs=whole(),
         compiler_params=params(12),
         name="add",
-    )(*partial_pieces)
-
-    shared_pieces = ring_send(shared_pieces)
+    )(shared_pieces[-1], *partial_pieces)
+
     returned = exchange(summed.reshape(slots, column_share), groups, halves=True)
 
     final_send = pl.pallas_call(
@@ -811,37 +815,24 @@
         name="combine",
     )(returned, gate_high, gate_low, resid_own, final, *shared_pieces)
 
-    final_arrived = exchange(final_send, groups)
-
-    places = requests * (leaf_len // tensors)
-    settled = pl.pallas_call(
-        functools.partial(
-            settle_kernel, tensors=tensors, leaf_len=leaf_len, groups=groups
-        ),
+    devices = groups * tensors
+    blocks = final_send.reshape(devices, slot_rows // devices, column_share)
+    final_arrived = lax.all_to_all(
+        blocks, ("dp", "tensor"), split_axis=0, concat_axis=0, tiled=True
+    ).reshape(slot_rows, column_share)
+
+    return pl.pallas_call(
+        functools.partial(settle_kernel, tensors=tensors, leaf_len=leaf_len, groups=groups),
         grid=(1,),
-        out_shape=[shape((places, column_share), bf16)] * tensors,
+        out_shape=shape((requests, leaf_len // tensors, model_width), bf16),
         in_specs=[
-            scalar(),
             pl.BlockSpec((slot_rows, LANES), lambda i: (0, local_heads)),
             fixed(slot_rows, column_share),
         ],
-        out_specs=[fixed(places, column_share)] * tensors,
-        compiler_params=params(24, 1),
+        out_specs=fixed(requests, leaf_len // tensors, model_width),
+        compiler_params=params(16, 1),
         name="settle",
-    )(index, query_arrived, final_arrived)
-    settled = ring_send(settled)
-    if tensors == 2:
-        first = index[0] == 0
-        own, other = settled
-        result = jnp.concatenate(
-            [jnp.where(first, own, other), jnp.where(first, other, own)], axis=1
-        )
-    else:
-        result = jnp.zeros((places, model_width), bf16)
-        for at, piece in enumerate(settled):
-            column = ((index[0] - at + tensors) % tensors) * column_share
-            result = lax.dynamic_update_slice(result, piece, (0, column))
-    return result.reshape(requests, leaf_len // tensors, model_width)
+    )(query_arrived, final_arrived)
 
 
 def solution(mesh):

time: 151 us -> 146 us (0.967)
  waiting for transfers between devices: 29.9 us -> 12.6 us
  blocking collectives: 64.4 us -> 80.1 us
  starting transfers between devices: 11.4 us -> 8.55 us
    all_to_all x0 -> x1, blocking collectives: none -> 17.6 us  [on_device(): lax.all_to_all(blocks, ('dp', 'tensor'), split_axis=0, concat_axis=0, til...]
    all_to_all x2 -> x1, waiting for transfers between devices: 13.7 us -> 0.27 us  [exchange(): lax.all_to_all(blocks, 'dp', split_axis=0, concat_axis=0, tiled=True, axi...]
    all_to_all x2 -> x1, starting transfers between devices: 7.14 us -> 3.58 us  [exchange(): lax.all_to_all(blocks, 'dp', split_axis=0, concat_axis=0, tiled=True, axi...]
    ppermute x3 -> x2, waiting for transfers between devices: 4.97 us -> 2.34 us  [ring_send(): lax.ppermute(pieces[step], 'tensor', [(i, (i + step) % count) for i in ra...]
    all_to_all x3, blocking collectives: 64.4 us -> 62.5 us  [exchange(): lax.all_to_all(blocks, 'dp', split_axis=0, concat_axis=0, tiled=True, axi...]
  transfers between devices with their start and end apart: 10 -> 8, of which waited for: 8 -> 5; matrix products, arithmetic and copies ran while one was open for 0% -> 0% of each run, Pallas kernels for 11% -> 12%
where the time goes in v2:
time: 146 us; the launch traced here: 145 us
  blocking collectives  80.1 us (55%)
  Pallas kernels  44.1 us (30%)
  waiting for transfers between devices  12.6 us (9%)
  starting transfers between devices  8.55 us (6%)
    all_to_all x3, blocking collectives, exchange(): lax.all_to_all(blocks, 'dp', split_axis=0, concat_axis=0, tiled=True, axi...  62.5 us
    all_to_all x1, blocking collectives, on_device(): lax.all_to_all(blocks, ('dp', 'tensor'), split_axis=0, concat_axis=0, til...  17.6 us
    pallas_call x1, Pallas kernels, on_device(): pl.pallas_call(functools.partial(expert_kernel, tensors=tensors, experts=...  12.7 us
    ppermute x2, waiting for transfers between devices, from_partner(): lax.ppermute(array, 'dp', [(i, (i + groups // 2) % groups) for i in range...  6.75 us
    pallas_call x1, Pallas kernels, on_device(): pl.pallas_call(functools.partial(leaf_kernel, heads=step_heads, leaf_len=...  6.07 us
    pallas_call x1, Pallas kernels, on_device(): pl.pallas_call(functools.partial(owner_kernel, heads=local_heads, request...  5.15 us
    pallas_call x1, Pallas kernels, on_device(): pl.pallas_call(functools.partial(shared_kernel, tensors=tensors), out_sha...  4.85 us
    pallas_call x1, Pallas kernels, on_device(): pl.pallas_call(functools.partial(query_kernel, tensors=tensors, heads=que...  4.14 us
  transfers between devices with their start and end apart: 8, of which 5 were waited for; matrix products, arithmetic and copies ran while one was open for 0% of the time, Pallas kernels for 12%

profile of v2, /device:TPU:0, one launch (start us, length us, event | category | flops | bytes accessed | tf_op | source)
XLA Modules:
  0.0 145.5 jit_solution(12725067087621794431)
XLA Ops:
  0.0 0.5 collective-permute-start
  0.5 1.5 prelude.1
  1.9 4.1 %queries.1 = (bf16[64,2048]{1,0:T(8,128)(2,1)S(1)}, bf16[64,2048]{1,0:T(8,128)(2,1)S(1)}, bf16[64,1024]{1,0:T(8,128)(2,1)S(1)}, bf16[256,1152]{1,0:T(8,128)(2,1)S(1)}) custom-call(s32[1]{0:T(128)} %bitcast.refs_0_, bf16[32,2048]{1,0:T(8,128)(2,1)} %bitcast.39, bf16[32,2048]{1,0:T(8,128)(2,1)S(1)} %collective-permute-done.refs_2_, f32[1,2048]{1,0:T(1,128)} %bitcast.42, ...), custom_call_target="tpu_custom_call" | custom-call | flops 268435456 | bytes 4194304 | tf_op jit(solution)/shard_map/queries/pallas_call | solution.py:602
  6.1 25.8 %all_to_all.25 = bf16[16,16,1152]{2,1,0:T(8,128)(2,1)S(1)} all-to-all(bf16[16,16,1152]{2,1,0:T(8,128)(2,1)S(1)} %bitcast.33), channel_id=1, replica_groups=mesh['dp'=16,'tensor'=2] {'dp'}, dimensions={0} | all-to-all | bytes 1179648 | tf_op jit(solution)/shard_map/all_to_all | solution.py:74
  31.9 5.2 %owner.1 = bf16[256,1152]{1,0:T(8,128)(2,1)} custom-call(bf16[256,1152]{1,0:T(8,128)(2,1)S(1)} %bitcast.23, bf16[2,896,1024]{2,1,0:T(8,128)(2,1)S(1)} %copy-done), custom_call_target="tpu_custom_call" | custom-call | flops 939524096 | bytes 3670016 | tf_op jit(solution)/shard_map/owner/pallas_call | solution.py:648
  37.0 3.6 %all-to-all-start.1 = ((bf16[16,16,1152]{2,1,0:T(8,128)(2,1)}), bf16[16,16,1152]{2,1,0:T(8,128)(2,1)S(1)}, u32[]{:S(2)}, u32[]{:S(2)}) async-start(bf16[16,16,1152]{2,1,0:T(8,128)(2,1)} %bitcast.12), calls=%async_computation.1 | async-start | bytes 1179648 | tf_op jit(solution)/shard_map/all_to_all | solution.py:74
  40.6 2.8 %collective-permute-start.1 = (f32[24,64]{1,0:T(8,128)S(1)}, f32[24,64]{1,0:T(8,128)S(1)}, u32[]{:S(2)}, u32[]{:S(2)}) collective-permute-start(f32[24,64]{1,0:T(8,128)S(1)} %get-tuple-element.39.table_ref), channel_id=1, source_target_pairs={{0,16},{2,18},{4,20},{6,22},{8,24},{10,26},{12,28},{14,30},{16,0},... | collective-permute-start | bytes 18440 | tf_op jit(solution)/shard_map/ppermute | solution.py:80
  43.4 6.1 %leaf.1 = (f32[64,1024]{1,0:T(8,128)S(1)}, f32[64,128]{1,0:T(8,128)S(1)}) custom-call(bf16[64,2048]{1,0:T(8,128)(2,1)S(1)} %get-tuple-element.41.normed_ref, bf16[64,1024]{1,0:T(8,128)(2,1)S(1)} %get-tuple-element.42.query_ref, bf16[2048,1024]{1,0:T(8,128)(2,1)} %key_ref.1, bf16[2048,1024]{1,0:T(8,128)(2,1)} %value_ref.1, ...), custom_call_target="tpu_custom_call" | custom-call | flops 536870912 | bytes 8388608 | tf_op jit(solution)/shard_map/leaf/pallas_call | solution.py:629
  49.5 0.0 copy-start.1
  49.5 6.7 %collective-permute-done.1.after_ref.far_table_ref = f32[24,64]{1,0:T(8,128)S(1)} collective-permute-done((f32[24,64]{1,0:T(8,128)S(1)}, f32[24,64]{1,0:T(8,128)S(1)}, u32[]{:S(2)}, u32[]{:S(2)}) %collective-permute-start.1) | collective-permute-done | bytes 6176 | tf_op jit(solution)/shard_map/ppermute | solution.py:80
  56.2 0.3 all-to-all-done.1
  56.5 2.7 %merge.1.after_ref.refs_4_ = bf16[64,2048]{1,0:T(8,128)(2,1)S(1)} custom-call(f32[24,64]{1,0:T(8,128)S(1)} %collective-permute-done.1.after_ref.far_table_ref, bf16[256,1152]{1,0:T(8,128)(2,1)S(1)} %bitcast.30, bf16[3,64,256]{2,1,0:T(8,128)(2,1)S(1)} %get-tuple-element.40.pick_ref, f32[64,1024]{1,0:T(8,128)S(1)} %get-tuple-element.43.leaf_ref, ...), custom_call_target="tpu_custom_call" | custom-call | flops 268435456 | bytes 4194304 | tf_op jit(solution)/shard_map/merge/pallas_call | solution.py:667
  59.2 0.1 collective-permute-start.2
  59.3 1.0 routing.1
  60.3 0.5 collective-permute-done.2.refs_5_
  60.8 0.2 middle.1
  61.1 1.1 collective-permute-start.3
  62.2 4.9 %shared.1 = (bf16[64,1024]{1,0:T(8,128)(2,1)S(1)}, bf16[64,1024]{1,0:T(8,128)(2,1)S(1)}) custom-call(s32[1]{0:T(128)} %bitcast.refs_0_, bf16[64,2048]{1,0:T(8,128)(2,1)S(1)} %get-tuple-element.47.refs_1_.after_ref, bf16[2,704,2048]{2,1,0:T(8,128)(2,1)} %bitcast.37, bf16[704,2048]{1,0:T(8,128)(2,1)} %refs_3_.1), custom_call_target="tpu_custom_call" | custom-call | flops 1 | bytes 1 | tf_op jit(solution)/shard_map/shared/pallas_call | solution.py:722
  67.0 3.5 %load.1 = (bf16[2,704,2048]{2,1,0:T(8,128)(2,1)S(1)}, bf16[704,2048]{1,0:T(8,128)(2,1)S(1)}) custom-call(bf16[64,2048]{1,0:T(8,128)(2,1)S(1)} %get-tuple-element.47.refs_1_.after_ref, bf16[4,2,704,2048]{3,2,1,0:T(8,128)(2,1)} %bitcast.35, bf16[4,704,2048]{2,1,0:T(8,128)(2,1)} %refs_6_.1), custom_call_target="tpu_custom_call" | custom-call | flops 1 | bytes 1 | tf_op jit(solution)/shard_map/load/pallas_call | solution.py:740
  70.6 0.0 collective-permute-done.3.far_ref
  70.6 0.4 dispatch.1
  71.0 18.6 %all_to_all.26 = bf16[8,64,1024]{2,1,0:T(8,128)(2,1)S(1)} all-to-all(bf16[8,64,1024]{2,1,0:T(8,128)(2,1)S(1)} %bitcast.27), channel_id=1, replica_groups={{0,2,4,6,8,10,12,14},{16,18,20,22,24,26,28,30},{1,3,5,7,9,11,13,15},{17..., dimensions={0} | all-to-all | bytes 2097152 | tf_op jit(solution)/shard_map/all_to_all | solution.py:74
  89.7 2.7 %collective-permute-done.4.refs_2_ = bf16[16,32,1024]{2,1,0:T(8,128)(2,1)S(1)} collective-permute-done((bf16[16,32,1024]{2,1,0:T(8,128)(2,1)S(1)}, bf16[16,32,1024]{2,1,0:T(8,128)(2,1)S(1)}, u32[]{:S(2)}, u32[]{:S(2)}) %collective-permute-start.4) | collective-permute-done | bytes 1048608 | tf_op jit(solution)/shard_map/ppermute | solution.py:55
  92.3 12.7 %experts.1 = (bf16[16,32,1024]{2,1,0:T(8,128)(2,1)S(1)}, bf16[16,32,1024]{2,1,0:T(8,128)(2,1)S(1)}) custom-call(s32[1]{0:T(128)} %bitcast.refs_0_, bf16[16,32,1024]{2,1,0:T(8,128)(2,1)S(1)} %bitcast.26, bf16[16,32,1024]{2,1,0:T(8,128)(2,1)S(1)} %collective-permute-done.4.refs_2_, bf16[2,704,2048]{2,1,0:T(8,128)(2,1)S(1)} %get-tuple-element.51.refs_3_, ...), custom_call_target="tpu_custom_call" | custom-call | flops 4429185024 | bytes 34603008 | tf_op jit(solution)/shard_map/experts/pallas_call | solution.py:767
  105.0 0.2 collective-permute-start.6
  105.2 0.4 collective-permute-start.5
  105.6 2.3 %collective-permute-done.5.after_ref.refs_6_ = bf16[64,1024]{1,0:T(8,128)(2,1)S(1)} collective-permute-done((bf16[64,1024]{1,0:T(8,128)(2,1)S(1)}, bf16[64,1024]{1,0:T(8,128)(2,1)S(1)}, u32[]{:S(2)}, u32[]{:S(2)}) %collective-permute-start.5) | collective-permute-done | bytes 131104 | tf_op jit(solution)/shard_map/ppermute | solution.py:65
  107.9 0.2 add.2
  108.1 18.1 %all_to_all.27 = bf16[8,64,1024]{2,1,0:T(8,128)(2,1)S(1)} all-to-all(bf16[8,64,1024]{2,1,0:T(8,128)(2,1)S(1)} %bitcast.28), channel_id=1, replica_groups={{0,2,4,6,8,10,12,14},{16,18,20,22,24,26,28,30},{1,3,5,7,9,11,13,15},{17..., dimensions={0} | all-to-all | bytes 2097152 | tf_op jit(solution)/shard_map/all_to_all | solution.py:74
  126.2 0.7 combine.1
  126.9 17.6 %all_to_all.28 = bf16[32,8,1024]{2,1,0:T(8,128)(2,1)S(1)} all-to-all(bf16[32,8,1024]{2,1,0:T(8,128)(2,1)S(1)} %bitcast.31), channel_id=1, replica_groups=mesh['dp'=16,'tensor'=2] {'dp','tensor'}, dimensions={0} | all-to-all | bytes 1048576 | tf_op jit(solution)/shard_map/all_to_all | solution.py:820
  144.5 1.0 settle.1
  (6 shorter events, 0.0 us)
Async XLA Ops:
  0.0 1.9 %collective-permute-start = (bf16[32,2048]{1,0:T(8,128)(2,1)}, bf16[32,2048]{1,0:T(8,128)(2,1)S(1)}, u32[]{:S(2)}, u32[]{:S(2)}) collective-permute-start(bf16[32,2048]{1,0:T(8,128)(2,1)} %bitcast.38), channel_id=1, source_target_pairs={{1,0},{0,1},{3,2},{2,3},{5,4},{4,5},{7,6},{6,7},{9,8},{8,9},{11,10... | collective-permute-start | bytes 393224 | tf_op jit(solution)/shard_map/ppermute | solution.py:55
  0.5 31.4 %copy-start = (bf16[2,896,1024]{2,1,0:T(8,128)(2,1)S(1)}, bf16[2,896,1024]{2,1,0:T(8,128)(2,1)}, u32[]{:S(2)}) copy-start(bf16[2,896,1024]{2,1,0:T(8,128)(2,1)} %kv_ref.1) | copy-start | bytes 11010052
  37.0 19.5 %all-to-all-start.1 = ((bf16[16,16,1152]{2,1,0:T(8,128)(2,1)}), bf16[16,16,1152]{2,1,0:T(8,128)(2,1)S(1)}, u32[]{:S(2)}, u32[]{:S(2)}) async-start(bf16[16,16,1152]{2,1,0:T(8,128)(2,1)} %bitcast.12), calls=%async_computation.1 | async-start | bytes 1179648 | tf_op jit(solution)/shard_map/all_to_all | solution.py:74
  40.6 15.6 %collective-permute-start.1 = (f32[24,64]{1,0:T(8,128)S(1)}, f32[24,64]{1,0:T(8,128)S(1)}, u32[]{:S(2)}, u32[]{:S(2)}) collective-permute-start(f32[24,64]{1,0:T(8,128)S(1)} %get-tuple-element.39.table_ref), channel_id=1, source_target_pairs={{0,16},{2,18},{4,20},{6,22},{8,24},{10,26},{12,28},{14,30},{16,0},... | collective-permute-start | bytes 18440 | tf_op jit(solution)/shard_map/ppermute | solution.py:80
  49.5 11.4 %copy-start.1 = (f32[2048]{0:T(1024)S(1)}, f32[2048]{0:T(1024)}, u32[]{:S(2)}) copy-start(f32[2048]{0:T(1024)} %param.28) | copy-start | bytes 24580
  59.2 1.6 %collective-permute-start.2 = (bf16[64,2048]{1,0:T(8,128)(2,1)S(1)}, bf16[64,2048]{1,0:T(8,128)(2,1)S(1)}, u32[]{:S(2)}, u32[]{:S(2)}) collective-permute-start(bf16[64,2048]{1,0:T(8,128)(2,1)S(1)} %merge.1.after_ref.refs_4_), channel_id=1, source_target_pairs={{1,0},{0,1},{3,2},{2,3},{5,4},{4,5},{7,6},{6,7},{9,8},{8,9},{11,10... | collective-permute-start | bytes 786440 | tf_op jit(solution)/shard_map/ppermute | solution.py:55
  61.1 9.5 %collective-permute-start.3 = (bf16[64,1024]{1,0:T(8,128)(2,1)S(1)}, bf16[64,1024]{1,0:T(8,128)(2,1)S(1)}, u32[]{:S(2)}, u32[]{:S(2)}) collective-permute-start(bf16[64,1024]{1,0:T(8,128)(2,1)S(1)} %get-tuple-element.50.own_ref), channel_id=1, source_target_pairs={{0,16},{2,18},{4,20},{6,22},{8,24},{10,26},{12,28},{14,30},{16,0},... | collective-permute-start | bytes 393224 | tf_op jit(solution)/shard_map/ppermute | solution.py:80
  89.6 2.7 %collective-permute-start.4 = (bf16[16,32,1024]{2,1,0:T(8,128)(2,1)S(1)}, bf16[16,32,1024]{2,1,0:T(8,128)(2,1)S(1)}, u32[]{:S(2)}, u32[]{:S(2)}) collective-permute-start(bf16[16,32,1024]{2,1,0:T(8,128)(2,1)S(1)} %bitcast.25), channel_id=1, source_target_pairs={{1,0},{0,1},{3,2},{2,3},{5,4},{4,5},{7,6},{6,7},{9,8},{8,9},{11,10... | collective-permute-start | bytes 3145736 | tf_op jit(solution)/shard_map/ppermute | solution.py:55
  105.0 2.9 %collective-permute-start.6 = (bf16[16,32,1024]{2,1,0:T(8,128)(2,1)S(1)}, bf16[16,32,1024]{2,1,0:T(8,128)(2,1)S(1)}, u32[]{:S(2)}, u32[]{:S(2)}) collective-permute-start(bf16[16,32,1024]{2,1,0:T(8,128)(2,1)S(1)} %get-tuple-element.57), channel_id=1, source_target_pairs={{0,1},{1,0},{2,3},{3,2},{4,5},{5,4},{6,7},{7,6},{8,9},{9,8},{10,11... | collective-permute-start | bytes 3145736 | tf_op jit(solution)/shard_map/ppermute | solution.py:65
  105.2 2.7 %collective-permute-start.5 = (bf16[64,1024]{1,0:T(8,128)(2,1)S(1)}, bf16[64,1024]{1,0:T(8,128)(2,1)S(1)}, u32[]{:S(2)}, u32[]{:S(2)}) collective-permute-start(bf16[64,1024]{1,0:T(8,128)(2,1)S(1)} %get-tuple-element.55), channel_id=1, source_target_pairs={{0,1},{1,0},{2,3},{3,2},{4,5},{5,4},{6,7},{7,6},{8,9},{9,8},{10,11... | collective-permute-start | bytes 393224 | tf_op jit(solution)/shard_map/ppermute | solution.py:65

commit v3 on v2

--- a/solution.py
+++ b/solution.py
@@ -404,13 +404,16 @@
 
 
 def shared_kernel(*refs, tensors):
-    index_ref, rows_ref, in_hbm_ref, down_hbm_ref = refs[:4]
-    pieces, refs = refs[4 : 4 + tensors], refs[4 + tensors :]
-    in_ref, down_ref, total_ref, semaphores = refs
+    index_ref, rows_ref, in_hbm_ref, down_hbm_ref, expert_in_ref, expert_down_ref = refs[:6]
+    pieces, refs = refs[6 : 6 + tensors], refs[6 + tensors :]
+    early_in_ref, early_down_ref, in_ref, down_ref, total_ref, semaphores = refs
+    early = early_in_ref.shape[0]
     copies = [
         pltpu.make_async_copy(in_hbm_ref.at[0], in_ref.at[0], semaphores.at[0]),
         pltpu.make_async_copy(in_hbm_ref.at[1], in_ref.at[1], semaphores.at[1]),
         pltpu.make_async_copy(down_hbm_ref, down_ref, semaphores.at[2]),
+        pltpu.make_async_copy(expert_in_ref.at[0:early], early_in_ref, semaphores.at[3]),
+        pltpu.make_async_copy(expert_down_ref.at[0], early_down_ref, semaphores.at[4]),
     ]
     for copy in copies:
         copy.start()
@@ -426,17 +429,8 @@
     for at, piece in enumerate(pieces):
         column = lax.rem(index_ref[0] + at, tensors) * width
         piece[...] = total_ref[:, pl.ds(pl.multiple_of(column, width), width)].astype(bf16)
-
-
-def load_kernel(after_ref, in_ref, down_ref, in_out_ref, down_out_ref, semaphores):
-    copies = [
-        pltpu.make_async_copy(in_ref.at[0], in_out_ref, semaphores.at[0]),
-        pltpu.make_async_copy(down_ref.at[0], down_out_ref, semaphores.at[1]),
-    ]
-    for copy in copies:
-        copy.start()
-    for copy in copies:
-        copy.wait()
+    copies[3].wait()
+    copies[4].wait()
 
 
 def rows_of_experts(piece, experts, capacity):
@@ -449,19 +443,21 @@
 
 def expert_kernel(*refs, tensors, experts, capacity):
     index_ref, arrived, refs = refs[0], refs[1 : 1 + tensors], refs[1 + tensors :]
-    (first_in_ref, first_down_ref, in_hbm_ref, down_hbm_ref), refs = refs[:4], refs[4:]
+    (early_in_ref, early_down_ref, in_hbm_ref, down_hbm_ref), refs = refs[:4], refs[4:]
     pieces, refs = refs[:tensors], refs[tensors:]
-    in_ref, down_ref, rows_ref, total_ref, semaphores = refs
-    copies = []
+    in_ref, down_ref, rows_ref, semaphores = refs
+    early = early_in_ref.shape[0]
+    in_copies, down_copies = {}, {}
     for e in range(1, experts):
-        copies.append(
-            (
-                pltpu.make_async_copy(in_hbm_ref.at[e], in_ref.at[e - 1], semaphores.at[0, e]),
-                pltpu.make_async_copy(down_hbm_ref.at[e], down_ref.at[e - 1], semaphores.at[1, e]),
+        down_copies[e] = pltpu.make_async_copy(
+            down_hbm_ref.at[e], down_ref.at[e - 1], semaphores.at[0, e]
+        )
+        if e >= early:
+            in_copies[e] = pltpu.make_async_copy(
+                in_hbm_ref.at[e], in_ref.at[e - early], semaphores.at[1, e]
             )
-        )
-        for copy in copies[-1]:
-            copy.start()
+            in_copies[e].start()
+        down_copies[e].start()
     groups, _, width = arrived[0].shape
     columns = [
         pl.ds(pl.multiple_of(lax.rem(index_ref[0] + at, tensors) * width, width), width)
@@ -470,23 +466,32 @@
     for at, piece in enumerate(arrived):
         for e, rows in enumerate(rows_of_experts(piece, experts, capacity)):
             rows_ref[e, :, columns[at]] = rows
+    together = max(1, 16 // capacity)
+    values = []
     for e in range(experts):
-        if e == 0:
-            gate_weight, up_weight, down = first_in_ref.at[0], first_in_ref.at[1], first_down_ref
+        if e < early:
+            weights = early_in_ref.at[e]
         else:
-            gate_weight, up_weight, down = in_ref.at[e - 1, 0], in_ref.at[e - 1, 1], down_ref.at[e - 1]
-            copies[e - 1][0].wait()
-        gate = dot_nt(rows_ref[e], gate_weight[...])
-        up = dot_nt(rows_ref[e], up_weight[...])
+            weights = in_ref.at[e - early]
+            in_copies[e].wait()
+        down = early_down_ref if e == 0 else down_ref.at[e - 1]
+        gate = dot_nt(rows_ref[e], weights[0])
+        up = dot_nt(rows_ref[e], weights[1])
         hidden = (gate / (1.0 + jnp.exp(-gate)) * up).astype(bf16)
         if e > 0:
-            copies[e - 1][1].wait()
-        mine = slice(e * capacity, (e + 1) * capacity)
-        for at in range(tensors):
-            value = dot(hidden, down[:, columns[at]])
-            total_ref[at, :, mine, :] = value.reshape(groups, capacity, width)
-    for at, piece in enumerate(pieces):
-        piece[...] = total_ref[at].astype(bf16)
+            down_copies[e].wait()
+        values.append(
+            [
+                dot(hidden, down[:, columns[at]]).reshape(groups, capacity, width)
+                for at in range(tensors)
+            ]
+        )
+        if len(values) == together or e == experts - 1:
+            mine = slice((e + 1 - len(values)) * capacity, (e + 1) * capacity)
+            for at, piece in enumerate(pieces):
+                parts = [value[at] for value in values]
+                piece[:, mine, :] = jnp.concatenate(parts, axis=1).astype(bf16)
+            values = []
 
 
 def add_kernel(after_ref, *refs):
@@ -583,7 +588,7 @@
         ],
         in_specs=[whole()] * 6,
         out_specs=[whole()] * 6,
-        compiler_params=params(24),
+        compiler_params=params(4),
         name="prelude",
     )(
         in_hbm(owner_rows), in_hbm(prefix_start.T), in_hbm(prefix_len.T), in_hbm(request_row),
@@ -616,7 +621,7 @@
             pltpu.VMEM((model_width, local_width), bf16),
             pltpu.SemaphoreType.DMA((local_heads // query_heads,)),
         ],
-        compiler_params=params(24),
+        compiler_params=params(10),
         cost_estimate=cost(2 * rows * model_width * local_width, 2 * model_width * local_width),
         name="queries",
     )(
@@ -639,7 +644,7 @@
             fixed(rows, LANES),
         ],
         out_specs=[columns(rows, step_width), fixed(rows, LANES)],
-        compiler_params=params(24, 1),
+        compiler_params=params(10, 1),
         cost_estimate=cost(4 * rows * model_width * local_width, 4 * model_width * local_width),
         name="leaf",
     )(normed, query, in_hbm(w_key), in_hbm(w_value), cosine, sine)
@@ -656,7 +661,7 @@
             pltpu.VMEM((3 * rows, local_width), bf16),
             pltpu.VMEM((3 * rows, send_width), bf16),
         ],
-        compiler_params=params(32),
+        compiler_params=params(16),
         cost_estimate=cost(4 * slot_rows * pool * local_width, 4 * pool * local_width),
         name="owner",
     )(query_arrived, prefix_kv)
@@ -676,7 +681,7 @@
             pltpu.VMEM((rows, local_width), bf16),
             pltpu.SemaphoreType.DMA((model_width // out_step,)),
         ],
-        compiler_params=params(24),
+        compiler_params=params(10),
         cost_estimate=cost(2 * rows * local_width * model_width, 2 * local_width * model_width),
         name="merge",
     )(far_table, back, pick, leaf_out, leaf_lse, in_hbm(w_out))
@@ -697,7 +702,7 @@
         ],
         in_specs=[scalar(), pl.BlockSpec(memory_space=pl.ANY)] + [whole()] * 2,
         out_specs=[whole()] * 4,
-        compiler_params=params(16),
+        compiler_params=params(6),
         cost_estimate=cost(1, 1),
         name="routing",
     )(half, partial_out, table, far_table)
@@ -712,53 +717,48 @@
         in_specs=[scalar(), pl.BlockSpec(memory_space=pl.ANY)] + [whole()] * (2 + tensors),
         out_specs=[whole()] * 3,
         scratch_shapes=[pltpu.VMEM((rows, model_width), f32)],
-        compiler_params=params(24),
+        compiler_params=params(4),
         name="middle",
     )(index, send, raw, mlp_gain.reshape(1, -1), *out_pieces)
 
     far_columns = from_partner(own_columns, groups)
     hbm = pl.BlockSpec(memory_space=pltpu.HBM)
     hidden = shared_out.shape[0]
-    shared_pieces = pl.pallas_call(
+    expert_hidden = expert_out.shape[1]
+    expert_in = in_hbm(jnp.transpose(expert_in, (0, 2, 3, 1)))
+    expert_out = in_hbm(expert_out)
+    early = max(1, local_experts // 2)
+    *shared_pieces, early_in, early_down = pl.pallas_call(
         functools.partial(shared_kernel, tensors=tensors),
-        out_shape=[shape((rows, column_share), bf16)] * tensors,
-        in_specs=[scalar(), whole(), hbm, hbm],
-        out_specs=[whole()] * tensors,
+        out_shape=[shape((rows, column_share), bf16)] * tensors
+        + [
+            pltpu.VMEM((early, 2, expert_hidden, model_width), bf16),
+            pltpu.VMEM((expert_hidden, model_width), bf16),
+        ],
+        in_specs=[scalar(), whole()] + [hbm] * 4,
+        out_specs=[whole()] * (tensors + 2),
         scratch_shapes=[
             pltpu.VMEM((2, hidden, model_width), bf16),
             pltpu.VMEM((hidden, model_width), bf16),
             pltpu.VMEM((rows, model_width), f32),
-            pltpu.SemaphoreType.DMA((3,)),
-        ],
-        compiler_params=params(16),
+            pltpu.SemaphoreType.DMA((5,)),
+        ],
+        compiler_params=params(11),
         cost_estimate=cost(1, 1),
         name="shared",
-    )(index, normed_mlp, in_hbm(jnp.transpose(shared_in, (1, 2, 0))), in_hbm(shared_out))
-    expert_hidden = expert_out.shape[1]
-    expert_in = in_hbm(jnp.transpose(expert_in, (0, 2, 3, 1)))
-    expert_out = in_hbm(expert_out)
-    first_in, first_down = pl.pallas_call(
-        load_kernel,
-        out_shape=[
-            pltpu.VMEM((2, expert_hidden, model_width), bf16),
-            pltpu.VMEM((expert_hidden, model_width), bf16),
-        ],
-        in_specs=[pl.BlockSpec(memory_space=pl.ANY), hbm, hbm],
-        out_specs=[whole()] * 2,
-        scratch_shapes=[pltpu.SemaphoreType.DMA((2,))],
-        compiler_params=params(1),
-        cost_estimate=cost(1, 1),
-        name="load",
-    )(normed_mlp, expert_in, expert_out)
+    )(
+        index, normed_mlp, in_hbm(jnp.transpose(shared_in, (1, 2, 0))), in_hbm(shared_out),
+        expert_in, expert_out,
+    )
 
     send_rows = pl.pallas_call(
         dispatch_kernel,
         out_shape=shape((slots, column_share), bf16),
         in_specs=[pl.BlockSpec(memory_space=pl.ANY)] * 2 + [whole()] * 3,
         out_specs=whole(),
-        compiler_params=params(8),
+        compiler_params=params(3),
         name="dispatch",
-    )(shared_pieces[0], first_down, send, own_columns, far_columns)
+    )(shared_pieces[0], early_down, send, own_columns, far_columns)
 
     arrived = exchange(send_rows, groups, halves=True)
 
@@ -772,13 +772,12 @@
         in_specs=[scalar()] + [whole()] * (tensors + 2) + [hbm, hbm],
         out_specs=[whole()] * tensors,
         scratch_shapes=[
-            pltpu.VMEM((local_experts - 1, 2, expert_hidden, model_width), bf16),
+            pltpu.VMEM((local_experts - early, 2, expert_hidden, model_width), bf16),
             pltpu.VMEM((local_experts - 1, expert_hidden, model_width), bf16),
             pltpu.VMEM((local_experts, groups * capacity, model_width), bf16),
-            pltpu.VMEM((tensors, groups, block, column_share), f32),
             pltpu.SemaphoreType.DMA((2, local_experts)),
         ],
-        compiler_params=params(35),
+        compiler_params=params(28),
         cost_estimate=cost(
             6 * slots * expert_hidden * model_width,
             6 * local_experts * expert_hidden * model_width,
@@ -787,8 +786,8 @@
     )(
         index,
         *arrived_pieces,
-        pltpu.with_memory_space_constraint(first_in, pltpu.VMEM),
-        pltpu.with_memory_space_constraint(first_down, pltpu.VMEM),
+        pltpu.with_memory_space_constraint(early_in, pltpu.VMEM),
+        pltpu.with_memory_space_constraint(early_down, pltpu.VMEM),
         expert_in,
         expert_out,
     )
@@ -800,7 +799,7 @@
         out_shape=shape((groups, block, column_share), bf16),
         in_specs=[pl.BlockSpec(memory_space=pl.ANY)] + [whole()] * tensors,
         out_specs=whole(),
-        compiler_params=params(12),
+        compiler_params=params(6),
         name="add",
     )(shared_pieces[-1], *partial_pieces)
 
@@ -811,7 +810,7 @@
         out_shape=shape((slot_rows, column_share), bf16),
         in_specs=[whole()] * (5 + tensors),
         out_specs=whole(),
-        compiler_params=params(24),
+        compiler_params=params(6),
         name="combine",
     )(returned, gate_high, gate_low, resid_own, final, *shared_pieces)
 
@@ -830,7 +829,7 @@
             fixed(slot_rows, column_share),
         ],
         out_specs=fixed(requests, leaf_len // tensors, model_width),
-        compiler_params=params(16, 1),
+        compiler_params=params(4, 1),
         name="settle",
     )(query_arrived, final_arrived)
 

time: 146 us -> 144 us (0.986)
  Pallas kernels: 44.1 us -> 42.3 us
    pallas_call x1 -> x0, Pallas kernels: 3.53 us -> none  [on_device(): pl.pallas_call(load_kernel, out_shape=[pltpu.VMEM((2, expert_hidden, mode...]
    pallas_call x1, Pallas kernels: 4.85 us -> 7.68 us  [on_device(): pl.pallas_call(functools.partial(shared_kernel, tensors=tensors), out_sha...]
  transfers between devices with their start and end apart: 8 -> 8, of which waited for: 5 -> 6; matrix products, arithmetic and copies ran while one was open for 0% -> 0% of each run, Pallas kernels for 12% -> 11%
where the time goes in v3:
time: 144 us
  blocking collectives  79.6 us (55%)
  Pallas kernels  42.3 us (29%)
  waiting for transfers between devices  13.1 us (9%)
  starting transfers between devices  8.55 us (6%)
    all_to_all x3, blocking collectives, exchange(): lax.all_to_all(blocks, 'dp', split_axis=0, concat_axis=0, tiled=True, axi...  62.1 us
    all_to_all x1, blocking collectives, on_device(): lax.all_to_all(blocks, ('dp', 'tensor'), split_axis=0, concat_axis=0, til...  17.4 us
    pallas_call x1, Pallas kernels, on_device(): pl.pallas_call(functools.partial(expert_kernel, tensors=tensors, experts=...  11.6 us
    pallas_call x1, Pallas kernels, on_device(): pl.pallas_call(functools.partial(shared_kernel, tensors=tensors), out_sha...  7.68 us
    ppermute x2, waiting for transfers between devices, from_partner(): lax.ppermute(array, 'dp', [(i, (i + groups // 2) % groups) for i in range...  7.26 us
    pallas_call x1, Pallas kernels, on_device(): pl.pallas_call(functools.partial(leaf_kernel, heads=step_heads, leaf_len=...  6.07 us
    pallas_call x1, Pallas kernels, on_device(): pl.pallas_call(functools.partial(owner_kernel, heads=local_heads, request...  5.15 us
    pallas_call x1, Pallas kernels, on_device(): pl.pallas_call(functools.partial(query_kernel, tensors=tensors, heads=que...  4.14 us
  transfers between devices with their start and end apart: 8, of which 6 were waited for; matrix products, arithmetic and copies ran while one was open for 0% of the time, Pallas kernels for 11%

profile of v3, /device:TPU:0, one launch (start us, length us, event | category | flops | bytes accessed | tf_op | source)
XLA Modules:
  0.0 143.7 jit_solution(10614981799399691961)
XLA Ops:
  0.0 0.5 collective-permute-start
  0.5 1.5 %prelude.1 = (bf16[256,64]{1,0:T(8,128)(2,1)S(1)}, bf16[256,128]{1,0:T(8,128)(2,1)S(1)}, f32[64,128]{1,0:T(8,128)S(1)}, f32[64,128]{1,0:T(8,128)S(1)}, f32[24,64...) custom-call(s32[3,8]{1,0:T(4,128)} %bitcast.43, s32[3,8]{1,0:T(4,128)} %bitcast.44, s32[3,8]{1,0:T(4,128)} %bitcast.45, ...), custom_call_target="tpu_custom_call" | custom-call | tf_op jit(solution)/shard_map/prelude/pallas_call | solution.py:579
  1.9 0.0 collective-permute-done.refs_2_
  1.9 4.1 %queries.1 = (bf16[64,2048]{1,0:T(8,128)(2,1)S(1)}, bf16[64,2048]{1,0:T(8,128)(2,1)S(1)}, bf16[64,1024]{1,0:T(8,128)(2,1)S(1)}, bf16[256,1152]{1,0:T(8,128)(2,1)S(1)}) custom-call(s32[1]{0:T(128)} %bitcast.refs_0_, bf16[32,2048]{1,0:T(8,128)(2,1)} %bitcast.39, bf16[32,2048]{1,0:T(8,128)(2,1)S(1)} %collective-permute-done.refs_2_, f32[1,2048]{1,0:T(1,128)} %bitcast.42, ...), custom_call_target="tpu_custom_call" | custom-call | flops 268435456 | bytes 4194304 | tf_op jit(solution)/shard_map/queries/pallas_call | solution.py:607
  6.1 25.8 %all_to_all.25 = bf16[16,16,1152]{2,1,0:T(8,128)(2,1)S(1)} all-to-all(bf16[16,16,1152]{2,1,0:T(8,128)(2,1)S(1)} %bitcast.33), channel_id=1, replica_groups=mesh['dp'=16,'tensor'=2] {'dp'}, dimensions={0} | all-to-all | bytes 1179648 | tf_op jit(solution)/shard_map/all_to_all | solution.py:74
  31.9 5.2 %owner.1 = bf16[256,1152]{1,0:T(8,128)(2,1)} custom-call(bf16[256,1152]{1,0:T(8,128)(2,1)S(1)} %bitcast.23, bf16[2,896,1024]{2,1,0:T(8,128)(2,1)S(1)} %copy-done), custom_call_target="tpu_custom_call" | custom-call | flops 939524096 | bytes 3670016 | tf_op jit(solution)/shard_map/owner/pallas_call | solution.py:653
  37.0 3.6 %all-to-all-start.1 = ((bf16[16,16,1152]{2,1,0:T(8,128)(2,1)}), bf16[16,16,1152]{2,1,0:T(8,128)(2,1)S(1)}, u32[]{:S(2)}, u32[]{:S(2)}) async-start(bf16[16,16,1152]{2,1,0:T(8,128)(2,1)} %bitcast.12), calls=%async_computation.1 | async-start | bytes 1179648 | tf_op jit(solution)/shard_map/all_to_all | solution.py:74
  40.6 2.8 %collective-permute-start.1 = (f32[24,64]{1,0:T(8,128)S(1)}, f32[24,64]{1,0:T(8,128)S(1)}, u32[]{:S(2)}, u32[]{:S(2)}) collective-permute-start(f32[24,64]{1,0:T(8,128)S(1)} %get-tuple-element.39.table_ref), channel_id=1, source_target_pairs={{0,16},{2,18},{4,20},{6,22},{8,24},{10,26},{12,28},{14,30},{16,0},... | collective-permute-start | bytes 18440 | tf_op jit(solution)/shard_map/ppermute | solution.py:80
  43.4 6.1 %leaf.1 = (f32[64,1024]{1,0:T(8,128)S(1)}, f32[64,128]{1,0:T(8,128)S(1)}) custom-call(bf16[64,2048]{1,0:T(8,128)(2,1)S(1)} %get-tuple-element.41.normed_ref, bf16[64,1024]{1,0:T(8,128)(2,1)S(1)} %get-tuple-element.42.query_ref, bf16[2048,1024]{1,0:T(8,128)(2,1)} %key_ref.1, bf16[2048,1024]{1,0:T(8,128)(2,1)} %value_ref.1, ...), custom_call_target="tpu_custom_call" | custom-call | flops 536870912 | bytes 8388608 | tf_op jit(solution)/shard_map/leaf/pallas_call | solution.py:634
  49.5 0.0 copy-start.1
  49.5 6.7 %collective-permute-done.1.after_ref.far_table_ref = f32[24,64]{1,0:T(8,128)S(1)} collective-permute-done((f32[24,64]{1,0:T(8,128)S(1)}, f32[24,64]{1,0:T(8,128)S(1)}, u32[]{:S(2)}, u32[]{:S(2)}) %collective-permute-start.1) | collective-permute-done | bytes 6176 | tf_op jit(solution)/shard_map/ppermute | solution.py:80
  56.2 0.3 all-to-all-done.1
  56.5 2.7 %merge.1.after_ref.refs_4_ = bf16[64,2048]{1,0:T(8,128)(2,1)S(1)} custom-call(f32[24,64]{1,0:T(8,128)S(1)} %collective-permute-done.1.after_ref.far_table_ref, bf16[256,1152]{1,0:T(8,128)(2,1)S(1)} %bitcast.30, bf16[3,64,256]{2,1,0:T(8,128)(2,1)S(1)} %get-tuple-element.40.pick_ref, f32[64,1024]{1,0:T(8,128)S(1)} %get-tuple-element.43.leaf_ref, ...), custom_call_target="tpu_custom_call" | custom-call | flops 268435456 | bytes 4194304 | tf_op jit(solution)/shard_map/merge/pallas_call | solution.py:672
  59.2 0.1 collective-permute-start.2
  59.3 1.0 routing.1
  60.3 0.5 collective-permute-done.2.refs_5_
  60.8 0.2 middle.1
  61.1 1.1 collective-permute-start.3
  62.2 7.7 %shared.1 = (bf16[64,1024]{1,0:T(8,128)(2,1)S(1)}, bf16[64,1024]{1,0:T(8,128)(2,1)S(1)}, bf16[2,2,704,2048]{3,2,1,0:T(8,128)(2,1)S(1)}, bf16[704,2048]{1,0:T(8,128)(2,1)S(1)}) custom-call(s32[1]{0:T(128)} %bitcast.refs_0_, bf16[64,2048]{1,0:T(8,128)(2,1)S(1)} %get-tuple-element.47.refs_1_, bf16[2,704,2048]{2,1,0:T(8,128)(2,1)} %bitcast.37, ...), custom_call_target="tpu_custom_call" | custom-call | flops 1 | bytes 1 | tf_op jit(solution)/shard_map/shared/pallas_call | solution.py:731
  69.9 0.5 collective-permute-done.3.far_ref
  70.4 0.4 dispatch.1
  70.8 18.3 %all_to_all.26 = bf16[8,64,1024]{2,1,0:T(8,128)(2,1)S(1)} all-to-all(bf16[8,64,1024]{2,1,0:T(8,128)(2,1)S(1)} %bitcast.27), channel_id=1, replica_groups={{0,2,4,6,8,10,12,14},{16,18,20,22,24,26,28,30},{1,3,5,7,9,11,13,15},{17..., dimensions={0} | all-to-all | bytes 2097152 | tf_op jit(solution)/shard_map/all_to_all | solution.py:74
  89.1 2.7 %collective-permute-done.4.refs_2_ = bf16[16,32,1024]{2,1,0:T(8,128)(2,1)S(1)} collective-permute-done((bf16[16,32,1024]{2,1,0:T(8,128)(2,1)S(1)}, bf16[16,32,1024]{2,1,0:T(8,128)(2,1)S(1)}, u32[]{:S(2)}, u32[]{:S(2)}) %collective-permute-start.4) | collective-permute-done | bytes 1048608 | tf_op jit(solution)/shard_map/ppermute | solution.py:55
  91.8 11.6 %experts.1 = (bf16[16,32,1024]{2,1,0:T(8,128)(2,1)S(1)}, bf16[16,32,1024]{2,1,0:T(8,128)(2,1)S(1)}) custom-call(s32[1]{0:T(128)} %bitcast.refs_0_, bf16[16,32,1024]{2,1,0:T(8,128)(2,1)S(1)} %bitcast.26, bf16[16,32,1024]{2,1,0:T(8,128)(2,1)S(1)} %collective-permute-done.4.refs_2_, bf16[2,2,704,2048]{3,2,1,0:T(8,128)(2,1)S(1)} %get-tuple-element.51.refs_3_, ...), custom_call_target="tpu_custom_call" | custom-call | flops 4429185024 | bytes 34603008 | tf_op jit(solution)/shard_map/experts/pallas_call | solution.py:767
  103.3 0.2 collective-permute-start.6
  103.5 0.4 collective-permute-start.5
  103.9 2.3 %collective-permute-done.5.after_ref.refs_6_ = bf16[64,1024]{1,0:T(8,128)(2,1)S(1)} collective-permute-done((bf16[64,1024]{1,0:T(8,128)(2,1)S(1)}, bf16[64,1024]{1,0:T(8,128)(2,1)S(1)}, u32[]{:S(2)}, u32[]{:S(2)}) %collective-permute-start.5) | collective-permute-done | bytes 131104 | tf_op jit(solution)/shard_map/ppermute | solution.py:65
  106.2 0.2 add.2
  106.5 18.0 %all_to_all.27 = bf16[8,64,1024]{2,1,0:T(8,128)(2,1)S(1)} all-to-all(bf16[8,64,1024]{2,1,0:T(8,128)(2,1)S(1)} %bitcast.28), channel_id=1, replica_groups={{0,2,4,6,8,10,12,14},{16,18,20,22,24,26,28,30},{1,3,5,7,9,11,13,15},{17..., dimensions={0} | all-to-all | bytes 2097152 | tf_op jit(solution)/shard_map/all_to_all | solution.py:74
  124.5 0.7 combine.1
  125.2 17.4 %all_to_all.28 = bf16[32,8,1024]{2,1,0:T(8,128)(2,1)S(1)} all-to-all(bf16[32,8,1024]{2,1,0:T(8,128)(2,1)S(1)} %bitcast.31), channel_id=1, replica_groups=mesh['dp'=16,'tensor'=2] {'dp','tensor'}, dimensions={0} | all-to-all | bytes 1048576 | tf_op jit(solution)/shard_map/all_to_all | solution.py:819
  142.6 1.0 settle.1
  (5 shorter events, 0.0 us)
Async XLA Ops:
  0.0 1.9 %collective-permute-start = (bf16[32,2048]{1,0:T(8,128)(2,1)}, bf16[32,2048]{1,0:T(8,128)(2,1)S(1)}, u32[]{:S(2)}, u32[]{:S(2)}) collective-permute-start(bf16[32,2048]{1,0:T(8,128)(2,1)} %bitcast.38), channel_id=1, source_target_pairs={{1,0},{0,1},{3,2},{2,3},{5,4},{4,5},{7,6},{6,7},{9,8},{8,9},{11,10... | collective-permute-start | bytes 393224 | tf_op jit(solution)/shard_map/ppermute | solution.py:55
  0.5 31.4 %copy-start = (bf16[2,896,1024]{2,1,0:T(8,128)(2,1)S(1)}, bf16[2,896,1024]{2,1,0:T(8,128)(2,1)}, u32[]{:S(2)}) copy-start(bf16[2,896,1024]{2,1,0:T(8,128)(2,1)} %kv_ref.1) | copy-start | bytes 11010052
  37.0 19.5 %all-to-all-start.1 = ((bf16[16,16,1152]{2,1,0:T(8,128)(2,1)}), bf16[16,16,1152]{2,1,0:T(8,128)(2,1)S(1)}, u32[]{:S(2)}, u32[]{:S(2)}) async-start(bf16[16,16,1152]{2,1,0:T(8,128)(2,1)} %bitcast.12), calls=%async_computation.1 | async-start | bytes 1179648 | tf_op jit(solution)/shard_map/all_to_all | solution.py:74
  40.6 15.6 %collective-permute-start.1 = (f32[24,64]{1,0:T(8,128)S(1)}, f32[24,64]{1,0:T(8,128)S(1)}, u32[]{:S(2)}, u32[]{:S(2)}) collective-permute-start(f32[24,64]{1,0:T(8,128)S(1)} %get-tuple-element.39.table_ref), channel_id=1, source_target_pairs={{0,16},{2,18},{4,20},{6,22},{8,24},{10,26},{12,28},{14,30},{16,0},... | collective-permute-start | bytes 18440 | tf_op jit(solution)/shard_map/ppermute | solution.py:80
  49.5 11.4 %copy-start.1 = (f32[2048]{0:T(1024)S(1)}, f32[2048]{0:T(1024)}, u32[]{:S(2)}) copy-start(f32[2048]{0:T(1024)} %param.28) | copy-start | bytes 24580
  59.2 1.6 %collective-permute-start.2 = (bf16[64,2048]{1,0:T(8,128)(2,1)S(1)}, bf16[64,2048]{1,0:T(8,128)(2,1)S(1)}, u32[]{:S(2)}, u32[]{:S(2)}) collective-permute-start(bf16[64,2048]{1,0:T(8,128)(2,1)S(1)} %merge.1.after_ref.refs_4_), channel_id=1, source_target_pairs={{1,0},{0,1},{3,2},{2,3},{5,4},{4,5},{7,6},{6,7},{9,8},{8,9},{11,10... | collective-permute-start | bytes 786440 | tf_op jit(solution)/shard_map/ppermute | solution.py:55
  61.1 9.3 %collective-permute-start.3 = (bf16[64,1024]{1,0:T(8,128)(2,1)S(1)}, bf16[64,1024]{1,0:T(8,128)(2,1)S(1)}, u32[]{:S(2)}, u32[]{:S(2)}) collective-permute-start(bf16[64,1024]{1,0:T(8,128)(2,1)S(1)} %get-tuple-element.50.own_ref), channel_id=1, source_target_pairs={{0,16},{2,18},{4,20},{6,22},{8,24},{10,26},{12,28},{14,30},{16,0},... | collective-permute-start | bytes 393224 | tf_op jit(solution)/shard_map/ppermute | solution.py:80
  89.1 2.7 %collective-permute-start.4 = (bf16[16,32,1024]{2,1,0:T(8,128)(2,1)S(1)}, bf16[16,32,1024]{2,1,0:T(8,128)(2,1)S(1)}, u32[]{:S(2)}, u32[]{:S(2)}) collective-permute-start(bf16[16,32,1024]{2,1,0:T(8,128)(2,1)S(1)} %bitcast.25), channel_id=1, source_target_pairs={{1,0},{0,1},{3,2},{2,3},{5,4},{4,5},{7,6},{6,7},{9,8},{8,9},{11,10... | collective-permute-start | bytes 3145736 | tf_op jit(solution)/shard_map/ppermute | solution.py:55
  103.3 2.9 %collective-permute-start.6 = (bf16[16,32,1024]{2,1,0:T(8,128)(2,1)S(1)}, bf16[16,32,1024]{2,1,0:T(8,128)(2,1)S(1)}, u32[]{:S(2)}, u32[]{:S(2)}) collective-permute-start(bf16[16,32,1024]{2,1,0:T(8,128)(2,1)S(1)} %get-tuple-element.57), channel_id=1, source_target_pairs={{0,1},{1,0},{2,3},{3,2},{4,5},{5,4},{6,7},{7,6},{8,9},{9,8},{10,11... | collective-permute-start | bytes 3145736 | tf_op jit(solution)/shard_map/ppermute | solution.py:65
  103.5 2.7 %collective-permute-start.5 = (bf16[64,1024]{1,0:T(8,128)(2,1)S(1)}, bf16[64,1024]{1,0:T(8,128)(2,1)S(1)}, u32[]{:S(2)}, u32[]{:S(2)}) collective-permute-start(bf16[64,1024]{1,0:T(8,128)(2,1)S(1)} %get-tuple-element.55), channel_id=1, source_target_pairs={{0,1},{1,0},{2,3},{3,2},{4,5},{5,4},{6,7},{7,6},{8,9},{9,8},{10,11... | collective-permute-start | bytes 393224 | tf_op jit(solution)/shard_map/ppermute | solution.py:65

commit v4 on v3

--- a/solution.py
+++ b/solution.py
@@ -441,9 +441,18 @@
         yield mine.astype(bf16)
 
 
+def own_half_kernel(index_ref, piece, early_in_ref, out_ref, *, experts, capacity):
+    width = piece.shape[2]
+    columns = pl.ds(pl.multiple_of(index_ref[0] * width, width), width)
+    rows = list(rows_of_experts(piece, experts, capacity))
+    for e in range(early_in_ref.shape[0]):
+        for part in range(2):
+            out_ref[e, part] = dot_nt(rows[e], early_in_ref[e, part, :, columns])
+
+
 def expert_kernel(*refs, tensors, experts, capacity):
     index_ref, arrived, refs = refs[0], refs[1 : 1 + tensors], refs[1 + tensors :]
-    (early_in_ref, early_down_ref, in_hbm_ref, down_hbm_ref), refs = refs[:4], refs[4:]
+    (half_ref, early_in_ref, early_down_ref, in_hbm_ref, down_hbm_ref), refs = refs[:5], refs[5:]
     pieces, refs = refs[:tensors], refs[tensors:]
     in_ref, down_ref, rows_ref, semaphores = refs
     early = early_in_ref.shape[0]
@@ -475,8 +484,15 @@
             weights = in_ref.at[e - early]
             in_copies[e].wait()
         down = early_down_ref if e == 0 else down_ref.at[e - 1]
-        gate = dot_nt(rows_ref[e], weights[0])
-        up = dot_nt(rows_ref[e], weights[1])
+        if e < early:
+            gate, up = half_ref[e, 0], half_ref[e, 1]
+            for at in range(1, tensors):
+                other = rows_ref[e, :, columns[at]]
+                gate = gate + dot_nt(other, weights[0, :, columns[at]])
+                up = up + dot_nt(other, weights[1, :, columns[at]])
+        else:
+            gate = dot_nt(rows_ref[e], weights[0])
+            up = dot_nt(rows_ref[e], weights[1])
         hidden = (gate / (1.0 + jnp.exp(-gate)) * up).astype(bf16)
         if e > 0:
             down_copies[e].wait()
@@ -764,12 +780,22 @@
 
     block = local_experts * capacity
     arrived_pieces = ring_get(arrived.reshape(groups, block, column_share), tensors)
+    early_in = pltpu.with_memory_space_constraint(early_in, pltpu.VMEM)
+    own_half = pl.pallas_call(
+        functools.partial(own_half_kernel, experts=local_experts, capacity=capacity),
+        out_shape=shape((early, 2, groups * capacity, expert_hidden), f32),
+        in_specs=[scalar()] + [whole()] * 2,
+        out_specs=whole(),
+        compiler_params=params(8),
+        cost_estimate=cost(1, 1),
+        name="own_half",
+    )(index, arrived_pieces[0], early_in)
     partial_pieces = pl.pallas_call(
         functools.partial(
             expert_kernel, tensors=tensors, experts=local_experts, capacity=capacity
         ),
         out_shape=[shape((groups, block, column_share), bf16)] * tensors,
-        in_specs=[scalar()] + [whole()] * (tensors + 2) + [hbm, hbm],
+        in_specs=[scalar()] + [whole()] * (tensors + 3) + [hbm, hbm],
         out_specs=[whole()] * tensors,
         scratch_shapes=[
             pltpu.VMEM((local_experts - early, 2, expert_hidden, model_width), bf16),
@@ -786,7 +812,8 @@
     )(
         index,
         *arrived_pieces,
-        pltpu.with_memory_space_constraint(early_in, pltpu.VMEM),
+        own_half,
+        early_in,
         pltpu.with_memory_space_constraint(early_down, pltpu.VMEM),
         expert_in,
         expert_out,

time: 144 us -> 143 us (level)
  waiting for transfers between devices: 13.1 us -> 11.2 us
    ppermute x3, waiting for transfers between devices: 3.2 us -> 1.3 us  [ring_get(): lax.ppermute(piece, 'tensor', [((i + step) % count, i) for i in range(cou...]
    pallas_call x0 -> x1, Pallas kernels: none -> 1.9 us  [on_device(): pl.pallas_call(functools.partial(own_half_kernel, experts=local_experts,...]
  transfers between devices with their start and end apart: 8 -> 8, of which waited for: 6 -> 6; matrix products, arithmetic and copies ran while one was open for 0% -> 0% of each run, Pallas kernels for 11% -> 13%
where the time goes in v4:
time: 143 us
  blocking collectives  79.6 us (56%)
  Pallas kernels  43.2 us (30%)
  waiting for transfers between devices  11.2 us (8%)
  starting transfers between devices  8.55 us (6%)
    all_to_all x3, blocking collectives, exchange(): lax.all_to_all(blocks, 'dp', split_axis=0, concat_axis=0, tiled=True, axi...  62.1 us
    all_to_all x1, blocking collectives, on_device(): lax.all_to_all(blocks, ('dp', 'tensor'), split_axis=0, concat_axis=0, til...  17.4 us
    pallas_call x1, Pallas kernels, on_device(): pl.pallas_call(functools.partial(expert_kernel, tensors=tensors, experts=...  10.5 us
    pallas_call x1, Pallas kernels, on_device(): pl.pallas_call(functools.partial(shared_kernel, tensors=tensors), out_sha...  7.68 us
    ppermute x2, waiting for transfers between devices, from_partner(): lax.ppermute(array, 'dp', [(i, (i + groups // 2) % groups) for i in range...  7.26 us
    pallas_call x1, Pallas kernels, on_device(): pl.pallas_call(functools.partial(leaf_kernel, heads=step_heads, leaf_len=...  6.07 us
    pallas_call x1, Pallas kernels, on_device(): pl.pallas_call(functools.partial(owner_kernel, heads=local_heads, request...  5.15 us
    pallas_call x1, Pallas kernels, on_device(): pl.pallas_call(functools.partial(query_kernel, tensors=tensors, heads=que...  4.14 us
  transfers between devices with their start and end apart: 8, of which 6 were waited for; matrix products, arithmetic and copies ran while one was open for 0% of the time, Pallas kernels for 13%

profile of v4, /device:TPU:0, one launch (start us, length us, event | category | flops | bytes accessed | tf_op | source)
XLA Modules:
  0.0 142.6 jit_solution(7313723739876988698)
XLA Ops:
  0.0 0.5 collective-permute-start
  0.5 1.5 %prelude.1 = (bf16[256,64]{1,0:T(8,128)(2,1)S(1)}, bf16[256,128]{1,0:T(8,128)(2,1)S(1)}, f32[64,128]{1,0:T(8,128)S(1)}, f32[64,128]{1,0:T(8,128)S(1)}, f32[24,64...) custom-call(s32[3,8]{1,0:T(4,128)} %bitcast.44, s32[3,8]{1,0:T(4,128)} %bitcast.45, s32[3,8]{1,0:T(4,128)} %bitcast.46, ...), custom_call_target="tpu_custom_call" | custom-call | tf_op jit(solution)/shard_map/prelude/pallas_call | solution.py:595
  1.9 4.1 %queries.1 = (bf16[64,2048]{1,0:T(8,128)(2,1)S(1)}, bf16[64,2048]{1,0:T(8,128)(2,1)S(1)}, bf16[64,1024]{1,0:T(8,128)(2,1)S(1)}, bf16[256,1152]{1,0:T(8,128)(2,1)S(1)}) custom-call(s32[1]{0:T(128)} %bitcast.refs_0_.index_ref, bf16[32,2048]{1,0:T(8,128)(2,1)} %bitcast.40, bf16[32,2048]{1,0:T(8,128)(2,1)S(1)} %collective-permute-done.refs_2_, ...), custom_call_target="tpu_custom_call" | custom-call | flops 268435456 | bytes 4194304 | tf_op jit(solution)/shard_map/queries/pallas_call | solution.py:623
  6.1 25.8 %all_to_all.25 = bf16[16,16,1152]{2,1,0:T(8,128)(2,1)S(1)} all-to-all(bf16[16,16,1152]{2,1,0:T(8,128)(2,1)S(1)} %bitcast.34), channel_id=1, replica_groups=mesh['dp'=16,'tensor'=2] {'dp'}, dimensions={0} | all-to-all | bytes 1179648 | tf_op jit(solution)/shard_map/all_to_all | solution.py:74
  31.9 5.2 %owner.1 = bf16[256,1152]{1,0:T(8,128)(2,1)} custom-call(bf16[256,1152]{1,0:T(8,128)(2,1)S(1)} %bitcast.26, bf16[2,896,1024]{2,1,0:T(8,128)(2,1)S(1)} %copy-done), custom_call_target="tpu_custom_call" | custom-call | flops 939524096 | bytes 3670016 | tf_op jit(solution)/shard_map/owner/pallas_call | solution.py:669
  37.0 3.6 %all-to-all-start.1 = ((bf16[16,16,1152]{2,1,0:T(8,128)(2,1)}), bf16[16,16,1152]{2,1,0:T(8,128)(2,1)S(1)}, u32[]{:S(2)}, u32[]{:S(2)}) async-start(bf16[16,16,1152]{2,1,0:T(8,128)(2,1)} %bitcast.12), calls=%async_computation.1 | async-start | bytes 1179648 | tf_op jit(solution)/shard_map/all_to_all | solution.py:74
  40.6 2.8 %collective-permute-start.1 = (f32[24,64]{1,0:T(8,128)S(1)}, f32[24,64]{1,0:T(8,128)S(1)}, u32[]{:S(2)}, u32[]{:S(2)}) collective-permute-start(f32[24,64]{1,0:T(8,128)S(1)} %get-tuple-element.39.table_ref), channel_id=1, source_target_pairs={{0,16},{2,18},{4,20},{6,22},{8,24},{10,26},{12,28},{14,30},{16,0},... | collective-permute-start | bytes 18440 | tf_op jit(solution)/shard_map/ppermute | solution.py:80
  43.4 6.1 %leaf.1 = (f32[64,1024]{1,0:T(8,128)S(1)}, f32[64,128]{1,0:T(8,128)S(1)}) custom-call(bf16[64,2048]{1,0:T(8,128)(2,1)S(1)} %get-tuple-element.41.normed_ref, bf16[64,1024]{1,0:T(8,128)(2,1)S(1)} %get-tuple-element.42.query_ref, bf16[2048,1024]{1,0:T(8,128)(2,1)} %key_ref.1, bf16[2048,1024]{1,0:T(8,128)(2,1)} %value_ref.1, ...), custom_call_target="tpu_custom_call" | custom-call | flops 536870912 | bytes 8388608 | tf_op jit(solution)/shard_map/leaf/pallas_call | solution.py:650
  49.5 0.0 copy-start.1
  49.5 6.7 %collective-permute-done.1.after_ref.far_table_ref = f32[24,64]{1,0:T(8,128)S(1)} collective-permute-done((f32[24,64]{1,0:T(8,128)S(1)}, f32[24,64]{1,0:T(8,128)S(1)}, u32[]{:S(2)}, u32[]{:S(2)}) %collective-permute-start.1) | collective-permute-done | bytes 6176 | tf_op jit(solution)/shard_map/ppermute | solution.py:80
  56.2 0.3 all-to-all-done.1
  56.5 2.7 %merge.1.after_ref.refs_4_ = bf16[64,2048]{1,0:T(8,128)(2,1)S(1)} custom-call(f32[24,64]{1,0:T(8,128)S(1)} %collective-permute-done.1.after_ref.far_table_ref, bf16[256,1152]{1,0:T(8,128)(2,1)S(1)} %bitcast.31, bf16[3,64,256]{2,1,0:T(8,128)(2,1)S(1)} %get-tuple-element.40.pick_ref, f32[64,1024]{1,0:T(8,128)S(1)} %get-tuple-element.43.leaf_ref, ...), custom_call_target="tpu_custom_call" | custom-call | flops 268435456 | bytes 4194304 | tf_op jit(solution)/shard_map/merge/pallas_call | solution.py:688
  59.2 0.1 collective-permute-start.2
  59.3 1.0 routing.1
  60.3 0.5 collective-permute-done.2.refs_5_
  60.8 0.2 middle.1
  61.1 1.1 collective-permute-start.3
  62.2 7.7 %shared.1 = (bf16[64,1024]{1,0:T(8,128)(2,1)S(1)}, bf16[64,1024]{1,0:T(8,128)(2,1)S(1)}, bf16[2,2,704,2048]{3,2,1,0:T(8,128)(2,1)S(1)}, bf16[704,2048]{1,0:T(8,128)(2,1)S(1)}) custom-call(s32[1]{0:T(128)} %bitcast.refs_0_.index_ref, bf16[64,2048]{1,0:T(8,128)(2,1)S(1)} %get-tuple-element.47.refs_1_, bf16[2,704,2048]{2,1,0:T(8,128)(2,1)} %bitcast.38, ...), custom_call_target="tpu_custom_call" | custom-call | flops 1 | bytes 1 | tf_op jit(solution)/shard_map/shared/pallas_call | solution.py:747
  69.9 0.5 collective-permute-done.3.far_ref
  70.4 0.4 dispatch.1
  70.8 18.3 %all_to_all.26 = bf16[8,64,1024]{2,1,0:T(8,128)(2,1)S(1)} all-to-all(bf16[8,64,1024]{2,1,0:T(8,128)(2,1)S(1)} %bitcast.28), channel_id=1, replica_groups={{0,2,4,6,8,10,12,14},{16,18,20,22,24,26,28,30},{1,3,5,7,9,11,13,15},{17..., dimensions={0} | all-to-all | bytes 2097152 | tf_op jit(solution)/shard_map/all_to_all | solution.py:74
  89.1 1.9 %own_half.1.refs_3_ = f32[2,2,128,704]{3,2,1,0:T(8,128)S(1)} custom-call(s32[1]{0:T(128)} %bitcast.refs_0_.index_ref, bf16[16,32,1024]{2,1,0:T(8,128)(2,1)S(1)} %bitcast.24, bf16[2,2,704,2048]{3,2,1,0:T(8,128)(2,1)S(1)} %get-tuple-element.51.early_in_ref.refs_4_), custom_call_target="tpu_custom_call" | custom-call | flops 1 | bytes 1 | tf_op jit(solution)/shard_map/own_half/pallas_call | solution.py:784
  91.0 0.8 collective-permute-done.4.refs_2_
  91.8 10.5 %experts.1 = (bf16[16,32,1024]{2,1,0:T(8,128)(2,1)S(1)}, bf16[16,32,1024]{2,1,0:T(8,128)(2,1)S(1)}) custom-call(s32[1]{0:T(128)} %bitcast.refs_0_.index_ref, bf16[16,32,1024]{2,1,0:T(8,128)(2,1)S(1)} %bitcast.25, bf16[16,32,1024]{2,1,0:T(8,128)(2,1)S(1)} %collective-permute-done.4.refs_2_, f32[2,2,128,704]{3,2,1,0:T(8,128)S(1)} %own_half.1.refs_3_, ...), custom_call_target="tpu_custom_call" | custom-call | flops 4429185024 | bytes 34603008 | tf_op jit(solution)/shard_map/experts/pallas_call | solution.py:793
  102.2 0.2 collective-permute-start.6
  102.4 0.4 collective-permute-start.5
  102.8 2.3 %collective-permute-done.5.after_ref.refs_6_ = bf16[64,1024]{1,0:T(8,128)(2,1)S(1)} collective-permute-done((bf16[64,1024]{1,0:T(8,128)(2,1)S(1)}, bf16[64,1024]{1,0:T(8,128)(2,1)S(1)}, u32[]{:S(2)}, u32[]{:S(2)}) %collective-permute-start.5) | collective-permute-done | bytes 131104 | tf_op jit(solution)/shard_map/ppermute | solution.py:65
  105.2 0.2 add.2
  105.4 18.0 %all_to_all.27 = bf16[8,64,1024]{2,1,0:T(8,128)(2,1)S(1)} all-to-all(bf16[8,64,1024]{2,1,0:T(8,128)(2,1)S(1)} %bitcast.29), channel_id=1, replica_groups={{0,2,4,6,8,10,12,14},{16,18,20,22,24,26,28,30},{1,3,5,7,9,11,13,15},{17..., dimensions={0} | all-to-all | bytes 2097152 | tf_op jit(solution)/shard_map/all_to_all | solution.py:74
  123.5 0.7 combine.1
  124.1 17.4 %all_to_all.28 = bf16[32,8,1024]{2,1,0:T(8,128)(2,1)S(1)} all-to-all(bf16[32,8,1024]{2,1,0:T(8,128)(2,1)S(1)} %bitcast.32), channel_id=1, replica_groups=mesh['dp'=16,'tensor'=2] {'dp','tensor'}, dimensions={0} | all-to-all | bytes 1048576 | tf_op jit(solution)/shard_map/all_to_all | solution.py:846
  141.5 1.0 settle.1
  (6 shorter events, 0.0 us)
Async XLA Ops:
  0.0 1.9 %collective-permute-start = (bf16[32,2048]{1,0:T(8,128)(2,1)}, bf16[32,2048]{1,0:T(8,128)(2,1)S(1)}, u32[]{:S(2)}, u32[]{:S(2)}) collective-permute-start(bf16[32,2048]{1,0:T(8,128)(2,1)} %bitcast.39), channel_id=1, source_target_pairs={{1,0},{0,1},{3,2},{2,3},{5,4},{4,5},{7,6},{6,7},{9,8},{8,9},{11,10... | collective-permute-start | bytes 393224 | tf_op jit(solution)/shard_map/ppermute | solution.py:55
  0.5 31.4 %copy-start = (bf16[2,896,1024]{2,1,0:T(8,128)(2,1)S(1)}, bf16[2,896,1024]{2,1,0:T(8,128)(2,1)}, u32[]{:S(2)}) copy-start(bf16[2,896,1024]{2,1,0:T(8,128)(2,1)} %kv_ref.1) | copy-start | bytes 11010052
  37.0 19.5 %all-to-all-start.1 = ((bf16[16,16,1152]{2,1,0:T(8,128)(2,1)}), bf16[16,16,1152]{2,1,0:T(8,128)(2,1)S(1)}, u32[]{:S(2)}, u32[]{:S(2)}) async-start(bf16[16,16,1152]{2,1,0:T(8,128)(2,1)} %bitcast.12), calls=%async_computation.1 | async-start | bytes 1179648 | tf_op jit(solution)/shard_map/all_to_all | solution.py:74
  40.6 15.6 %collective-permute-start.1 = (f32[24,64]{1,0:T(8,128)S(1)}, f32[24,64]{1,0:T(8,128)S(1)}, u32[]{:S(2)}, u32[]{:S(2)}) collective-permute-start(f32[24,64]{1,0:T(8,128)S(1)} %get-tuple-element.39.table_ref), channel_id=1, source_target_pairs={{0,16},{2,18},{4,20},{6,22},{8,24},{10,26},{12,28},{14,30},{16,0},... | collective-permute-start | bytes 18440 | tf_op jit(solution)/shard_map/ppermute | solution.py:80
  49.5 11.4 %copy-start.1 = (f32[2048]{0:T(1024)S(1)}, f32[2048]{0:T(1024)}, u32[]{:S(2)}) copy-start(f32[2048]{0:T(1024)} %param.28) | copy-start | bytes 24580
  59.2 1.6 %collective-permute-start.2 = (bf16[64,2048]{1,0:T(8,128)(2,1)S(1)}, bf16[64,2048]{1,0:T(8,128)(2,1)S(1)}, u32[]{:S(2)}, u32[]{:S(2)}) collective-permute-start(bf16[64,2048]{1,0:T(8,128)(2,1)S(1)} %merge.1.after_ref.refs_4_), channel_id=1, source_target_pairs={{1,0},{0,1},{3,2},{2,3},{5,4},{4,5},{7,6},{6,7},{9,8},{8,9},{11,10... | collective-permute-start | bytes 786440 | tf_op jit(solution)/shard_map/ppermute | solution.py:55
  61.1 9.3 %collective-permute-start.3 = (bf16[64,1024]{1,0:T(8,128)(2,1)S(1)}, bf16[64,1024]{1,0:T(8,128)(2,1)S(1)}, u32[]{:S(2)}, u32[]{:S(2)}) collective-permute-start(bf16[64,1024]{1,0:T(8,128)(2,1)S(1)} %get-tuple-element.50.own_ref), channel_id=1, source_target_pairs={{0,16},{2,18},{4,20},{6,22},{8,24},{10,26},{12,28},{14,30},{16,0},... | collective-permute-start | bytes 393224 | tf_op jit(solution)/shard_map/ppermute | solution.py:80
  89.1 2.7 %collective-permute-start.4 = (bf16[16,32,1024]{2,1,0:T(8,128)(2,1)S(1)}, bf16[16,32,1024]{2,1,0:T(8,128)(2,1)S(1)}, u32[]{:S(2)}, u32[]{:S(2)}) collective-permute-start(bf16[16,32,1024]{2,1,0:T(8,128)(2,1)S(1)} %bitcast.23), channel_id=1, source_target_pairs={{1,0},{0,1},{3,2},{2,3},{5,4},{4,5},{7,6},{6,7},{9,8},{8,9},{11,10... | collective-permute-start | bytes 3145736 | tf_op jit(solution)/shard_map/ppermute | solution.py:55
  102.2 2.9 %collective-permute-start.6 = (bf16[16,32,1024]{2,1,0:T(8,128)(2,1)S(1)}, bf16[16,32,1024]{2,1,0:T(8,128)(2,1)S(1)}, u32[]{:S(2)}, u32[]{:S(2)}) collective-permute-start(bf16[16,32,1024]{2,1,0:T(8,128)(2,1)S(1)} %get-tuple-element.57), channel_id=1, source_target_pairs={{0,1},{1,0},{2,3},{3,2},{4,5},{5,4},{6,7},{7,6},{8,9},{9,8},{10,11... | collective-permute-start | bytes 3145736 | tf_op jit(solution)/shard_map/ppermute | solution.py:65
  102.4 2.7 %collective-permute-start.5 = (bf16[64,1024]{1,0:T(8,128)(2,1)S(1)}, bf16[64,1024]{1,0:T(8,128)(2,1)S(1)}, u32[]{:S(2)}, u32[]{:S(2)}) collective-permute-start(bf16[64,1024]{1,0:T(8,128)(2,1)S(1)} %get-tuple-element.55), channel_id=1, source_target_pairs={{0,1},{1,0},{2,3},{3,2},{4,5},{5,4},{6,7},{7,6},{8,9},{9,8},{10,11... | collective-permute-start | bytes 393224 | tf_op jit(solution)/shard_map/ppermute | solution.py:65

commit v5 on v4

--- a/solution.py
+++ b/solution.py
@@ -328,15 +328,18 @@
         bias = jnp.where((key >= first[part]) & (key < last[part]), 0.0, HIDE)
         ones = jnp.ones((size, HEAD_DIM), bf16)
         sums = jnp.zeros((count, LANES), f32)
+        at = [slice(head * HEAD_DIM, (head + 1) * HEAD_DIM) for head in range(heads)]
+        scores = [
+            dot_nt(query_ref[part, one], kv_ref[0, keys, one]) * (scale * LOG2E) + bias
+            for one in at
+        ]
+        highest = [jnp.max(one, axis=1, keepdims=True) for one in scores]
+        weights = [jnp.exp2(one - high).astype(bf16) for one, high in zip(scores, highest)]
         for head in range(heads):
-            at = slice(head * HEAD_DIM, (head + 1) * HEAD_DIM)
-            scores = dot_nt(query_ref[part, at], kv_ref[0, keys, at]) * (scale * LOG2E) + bias
-            highest = jnp.max(scores, axis=1, keepdims=True)
-            weights = jnp.exp2(scores - highest).astype(bf16)
-            both = dot(weights, jnp.concatenate([kv_ref[1, keys, at], ones], axis=1))
+            both = dot(weights[head], jnp.concatenate([kv_ref[1, keys, at[head]], ones], axis=1))
             total = both[:, HEAD_DIM:]
-            out_ref[part, at] = (both[:, :HEAD_DIM] / total).astype(bf16)
-            lse = highest * LN2 + jnp.log(total)
+            out_ref[part, at[head]] = (both[:, :HEAD_DIM] / total).astype(bf16)
+            lse = highest[head] * LN2 + jnp.log(total)
             lse_high = lse.astype(bf16).astype(f32)
             sums = jnp.where(lane == head, lse_high, sums)
             sums = jnp.where(lane == head + heads, lse - lse_high, sums)

time: 143 us -> 141 us (0.986)
  Pallas kernels: 43.2 us -> 41.6 us
    pallas_call x1, Pallas kernels: 5.15 us -> 3.57 us  [on_device(): pl.pallas_call(functools.partial(owner_kernel, heads=local_heads, request...]
where the time goes in v5:
time: 141 us
  blocking collectives  79.6 us (56%)
  Pallas kernels  41.6 us (30%)
  waiting for transfers between devices  11.2 us (8%)
  starting transfers between devices  8.55 us (6%)
    all_to_all x3, blocking collectives, exchange(): lax.all_to_all(blocks, 'dp', split_axis=0, concat_axis=0, tiled=True, axi...  62.2 us
    all_to_all x1, blocking collectives, on_device(): lax.all_to_all(blocks, ('dp', 'tensor'), split_axis=0, concat_axis=0, til...  17.4 us
    pallas_call x1, Pallas kernels, on_device(): pl.pallas_call(functools.partial(expert_kernel, tensors=tensors, experts=...  10.5 us
    pallas_call x1, Pallas kernels, on_device(): pl.pallas_call(functools.partial(shared_kernel, tensors=tensors), out_sha...  7.68 us
    ppermute x2, waiting for transfers between devices, from_partner(): lax.ppermute(array, 'dp', [(i, (i + groups // 2) % groups) for i in range...  7.26 us
    pallas_call x1, Pallas kernels, on_device(): pl.pallas_call(functools.partial(leaf_kernel, heads=step_heads, leaf_len=...  6.07 us
    pallas_call x1, Pallas kernels, on_device(): pl.pallas_call(functools.partial(query_kernel, tensors=tensors, heads=que...  4.14 us
    ppermute x2, starting transfers between devices, from_partner(): lax.ppermute(array, 'dp', [(i, (i + groups // 2) % groups) for i in range...  3.86 us
  transfers between devices with their start and end apart: 8, of which 6 were waited for; matrix products, arithmetic and copies ran while one was open for 0% of the time, Pallas kernels for 13%

profile of v5, /device:TPU:0, one launch (start us, length us, event | category | flops | bytes accessed | tf_op | source)
XLA Modules:
  0.0 141.0 jit_solution(14628973981762214070)
XLA Ops:
  0.0 0.5 collective-permute-start
  0.5 1.5 %prelude.1 = (bf16[256,64]{1,0:T(8,128)(2,1)S(1)}, bf16[256,128]{1,0:T(8,128)(2,1)S(1)}, f32[64,128]{1,0:T(8,128)S(1)}, f32[64,128]{1,0:T(8,128)S(1)}, f32[24,64...) custom-call(s32[3,8]{1,0:T(4,128)} %bitcast.44, s32[3,8]{1,0:T(4,128)} %bitcast.45, s32[3,8]{1,0:T(4,128)} %bitcast.46, ...), custom_call_target="tpu_custom_call" | custom-call | tf_op jit(solution)/shard_map/prelude/pallas_call | solution.py:598
  1.9 4.1 %queries.1 = (bf16[64,2048]{1,0:T(8,128)(2,1)S(1)}, bf16[64,2048]{1,0:T(8,128)(2,1)S(1)}, bf16[64,1024]{1,0:T(8,128)(2,1)S(1)}, bf16[256,1152]{1,0:T(8,128)(2,1)S(1)}) custom-call(s32[1]{0:T(128)} %bitcast.refs_0_.index_ref, bf16[32,2048]{1,0:T(8,128)(2,1)} %bitcast.40, bf16[32,2048]{1,0:T(8,128)(2,1)S(1)} %collective-permute-done.refs_2_, ...), custom_call_target="tpu_custom_call" | custom-call | flops 268435456 | bytes 4194304 | tf_op jit(solution)/shard_map/queries/pallas_call | solution.py:626
  6.1 25.8 %all_to_all.25 = bf16[16,16,1152]{2,1,0:T(8,128)(2,1)S(1)} all-to-all(bf16[16,16,1152]{2,1,0:T(8,128)(2,1)S(1)} %bitcast.34), channel_id=1, replica_groups=mesh['dp'=16,'tensor'=2] {'dp'}, dimensions={0} | all-to-all | bytes 1179648 | tf_op jit(solution)/shard_map/all_to_all | solution.py:74
  31.9 3.6 %owner.1 = bf16[256,1152]{1,0:T(8,128)(2,1)} custom-call(bf16[256,1152]{1,0:T(8,128)(2,1)S(1)} %bitcast.26, bf16[2,896,1024]{2,1,0:T(8,128)(2,1)S(1)} %copy-done), custom_call_target="tpu_custom_call" | custom-call | flops 939524096 | bytes 3670016 | tf_op jit(solution)/shard_map/owner/pallas_call | solution.py:672
  35.5 3.6 %all-to-all-start.1 = ((bf16[16,16,1152]{2,1,0:T(8,128)(2,1)}), bf16[16,16,1152]{2,1,0:T(8,128)(2,1)S(1)}, u32[]{:S(2)}, u32[]{:S(2)}) async-start(bf16[16,16,1152]{2,1,0:T(8,128)(2,1)} %bitcast.12), calls=%async_computation.1 | async-start | bytes 1179648 | tf_op jit(solution)/shard_map/all_to_all | solution.py:74
  39.0 2.8 %collective-permute-start.1 = (f32[24,64]{1,0:T(8,128)S(1)}, f32[24,64]{1,0:T(8,128)S(1)}, u32[]{:S(2)}, u32[]{:S(2)}) collective-permute-start(f32[24,64]{1,0:T(8,128)S(1)} %get-tuple-element.39.table_ref), channel_id=1, source_target_pairs={{0,16},{2,18},{4,20},{6,22},{8,24},{10,26},{12,28},{14,30},{16,0},... | collective-permute-start | bytes 18440 | tf_op jit(solution)/shard_map/ppermute | solution.py:80
  41.8 6.1 %leaf.1 = (f32[64,1024]{1,0:T(8,128)S(1)}, f32[64,128]{1,0:T(8,128)S(1)}) custom-call(bf16[64,2048]{1,0:T(8,128)(2,1)S(1)} %get-tuple-element.41.normed_ref, bf16[64,1024]{1,0:T(8,128)(2,1)S(1)} %get-tuple-element.42.query_ref, bf16[2048,1024]{1,0:T(8,128)(2,1)} %key_ref.1, bf16[2048,1024]{1,0:T(8,128)(2,1)} %value_ref.1, ...), custom_call_target="tpu_custom_call" | custom-call | flops 536870912 | bytes 8388608 | tf_op jit(solution)/shard_map/leaf/pallas_call | solution.py:653
  47.9 0.0 copy-start.1
  47.9 6.7 %collective-permute-done.1.after_ref.far_table_ref = f32[24,64]{1,0:T(8,128)S(1)} collective-permute-done((f32[24,64]{1,0:T(8,128)S(1)}, f32[24,64]{1,0:T(8,128)S(1)}, u32[]{:S(2)}, u32[]{:S(2)}) %collective-permute-start.1) | collective-permute-done | bytes 6176 | tf_op jit(solution)/shard_map/ppermute | solution.py:80
  54.6 0.3 all-to-all-done.1
  54.9 2.7 %merge.1.after_ref.refs_4_ = bf16[64,2048]{1,0:T(8,128)(2,1)S(1)} custom-call(f32[24,64]{1,0:T(8,128)S(1)} %collective-permute-done.1.after_ref.far_table_ref, bf16[256,1152]{1,0:T(8,128)(2,1)S(1)} %bitcast.31, bf16[3,64,256]{2,1,0:T(8,128)(2,1)S(1)} %get-tuple-element.40.pick_ref, f32[64,1024]{1,0:T(8,128)S(1)} %get-tuple-element.43.leaf_ref, ...), custom_call_target="tpu_custom_call" | custom-call | flops 268435456 | bytes 4194304 | tf_op jit(solution)/shard_map/merge/pallas_call | solution.py:691
  57.7 0.1 collective-permute-start.2
  57.7 1.0 routing.1
  58.7 0.5 collective-permute-done.2.refs_5_
  59.3 0.2 middle.1
  59.5 1.1 collective-permute-start.3
  60.6 7.7 %shared.1 = (bf16[64,1024]{1,0:T(8,128)(2,1)S(1)}, bf16[64,1024]{1,0:T(8,128)(2,1)S(1)}, bf16[2,2,704,2048]{3,2,1,0:T(8,128)(2,1)S(1)}, bf16[704,2048]{1,0:T(8,128)(2,1)S(1)}) custom-call(s32[1]{0:T(128)} %bitcast.refs_0_.index_ref, bf16[64,2048]{1,0:T(8,128)(2,1)S(1)} %get-tuple-element.47.refs_1_, bf16[2,704,2048]{2,1,0:T(8,128)(2,1)} %bitcast.38, ...), custom_call_target="tpu_custom_call" | custom-call | flops 1 | bytes 1 | tf_op jit(solution)/shard_map/shared/pallas_call | solution.py:750
  68.3 0.5 collective-permute-done.3.far_ref
  68.8 0.4 dispatch.1
  69.2 18.3 %all_to_all.26 = bf16[8,64,1024]{2,1,0:T(8,128)(2,1)S(1)} all-to-all(bf16[8,64,1024]{2,1,0:T(8,128)(2,1)S(1)} %bitcast.28), channel_id=1, replica_groups={{0,2,4,6,8,10,12,14},{16,18,20,22,24,26,28,30},{1,3,5,7,9,11,13,15},{17..., dimensions={0} | all-to-all | bytes 2097152 | tf_op jit(solution)/shard_map/all_to_all | solution.py:74
  87.5 1.9 %own_half.1.refs_3_ = f32[2,2,128,704]{3,2,1,0:T(8,128)S(1)} custom-call(s32[1]{0:T(128)} %bitcast.refs_0_.index_ref, bf16[16,32,1024]{2,1,0:T(8,128)(2,1)S(1)} %bitcast.24, bf16[2,2,704,2048]{3,2,1,0:T(8,128)(2,1)S(1)} %get-tuple-element.51.early_in_ref.refs_4_), custom_call_target="tpu_custom_call" | custom-call | flops 1 | bytes 1 | tf_op jit(solution)/shard_map/own_half/pallas_call | solution.py:787
  89.4 0.8 collective-permute-done.4.refs_2_
  90.2 10.5 %experts.1 = (bf16[16,32,1024]{2,1,0:T(8,128)(2,1)S(1)}, bf16[16,32,1024]{2,1,0:T(8,128)(2,1)S(1)}) custom-call(s32[1]{0:T(128)} %bitcast.refs_0_.index_ref, bf16[16,32,1024]{2,1,0:T(8,128)(2,1)S(1)} %bitcast.25, bf16[16,32,1024]{2,1,0:T(8,128)(2,1)S(1)} %collective-permute-done.4.refs_2_, f32[2,2,128,704]{3,2,1,0:T(8,128)S(1)} %own_half.1.refs_3_, ...), custom_call_target="tpu_custom_call" | custom-call | flops 4429185024 | bytes 34603008 | tf_op jit(solution)/shard_map/experts/pallas_call | solution.py:796
  100.6 0.2 collective-permute-start.6
  100.9 0.3 collective-permute-start.5
  101.2 2.3 %collective-permute-done.5.after_ref.refs_6_ = bf16[64,1024]{1,0:T(8,128)(2,1)S(1)} collective-permute-done((bf16[64,1024]{1,0:T(8,128)(2,1)S(1)}, bf16[64,1024]{1,0:T(8,128)(2,1)S(1)}, u32[]{:S(2)}, u32[]{:S(2)}) %collective-permute-start.5) | collective-permute-done | bytes 131104 | tf_op jit(solution)/shard_map/ppermute | solution.py:65
  103.5 0.2 add.2
  103.8 18.1 %all_to_all.27 = bf16[8,64,1024]{2,1,0:T(8,128)(2,1)S(1)} all-to-all(bf16[8,64,1024]{2,1,0:T(8,128)(2,1)S(1)} %bitcast.29), channel_id=1, replica_groups={{0,2,4,6,8,10,12,14},{16,18,20,22,24,26,28,30},{1,3,5,7,9,11,13,15},{17..., dimensions={0} | all-to-all | bytes 2097152 | tf_op jit(solution)/shard_map/all_to_all | solution.py:74
  121.9 0.7 combine.1
  122.5 17.4 %all_to_all.28 = bf16[32,8,1024]{2,1,0:T(8,128)(2,1)S(1)} all-to-all(bf16[32,8,1024]{2,1,0:T(8,128)(2,1)S(1)} %bitcast.32), channel_id=1, replica_groups=mesh['dp'=16,'tensor'=2] {'dp','tensor'}, dimensions={0} | all-to-all | bytes 1048576 | tf_op jit(solution)/shard_map/all_to_all | solution.py:849
  140.0 1.0 settle.1
  (6 shorter events, 0.0 us)
Async XLA Ops:
  0.0 1.9 %collective-permute-start = (bf16[32,2048]{1,0:T(8,128)(2,1)}, bf16[32,2048]{1,0:T(8,128)(2,1)S(1)}, u32[]{:S(2)}, u32[]{:S(2)}) collective-permute-start(bf16[32,2048]{1,0:T(8,128)(2,1)} %bitcast.39), channel_id=1, source_target_pairs={{1,0},{0,1},{3,2},{2,3},{5,4},{4,5},{7,6},{6,7},{9,8},{8,9},{11,10... | collective-permute-start | bytes 393224 | tf_op jit(solution)/shard_map/ppermute | solution.py:55
  0.5 31.4 %copy-start = (bf16[2,896,1024]{2,1,0:T(8,128)(2,1)S(1)}, bf16[2,896,1024]{2,1,0:T(8,128)(2,1)}, u32[]{:S(2)}) copy-start(bf16[2,896,1024]{2,1,0:T(8,128)(2,1)} %kv_ref.1) | copy-start | bytes 11010052
  35.5 19.5 %all-to-all-start.1 = ((bf16[16,16,1152]{2,1,0:T(8,128)(2,1)}), bf16[16,16,1152]{2,1,0:T(8,128)(2,1)S(1)}, u32[]{:S(2)}, u32[]{:S(2)}) async-start(bf16[16,16,1152]{2,1,0:T(8,128)(2,1)} %bitcast.12), calls=%async_computation.1 | async-start | bytes 1179648 | tf_op jit(solution)/shard_map/all_to_all | solution.py:74
  39.0 15.6 %collective-permute-start.1 = (f32[24,64]{1,0:T(8,128)S(1)}, f32[24,64]{1,0:T(8,128)S(1)}, u32[]{:S(2)}, u32[]{:S(2)}) collective-permute-start(f32[24,64]{1,0:T(8,128)S(1)} %get-tuple-element.39.table_ref), channel_id=1, source_target_pairs={{0,16},{2,18},{4,20},{6,22},{8,24},{10,26},{12,28},{14,30},{16,0},... | collective-permute-start | bytes 18440 | tf_op jit(solution)/shard_map/ppermute | solution.py:80
  47.9 11.4 %copy-start.1 = (f32[2048]{0:T(1024)S(1)}, f32[2048]{0:T(1024)}, u32[]{:S(2)}) copy-start(f32[2048]{0:T(1024)} %param.28) | copy-start | bytes 24580
  57.7 1.6 %collective-permute-start.2 = (bf16[64,2048]{1,0:T(8,128)(2,1)S(1)}, bf16[64,2048]{1,0:T(8,128)(2,1)S(1)}, u32[]{:S(2)}, u32[]{:S(2)}) collective-permute-start(bf16[64,2048]{1,0:T(8,128)(2,1)S(1)} %merge.1.after_ref.refs_4_), channel_id=1, source_target_pairs={{1,0},{0,1},{3,2},{2,3},{5,4},{4,5},{7,6},{6,7},{9,8},{8,9},{11,10... | collective-permute-start | bytes 786440 | tf_op jit(solution)/shard_map/ppermute | solution.py:55
  59.5 9.3 %collective-permute-start.3 = (bf16[64,1024]{1,0:T(8,128)(2,1)S(1)}, bf16[64,1024]{1,0:T(8,128)(2,1)S(1)}, u32[]{:S(2)}, u32[]{:S(2)}) collective-permute-start(bf16[64,1024]{1,0:T(8,128)(2,1)S(1)} %get-tuple-element.50.own_ref), channel_id=1, source_target_pairs={{0,16},{2,18},{4,20},{6,22},{8,24},{10,26},{12,28},{14,30},{16,0},... | collective-permute-start | bytes 393224 | tf_op jit(solution)/shard_map/ppermute | solution.py:80
  87.5 2.7 %collective-permute-start.4 = (bf16[16,32,1024]{2,1,0:T(8,128)(2,1)S(1)}, bf16[16,32,1024]{2,1,0:T(8,128)(2,1)S(1)}, u32[]{:S(2)}, u32[]{:S(2)}) collective-permute-start(bf16[16,32,1024]{2,1,0:T(8,128)(2,1)S(1)} %bitcast.23), channel_id=1, source_target_pairs={{1,0},{0,1},{3,2},{2,3},{5,4},{4,5},{7,6},{6,7},{9,8},{8,9},{11,10... | collective-permute-start | bytes 3145736 | tf_op jit(solution)/shard_map/ppermute | solution.py:55
  100.6 2.9 %collective-permute-start.6 = (bf16[16,32,1024]{2,1,0:T(8,128)(2,1)S(1)}, bf16[16,32,1024]{2,1,0:T(8,128)(2,1)S(1)}, u32[]{:S(2)}, u32[]{:S(2)}) collective-permute-start(bf16[16,32,1024]{2,1,0:T(8,128)(2,1)S(1)} %get-tuple-element.57), channel_id=1, source_target_pairs={{0,1},{1,0},{2,3},{3,2},{4,5},{5,4},{6,7},{7,6},{8,9},{9,8},{10,11... | collective-permute-start | bytes 3145736 | tf_op jit(solution)/shard_map/ppermute | solution.py:65
  100.9 2.7 %collective-permute-start.5 = (bf16[64,1024]{1,0:T(8,128)(2,1)S(1)}, bf16[64,1024]{1,0:T(8,128)(2,1)S(1)}, u32[]{:S(2)}, u32[]{:S(2)}) collective-permute-start(bf16[64,1024]{1,0:T(8,128)(2,1)S(1)} %get-tuple-element.55), channel_id=1, source_target_pairs={{0,1},{1,0},{2,3},{3,2},{4,5},{5,4},{6,7},{7,6},{8,9},{9,8},{10,11... | collective-permute-start | bytes 393224 | tf_op jit(solution)/shard_map/ppermute | solution.py:65
